TPU v7x, 32 devices: a whole 2x2x4 slice. The times are simulated.
32 devices in a mesh: dp: 4 (over x, core), ex: 2 (over y), ey: 4 (over z).
Axes of the slice: x: 2, y: 2, z: 4, core: 2. Of those that a mesh axis runs over, the one named last changes fastest.
Arguments:
- tokens: bfloat16 [2, 1536, 2048], P(None, ('dp', 'ex', 'ey')), parts along dimension 1, may hold values from -6 to 6
- expert_ids: int32 [2, 1536, 8], P(None, ('dp', 'ex', 'ey')), parts along dimension 1, may hold values from 0 to 7, as said below
- slot_ids: int32 [2, 1536, 8], P(None, ('dp', 'ex', 'ey')), parts along dimension 1, may hold values from 0 to 47, as said below
- gate_values: float32 [2, 1536, 8], P(None, ('dp', 'ex', 'ey')), parts along dimension 1, may hold values from 0.05 to 1
- gate_weight: bfloat16 [8, 2048, 1024], P(('ex', 'ey')), may hold values from -0.125 to 0.125
- up_weight: bfloat16 [8, 2048, 1024], P(('ex', 'ey')), may hold values from -0.125 to 0.125
- down_weight: bfloat16 [8, 1024, 2048], P(('ex', 'ey')), may hold values from -0.1875 to 0.1875
Outputs:
- mixture: bfloat16 [2, 1536, 2048], P(None, ('dp', 'ex', 'ey')), parts along dimension 1
There are 4 independent parts, one for each index of `dp`. A program takes and returns all parts, laid end to end along the dimension named above; an argument that names none is the same for every part. Nothing has to cross between parts.
Inputs may be any that keep to these rules, and one draw needn't show every extreme that they name: `expert_ids`: each token names 8 different experts. `slot_ids`: within one micro-batch, one block of 48 tokens and one expert, the assignments are numbered 0, 1, 2, ... in a drawn priority order; an assignment keeps its number as slot if it is below 60, else it is -1. In every block some expert receives an assignment from each of its 48 tokens.
All inputs are finite; a program needn't handle non-finite values.
Results may differ from a plain program's by a relative error of at most 0.0057.
Values may be sent and summed in bfloat16 or wider, within the bound.
No kernel may reach another device: no remote copies, remote signals or barrier semaphores. Data moves between devices by JAX's collectives and lax.ppermute only.
A program may use at most 64 MiB of HBM per device.

v0:
```python
import jax
import jax.numpy as jnp
from jax import lax
from jax.sharding import PartitionSpec as P

TOP = 8


def per_device(tokens, expert_ids, slot_ids, gate_values, gate_weight, up_weight, down_weight):
    across_x = lax.axis_size("ex")
    across_y = lax.axis_size("ey")
    experts = across_x * across_y
    micro, tok_dev, width = tokens.shape
    slot_count = (tok_dev * TOP * 5 + 4 * experts - 1) // (4 * experts)
    cells = experts * slot_count
    gate_matrix = gate_weight[0]
    up_matrix = up_weight[0]
    down_matrix = down_weight[0]
    columns = jnp.arange(cells, dtype=jnp.int32)

    def expert_apply(received):
        flat = received.reshape(-1, width)
        gate_part = jnp.dot(flat, gate_matrix, preferred_element_type=jnp.float32)
        up_part = jnp.dot(flat, up_matrix, preferred_element_type=jnp.float32)
        hidden = (jax.nn.silu(gate_part) * up_part).astype(jnp.bfloat16)
        output = jnp.dot(hidden, down_matrix, preferred_element_type=jnp.float32).astype(
            jnp.bfloat16
        )
        return output.reshape(received.shape)

    def route_slots(buffer):
        return lax.all_to_all(
            expert_apply(
                lax.all_to_all(buffer, ("ex", "ey"), split_axis=0, concat_axis=0, tiled=True)
            ),
            ("ex", "ey"),
            split_axis=0,
            concat_axis=0,
            tiled=True,
        )

    buffers = []
    mixings = []
    for index in range(micro):
        chosen = expert_ids[index]
        places = slot_ids[index]
        cell_index = jnp.where(places >= 0, chosen * slot_count + places, -1)
        one_hot = cell_index[:, :, None] == columns[None, None, :]
        selection = jnp.sum(one_hot.astype(jnp.float32), axis=1).astype(jnp.bfloat16)
        mixing = jnp.sum(
            jnp.where(one_hot, gate_values[index][:, :, None], jnp.float32(0.0)), axis=1
        )
        gathered = jnp.dot(selection.T, tokens[index], preferred_element_type=jnp.float32)
        buffers.append(gathered.astype(jnp.bfloat16).reshape(experts, slot_count, width))
        mixings.append(mixing)
    outputs = [route_slots(buffers[index]) for index in range(micro)]
    results = []
    for index in range(micro):
        flat_out = outputs[index].reshape(cells, width).astype(jnp.float32)
        mixture = jnp.dot(mixings[index], flat_out, precision=lax.Precision.HIGHEST)
        results.append(mixture.astype(jnp.bfloat16))
    return jnp.stack(results, axis=0)


def solution(mesh):
    in_specs = (
        P(None, ("dp", "ex", "ey"), None),
        P(None, ("dp", "ex", "ey"), None),
        P(None, ("dp", "ex", "ey"), None),
        P(None, ("dp", "ex", "ey"), None),
        P(("ex", "ey"), None, None),
        P(("ex", "ey"), None, None),
        P(("ex", "ey"), None, None),
    )
    out_specs = P(None, ("dp", "ex", "ey"), None)
    return jax.shard_map(
        per_device, mesh=mesh, in_specs=in_specs, out_specs=out_specs, check_vma=False
    )
```

profile of v0, /device:TPU:0, one launch (start us, length us, event | category | flops | bytes accessed | tf_op | source)
XLA Modules:
  0.0 220.5 jit_solution(15190327156613904789)
XLA Ops:
  2.2 1.6 convolution_convert_fusion
  3.8 1.5 reshape.74
  5.3 7.4 %all-to-all-start.2 = ((bf16[8,60,2048]{2,1,0:T(8,128)(2,1)}), bf16[8,60,2048]{2,1,0:T(8,128)(2,1)S(1)}, u32[]{:S(2)}, u32[]{:S(2)}) async-start(bf16[8,60,2048]{2,1,0:T(8,128)(2,1)} %reshape.74), calls=%async_computation.2 | async-start | bytes 4194304 | tf_op jit(solution)/shard_map/all_to_all | solution.py:34
  13.5 2.0 convolution_convert_fusion.1
  15.5 2.7 %reshape.70 = bf16[8,60,2048]{2,1,0:T(8,128)(2,1)} reshape(bf16[480,2048]{1,0:T(8,128)(2,1)} %convolution_convert_fusion.1) | data formatting | bytes 3932160 | tf_op jit(solution)/shard_map/reshape | solution.py:54
  18.2 43.7 %all-to-all-done.2 = bf16[8,60,2048]{2,1,0:T(8,128)(2,1)S(1)} async-done(((bf16[8,60,2048]{2,1,0:T(8,128)(2,1)}), bf16[8,60,2048]{2,1,0:T(8,128)(2,1)S(1)}, u32[]{:S(2)}, u32[]{:S(2)}) %all-to-all-start.2) | async-done | bytes 1966112 | tf_op jit(solution)/shard_map/all_to_all | solution.py:34
  61.8 4.3 %all-to-all-start = ((bf16[8,60,2048]{2,1,0:T(8,128)(2,1)}), bf16[8,60,2048]{2,1,0:T(8,128)(2,1)}, u32[]{:S(2)}, u32[]{:S(2)}) async-start(bf16[8,60,2048]{2,1,0:T(8,128)(2,1)} %reshape.70), calls=%async_computation | async-start | bytes 4194304 | tf_op jit(solution)/shard_map/all_to_all | solution.py:34
  66.2 1.5 reshape.75
  67.7 6.4 %fusion.8 = f32[480,1024]{1,0:T(8,128)} fusion(bf16[480,2048]{1,0:T(8,128)(2,1)} %reshape.75, bf16[1,2048,1024]{2,1,0:T(8,128)(2,1)} %param.11), kind=kOutput, calls=%fused_computation.8 | convolution fusion | flops 2013265920 | bytes 8126464 | tf_op jit(solution)/shard_map/dot_general | solution.py:23
  74.1 9.6 %fusion.15 = bf16[480,2048]{1,0:T(8,128)(2,1)} fusion(bf16[1,1024,2048]{2,1,0:T(8,128)(2,1)} %param.13, f32[480,1024]{1,0:T(8,128)} %fusion.8, bf16[480,2048]{1,0:T(8,128)(2,1)S(1)} %copy-done, bf16[1,2048,1024]{2,1,0:T(8,128)(2,1)} %param.12), kind=kOutput, calls=%fused_computation.13 | convolution fusion | flops 4030464000 | bytes 14286848 | tf_op jit(solution)/shard_map/dot_general | solution.py:26
  83.7 2.7 %reshape.76 = bf16[8,60,2048]{2,1,0:T(8,128)(2,1)} reshape(bf16[480,2048]{1,0:T(8,128)(2,1)} %fusion.15) | data formatting | bytes 3932160 | tf_op jit(solution)/shard_map/reshape | solution.py:29
  86.4 27.9 %all-to-all-done = bf16[8,60,2048]{2,1,0:T(8,128)(2,1)} async-done(((bf16[8,60,2048]{2,1,0:T(8,128)(2,1)}), bf16[8,60,2048]{2,1,0:T(8,128)(2,1)}, u32[]{:S(2)}, u32[]{:S(2)}) %all-to-all-start) | async-done | bytes 1966112 | tf_op jit(solution)/shard_map/all_to_all | solution.py:34
  114.4 3.8 %all-to-all-start.3 = ((bf16[8,60,2048]{2,1,0:T(8,128)(2,1)}), bf16[8,60,2048]{2,1,0:T(8,128)(2,1)S(1)}, u32[]{:S(2)}, u32[]{:S(2)}) async-start(bf16[8,60,2048]{2,1,0:T(8,128)(2,1)} %reshape.76), calls=%async_computation.3 | async-start | bytes 4194304 | tf_op jit(solution)/shard_map/all_to_all | solution.py:32
  118.2 2.7 %reshape.71 = bf16[480,2048]{1,0:T(8,128)(2,1)} reshape(bf16[8,60,2048]{2,1,0:T(8,128)(2,1)} %all-to-all-done) | data formatting | bytes 3932160 | tf_op jit(solution)/shard_map/reshape | solution.py:22
  120.9 6.3 %fusion.10 = f32[480,1024]{1,0:T(8,128)} fusion(bf16[480,2048]{1,0:T(8,128)(2,1)} %reshape.71, bf16[1,2048,1024]{2,1,0:T(8,128)(2,1)} %param.11), kind=kOutput, calls=%fused_computation.10 | convolution fusion | flops 2013265920 | bytes 8126464 | tf_op jit(solution)/shard_map/dot_general | solution.py:23
  127.1 10.2 %fusion.12 = bf16[480,2048]{1,0:T(8,128)(2,1)} fusion(bf16[1,1024,2048]{2,1,0:T(8,128)(2,1)} %param.13, f32[480,1024]{1,0:T(8,128)} %fusion.10, bf16[480,2048]{1,0:T(8,128)(2,1)} %reshape.71, bf16[1,2048,1024]{2,1,0:T(8,128)(2,1)} %param.12), kind=kOutput, calls=%fused_computation.12 | convolution fusion | flops 4030464000 | bytes 14286848 | tf_op jit(solution)/shard_map/dot_general | solution.py:26
  137.3 2.7 %reshape.72 = bf16[8,60,2048]{2,1,0:T(8,128)(2,1)} reshape(bf16[480,2048]{1,0:T(8,128)(2,1)} %fusion.12) | data formatting | bytes 3932160 | tf_op jit(solution)/shard_map/reshape | solution.py:29
  140.0 25.6 %all-to-all-done.3 = bf16[8,60,2048]{2,1,0:T(8,128)(2,1)S(1)} async-done(((bf16[8,60,2048]{2,1,0:T(8,128)(2,1)}), bf16[8,60,2048]{2,1,0:T(8,128)(2,1)S(1)}, u32[]{:S(2)}, u32[]{:S(2)}) %all-to-all-start.3) | async-done | bytes 1966112 | tf_op jit(solution)/shard_map/all_to_all | solution.py:32
  165.6 4.3 %all-to-all-start.1 = ((bf16[8,60,2048]{2,1,0:T(8,128)(2,1)}), bf16[8,60,2048]{2,1,0:T(8,128)(2,1)}, u32[]{:S(2)}, u32[]{:S(2)}) async-start(bf16[8,60,2048]{2,1,0:T(8,128)(2,1)} %reshape.72), calls=%async_computation.1 | async-start | bytes 4194304 | tf_op jit(solution)/shard_map/all_to_all | solution.py:32
  169.9 1.5 reshape.77
  171.4 2.7 %fusion.19 = bf16[1,48,2048]{2,1,0:T(8,128)(2,1)S(1)} fusion(f32[48,480]{1,0:T(8,128)S(1)} %get-tuple-element.8, bf16[480,2048]{1,0:T(8,128)(2,1)} %reshape.77), kind=kOutput, calls=%fused_computation.19 | convolution fusion | flops 566329344 | bytes 2254848 | tf_op jit(solution)/shard_map/dot_general | solution.py:60
  174.1 42.8 %all-to-all-done.1 = bf16[8,60,2048]{2,1,0:T(8,128)(2,1)} async-done(((bf16[8,60,2048]{2,1,0:T(8,128)(2,1)}), bf16[8,60,2048]{2,1,0:T(8,128)(2,1)}, u32[]{:S(2)}, u32[]{:S(2)}) %all-to-all-start.1) | async-done | bytes 1966112 | tf_op jit(solution)/shard_map/all_to_all | solution.py:32
  216.9 1.7 reshape.73
  218.6 1.1 fusion.18
  (13 shorter events, 3.6 us)
Async XLA Ops:
  5.3 8.1 %copy-start.1 = (bf16[2,48,2048]{2,1,0:T(8,128)(2,1)S(1)}, bf16[2,48,2048]{2,1,0:T(8,128)(2,1)}, u32[]{:S(2)}) copy-start(bf16[2,48,2048]{2,1,0:T(8,128)(2,1)} %param.7) | copy-start | bytes 1179652
  5.3 56.5 %all-to-all-start.2 = ((bf16[8,60,2048]{2,1,0:T(8,128)(2,1)}), bf16[8,60,2048]{2,1,0:T(8,128)(2,1)S(1)}, u32[]{:S(2)}, u32[]{:S(2)}) async-start(bf16[8,60,2048]{2,1,0:T(8,128)(2,1)} %reshape.74), calls=%async_computation.2 | async-start | bytes 4194304 | tf_op jit(solution)/shard_map/all_to_all | solution.py:34
  61.8 52.5 %all-to-all-start = ((bf16[8,60,2048]{2,1,0:T(8,128)(2,1)}), bf16[8,60,2048]{2,1,0:T(8,128)(2,1)}, u32[]{:S(2)}, u32[]{:S(2)}) async-start(bf16[8,60,2048]{2,1,0:T(8,128)(2,1)} %reshape.70), calls=%async_computation | async-start | bytes 4194304 | tf_op jit(solution)/shard_map/all_to_all | solution.py:34
  67.7 6.4 %copy-start = (bf16[480,2048]{1,0:T(8,128)(2,1)S(1)}, bf16[480,2048]{1,0:T(8,128)(2,1)}, u32[]{:S(2)}) copy-start(bf16[480,2048]{1,0:T(8,128)(2,1)} %reshape.75) | copy-start | bytes 5898244
  114.4 51.2 %all-to-all-start.3 = ((bf16[8,60,2048]{2,1,0:T(8,128)(2,1)}), bf16[8,60,2048]{2,1,0:T(8,128)(2,1)S(1)}, u32[]{:S(2)}, u32[]{:S(2)}) async-start(bf16[8,60,2048]{2,1,0:T(8,128)(2,1)} %reshape.76), calls=%async_computation.3 | async-start | bytes 4194304 | tf_op jit(solution)/shard_map/all_to_all | solution.py:32
  165.6 51.3 %all-to-all-start.1 = ((bf16[8,60,2048]{2,1,0:T(8,128)(2,1)}), bf16[8,60,2048]{2,1,0:T(8,128)(2,1)}, u32[]{:S(2)}, u32[]{:S(2)}) async-start(bf16[8,60,2048]{2,1,0:T(8,128)(2,1)} %reshape.72), calls=%async_computation.1 | async-start | bytes 4194304 | tf_op jit(solution)/shard_map/all_to_all | solution.py:32
where the time goes:
time: 221 us
  waiting for transfers between devices  140 us (63%)
  matrix products  39.9 us (18%)
  starting transfers between devices  19.9 us (9%)
  local copies, waits for them, and re-layouts  18.1 us (8%)
  other arithmetic  2.62 us (1%)
    all_to_all x2, waiting for transfers between devices, route_slots(): lax.all_to_all(buffer, ('ex', 'ey'), split_axis=0, concat_axis=0, tiled=T...  71.6 us
    all_to_all x2, waiting for transfers between devices, route_slots(): lax.all_to_all(expert_apply(lax.all_to_all(buffer, ('ex', 'ey'), split_ax...  68.3 us
    dot_general x2, matrix products, expert_apply(): jnp.dot(hidden, down_matrix, preferred_element_type=jnp.float32)  19.8 us
    dot_general x2, matrix products, expert_apply(): gate_part = jnp.dot(flat, gate_matrix, preferred_element_type=jnp.float32)  12.7 us
    all_to_all x2, starting transfers between devices, route_slots(): lax.all_to_all(buffer, ('ex', 'ey'), split_axis=0, concat_axis=0, tiled=T...  11.7 us
    all_to_all x2, starting transfers between devices, route_slots(): lax.all_to_all(expert_apply(lax.all_to_all(buffer, ('ex', 'ey'), split_ax...  8.12 us
    reshape x2, local copies, waits for them, and re-layouts, expert_apply(): return output.reshape(received.shape)  5.42 us
  transfers between devices with their start and end apart: 4, of which 4 were waited for; matrix products, arithmetic and copies ran while one was open for 23% of the time, Pallas kernels for 0%

commit v1 on v0

--- a/solution.py
+++ b/solution.py
@@ -1,12 +1,16 @@
+import functools
+
 import jax
 import jax.numpy as jnp
 from jax import lax
+from jax.experimental import pallas as pl
+from jax.experimental.pallas import tpu as pltpu
 from jax.sharding import PartitionSpec as P
 
 TOP = 8
 
 
-def per_device(tokens, expert_ids, slot_ids, gate_values, gate_weight, up_weight, down_weight):
+def slot_layer(tokens, expert_ids, slot_ids, gate_values, gate_weight, up_weight, down_weight):
     across_x = lax.axis_size("ex")
     across_y = lax.axis_size("ey")
     experts = across_x * across_y
@@ -60,6 +64,273 @@
         mixture = jnp.dot(mixings[index], flat_out, precision=lax.Precision.HIGHEST)
         results.append(mixture.astype(jnp.bfloat16))
     return jnp.stack(results, axis=0)
+
+
+def pack_kernel(tokens_ref, *refs):
+    micro, tok_dev, width = tokens_ref.shape
+    routing = refs[:3]
+    blocks = refs[3 : 3 + micro]
+    ids_ref, slots_ref, gates_ref, spread_ref, small_semaphores, semaphores = refs[3 + micro :]
+    choices = ids_ref.shape[1]
+    small_copies = [
+        pltpu.make_async_copy(source, target, small_semaphores.at[index])
+        for index, (source, target) in enumerate(zip(routing, (ids_ref, slots_ref, gates_ref)))
+    ]
+    rows = blocks[0].shape[0]
+    groups = tok_dev // rows
+    copies = [
+        pltpu.make_async_copy(
+            tokens_ref.at[index, pl.ds(group * rows, rows)],
+            block.at[:, pl.ds(group * width, width)],
+            semaphores.at[index, group],
+        )
+        for index, block in enumerate(blocks)
+        for group in range(groups)
+    ]
+    for copy in small_copies + copies:
+        copy.start()
+    for copy in small_copies:
+        copy.wait()
+    names = lax.broadcasted_iota(jnp.int32, (choices, tok_dev), 0)
+    for index, block in enumerate(blocks):
+        ids = ids_ref[index]
+        kept = jnp.where(slots_ref[index] >= 0, gates_ref[index], jnp.float32(0.0))
+        share = jnp.zeros((choices, tok_dev), jnp.float32)
+        for choice in range(choices):
+            share += jnp.where(
+                ids[choice : choice + 1] == names, kept[choice : choice + 1], jnp.float32(0.0)
+            )
+        spread_ref[...] = jnp.zeros_like(spread_ref)
+        for piece in range(3):
+            rounded = share.astype(jnp.bfloat16).astype(jnp.float32)
+            share = share - rounded
+            for group in range(groups):
+                place = (group * 3 + piece) * choices
+                spread_ref[pl.ds(place, choices), pl.ds(0, rows)] = rounded[
+                    :, group * rows : (group + 1) * rows
+                ]
+        block[:, pl.ds(groups * width, 128)] = spread_ref[...].T[:rows].astype(jnp.bfloat16)
+    for copy in copies:
+        copy.wait()
+
+
+def pack(tokens, expert_ids, slot_ids, gate_values):
+    micro, tok_dev, width = tokens.shape
+    rows = 16
+    groups = tok_dev // rows
+    columns = [
+        jnp.transpose(array, (0, 2, 1)) for array in (expert_ids, slot_ids, gate_values)
+    ]
+    outside = [
+        pltpu.with_memory_space_constraint(array, pltpu.HBM) for array in [tokens] + columns
+    ]
+    inside = pl.BlockSpec(memory_space=pltpu.VMEM)
+    return pl.pallas_call(
+        pack_kernel,
+        in_specs=[pl.BlockSpec(memory_space=pl.ANY)] * len(outside),
+        out_specs=[inside] * micro,
+        out_shape=[pltpu.VMEM((rows, groups * width + 128), jnp.bfloat16)] * micro,
+        scratch_shapes=[pltpu.VMEM(array.shape, array.dtype) for array in columns]
+        + [
+            pltpu.VMEM((128, 128), jnp.float32),
+            pltpu.SemaphoreType.DMA((len(columns),)),
+            pltpu.SemaphoreType.DMA((micro, groups)),
+        ],
+        compiler_params=pltpu.CompilerParams(vmem_limit_bytes=4 * 1024 * 1024),
+        cost_estimate=pl.CostEstimate(
+            flops=10000000000, bytes_accessed=0, transcendentals=0
+        ),
+    )(*outside)
+
+
+def pass_on(block, stride):
+    across_x = lax.axis_size("ex")
+    across_y = lax.axis_size("ey")
+    ring = []
+    for row in range(across_x):
+        places = [row * across_y + column for column in range(across_y)]
+        ring += places if row % 2 == 0 else places[::-1]
+    count = len(ring)
+    pairs = [(ring[index], ring[(index + stride) % count]) for index in range(count)]
+    return lax.ppermute(block, ("ex", "ey"), pairs)
+
+
+def mark_kernel(marker_ref):
+    marker_ref[...] = jnp.zeros_like(marker_ref)
+
+
+def mark():
+    return pl.pallas_call(
+        mark_kernel,
+        out_specs=pl.BlockSpec(memory_space=pltpu.VMEM),
+        out_shape=pltpu.VMEM((8, 128), jnp.float32),
+        compiler_params=pltpu.CompilerParams(vmem_limit_bytes=1024 * 1024),
+        cost_estimate=pl.CostEstimate(flops=0, bytes_accessed=25000000, transcendentals=0),
+    )()
+
+
+def expert_kernel(count, *refs):
+    blocks = refs[:count]
+    gate_ref, up_ref, down_ref = refs[count : count + 3]
+    rows_ref, weight_ref, hidden_ref = refs[-3:]
+    outputs = refs[-3 - count : -3]
+    _, width, hidden_width = gate_ref.shape
+    rows = blocks[0].shape[0]
+    groups = blocks[0].shape[1] // width
+    tok_dev = rows * groups
+    part = 256
+
+    me = lax.axis_index("ex") * lax.axis_size("ey") + lax.axis_index("ey")
+    experts = lax.axis_size("ex") * lax.axis_size("ey")
+    lane = lax.broadcasted_iota(jnp.int32, (rows, 128), 1)
+    for index, block in enumerate(blocks):
+        gates = block[:, groups * width :].astype(jnp.float32)
+        for group in range(groups):
+            span = pl.ds(index * tok_dev + group * rows, rows)
+            rows_ref[span, :] = block[:, group * width : (group + 1) * width]
+            mine = lane < 0
+            for piece in range(3):
+                mine = mine | (lane == me + (group * 3 + piece) * experts)
+            weight_ref[span, :] = jnp.broadcast_to(
+                jnp.sum(jnp.where(mine, gates, jnp.float32(0.0)), axis=-1, keepdims=True),
+                (rows, 128),
+            )
+
+    for start in range(0, hidden_width, part):
+        columns = pl.ds(start, part)
+        tokens = rows_ref[...]
+        gate_part = jnp.dot(tokens, gate_ref[0, :, columns], preferred_element_type=jnp.float32)
+        up_part = jnp.dot(tokens, up_ref[0, :, columns], preferred_element_type=jnp.float32)
+        hidden_ref[:, columns] = (jax.nn.silu(gate_part) * up_part).astype(jnp.bfloat16)
+
+    for start in range(0, width, part):
+        columns = pl.ds(start, part)
+        output = jnp.dot(
+            hidden_ref[...], down_ref[0, :, columns], preferred_element_type=jnp.float32
+        )
+        output = output * weight_ref[:, :1]
+        for index, out in enumerate(outputs):
+            out[:, columns] = output[index * tok_dev : (index + 1) * tok_dev].astype(out.dtype)
+
+
+def run_expert(blocks, kinds, earlier, weights):
+    count = len(blocks)
+    _, width, hidden = weights[0].shape
+    tok_dev = blocks[0].shape[0] * (blocks[0].shape[1] // width)
+    rows = count * tok_dev
+    inside = [pltpu.with_memory_space_constraint(array, pltpu.VMEM) for array in blocks + weights]
+    in_vmem = pl.BlockSpec(memory_space=pltpu.VMEM)
+    out_shape = [pltpu.VMEM((tok_dev, width), kind) for kind in kinds]
+    return pl.pallas_call(
+        functools.partial(expert_kernel, count),
+        in_specs=[in_vmem] * len(inside) + [pl.BlockSpec(memory_space=pl.ANY)] * len(earlier),
+        out_specs=[in_vmem] * len(out_shape),
+        out_shape=out_shape,
+        scratch_shapes=[
+            pltpu.VMEM((rows, width), jnp.bfloat16),
+            pltpu.VMEM((rows, 128), jnp.float32),
+            pltpu.VMEM((rows, hidden), jnp.bfloat16),
+        ],
+        compiler_params=pltpu.CompilerParams(vmem_limit_bytes=16 * 1024 * 1024),
+        cost_estimate=pl.CostEstimate(
+            flops=6 * rows * width * hidden,
+            bytes_accessed=6 * width * hidden + 6 * rows * width,
+            transcendentals=rows * hidden,
+        ),
+    )(*inside, *earlier)
+
+
+def after(array, others):
+    return lax.optimization_barrier([array] + list(others))[0]
+
+
+def dense_layer(tokens, expert_ids, slot_ids, gate_values, gate_weight, up_weight, down_weight):
+    experts = lax.axis_size("ex") * lax.axis_size("ey")
+    micro = tokens.shape[0]
+
+    packed = pack(tokens, expert_ids, slot_ids, gate_values)
+
+    long_chains = [(index, 1 if index % 2 == 0 else -1) for index in range(micro)]
+    short_chains = [(index, -stride) for index, stride in long_chains]
+    chains = long_chains + short_chains[::-1]
+    long_reach, short_reach = experts // 2, (experts - 1) // 2
+
+    gathered = [{0: packed[index]} for index in range(micro)]
+    outputs = [{} for index in range(micro)]
+    carried = {}
+
+    def gather_hop(some, hop, others):
+        for index, stride in some:
+            block = gathered[index][-(hop - 1) * stride]
+            with jax.named_scope(f"gather{index}_{stride:+d}_hop{hop}"):
+                gathered[index][-hop * stride] = pass_on(after(block, others), stride)
+            others = others
+
+    def sum_hop(some, left, others):
+        sent = []
+        for index, stride in some:
+            partial = outputs[index][-left * stride]
+            before = []
+            if (index, stride) in carried:
+                before = [carried[index, stride]]
+                partial = partial + carried[index, stride].astype(jnp.float32)
+            partial = after(partial.astype(jnp.bfloat16), others)
+            with jax.named_scope(f"sum{index}_{-stride:+d}_left{left}"):
+                carried[index, stride] = pass_on(partial, -stride)
+            sent.append(partial)
+            others = others
+        return sent
+
+    def expert(some, hops, earlier):
+        keys = [(index, -hop * stride) for hop in hops for index, stride in some]
+        keys = list(dict.fromkeys(keys))
+        first = {(index, -long_reach * stride) for index, stride in long_chains}
+        first |= {(index, -short_reach * stride) for index, stride in short_chains}
+        answers = run_expert(
+            [gathered[index][place] for index, place in keys],
+            [jnp.bfloat16 if key in first else jnp.float32 for key in keys],
+            earlier,
+            weights,
+        )
+        for (index, place), answer in zip(keys, answers):
+            outputs[index][place] = answer
+        return [answers[0]]
+
+    weights = [gate_weight, up_weight, down_weight]
+    marker = mark()
+    done = []
+    for hop in range(1, short_reach + 1):
+        gather_hop(long_chains, hop, [marker])
+        gather_hop(short_chains[::-1], hop, [])
+        if hop == short_reach - 1:
+            done = expert(chains, range(short_reach - 2, -1, -1), [])
+    done = expert(chains, [short_reach - 1], done)
+    gather_hop(long_chains, long_reach, done)
+    done = expert(long_chains, [short_reach], done)
+    done = expert(short_chains[::-1], [short_reach], done)
+    last = [gathered[index][-long_reach * stride] for index, stride in long_chains]
+    done = expert(long_chains, [long_reach], done)
+    for left in range(long_reach, 0, -1):
+        sent = sum_hop(long_chains, left, [])
+        if left > 1:
+            sent = sum_hop(short_chains[:1], left - 1, last + sent)
+            sum_hop(short_chains[1:], left - 1, last + sent)
+
+    results = []
+    for index in range(micro):
+        total = outputs[index][0]
+        for stride in (1, -1):
+            total = total + carried[index, stride].astype(jnp.float32)
+        results.append(total.astype(jnp.bfloat16))
+    return jnp.stack(results, axis=0)
+
+
+def per_device(tokens, expert_ids, slot_ids, gate_values, gate_weight, up_weight, down_weight):
+    experts = lax.axis_size("ex") * lax.axis_size("ey")
+    layer = dense_layer if experts == expert_ids.shape[-1] else slot_layer
+    return layer(
+        tokens, expert_ids, slot_ids, gate_values, gate_weight, up_weight, down_weight
+    )
 
 
 def solution(mesh):

time: 221 us -> 71.9 us (0.33)
  waiting for transfers between devices: 140 us -> 25.1 us
  matrix products: 39.9 us -> 0 us
  local copies, waits for them, and re-layouts: 18.1 us -> 0.01 us
  Pallas kernels: 0 us -> 14.6 us
  starting transfers between devices: 19.9 us -> 30.6 us
    all_to_all x4 -> x0, waiting for transfers between devices: 140 us -> none  [the longest x2 71.6 us: route_slots(): lax.all_to_all(buffer, ('ex', 'ey'), split_axis=0, concat_axis=0, tiled=T...]
    dot_general x8 -> x0, matrix products: 39.9 us -> none  [the longest x2 19.8 us: expert_apply(): jnp.dot(hidden, down_matrix, preferred_element_type=jnp.float32)]
    ppermute x0 -> x28, starting transfers between devices: none -> 30.6 us  [pass_on(): return lax.ppermute(block, ('ex', 'ey'), pairs)]
    ppermute x0 -> x28, waiting for transfers between devices: none -> 25.1 us  [pass_on(): return lax.ppermute(block, ('ex', 'ey'), pairs)]
    all_to_all x4 -> x0, starting transfers between devices: 19.9 us -> none  [the longest x2 11.7 us: route_slots(): lax.all_to_all(buffer, ('ex', 'ey'), split_axis=0, concat_axis=0, tiled=T...]
    reshape x8 -> x0, local copies, waits for them, and re-layouts: 17.1 us -> none  [the longest x2 5.42 us: expert_apply(): return output.reshape(received.shape)]
    pallas_call x0 -> x6, Pallas kernels: none -> 14.6 us  [the longest x5 13.3 us: run_expert(): pl.pallas_call(functools.partial(expert_kernel, count), in_specs=[in_vmem...]
  transfers between devices with their start and end apart: 4 -> 28, of which waited for: 4 -> 12; matrix products, arithmetic and copies ran while one was open for 23% -> 1% of each run, Pallas kernels for 0% -> 15%
where the time goes in v1:
time: 71.9 us; the launch traced here: 71.8 us
  starting transfers between devices  30.6 us (43%)
  waiting for transfers between devices  25.1 us (35%)
  Pallas kernels  14.6 us (20%)
  other arithmetic  1.35 us (2%)
    ppermute x28, starting transfers between devices, pass_on(): return lax.ppermute(block, ('ex', 'ey'), pairs)  30.6 us
    ppermute x28, waiting for transfers between devices, pass_on(): return lax.ppermute(block, ('ex', 'ey'), pairs)  25.1 us
    pallas_call x5, Pallas kernels, run_expert(): pl.pallas_call(functools.partial(expert_kernel, count), in_specs=[in_vmem...  13.3 us
  transfers between devices with their start and end apart: 28, of which 12 were waited for; matrix products, arithmetic and copies ran while one was open for 1% of the time, Pallas kernels for 15%

profile of v1, /device:TPU:0, one launch (start us, length us, event | category | flops | bytes accessed | tf_op | source)
XLA Modules:
  0.0 71.8 jit_solution(2574828783989202614)
XLA Ops:
  1.3 3.0 %collective-permute-start.1 = (bf16[16,6272]{1,0:T(8,128)(2,1)S(1)}, bf16[16,6272]{1,0:T(8,128)(2,1)S(1)}, u32[]{:S(2)}, u32[]{:S(2)}) collective-permute-start(bf16[16,6272]{1,0:T(8,128)(2,1)S(1)} %get-tuple-element.40.refs_5_), channel_id=1, source_target_pairs={{0,4},{1,0},{2,1},{3,2},{7,3},{6,7},{5,6},{4,5},{8,12},{9,8},{10,9... | collective-permute-start | bytes 602120 | tf_op jit(solution)/shard_map/gather1_-1_hop1/ppermute | solution.py:155
  4.4 2.0 %collective-permute-start.2 = (bf16[16,6272]{1,0:T(8,128)(2,1)S(1)}, bf16[16,6272]{1,0:T(8,128)(2,1)S(1)}, u32[]{:S(2)}, u32[]{:S(2)}) collective-permute-start(bf16[16,6272]{1,0:T(8,128)(2,1)S(1)} %get-tuple-element.40.refs_5_), channel_id=1, source_target_pairs={{0,1},{1,2},{2,3},{3,7},{7,6},{6,5},{5,4},{4,0},{8,9},{9,10},{10,1... | collective-permute-start | bytes 602120 | tf_op jit(solution)/shard_map/gather1_+1_hop1/ppermute | solution.py:155
  6.5 3.7 %collective-permute-done.1.refs_1_ = bf16[16,6272]{1,0:T(8,128)(2,1)S(1)} collective-permute-done((bf16[16,6272]{1,0:T(8,128)(2,1)S(1)}, bf16[16,6272]{1,0:T(8,128)(2,1)S(1)}, u32[]{:S(2)}, u32[]{:S(2)}) %collective-permute-start.1) | collective-permute-done | bytes 200736 | tf_op jit(solution)/shard_map/gather1_-1_hop1/ppermute | solution.py:155
  10.2 2.0 %collective-permute-start.5 = (bf16[16,6272]{1,0:T(8,128)(2,1)S(1)}, bf16[16,6272]{1,0:T(8,128)(2,1)S(1)}, u32[]{:S(2)}, u32[]{:S(2)}) collective-permute-start(bf16[16,6272]{1,0:T(8,128)(2,1)S(1)} %collective-permute-done.1.refs_1_), channel_id=1, source_target_pairs={{0,4},{1,0},{2,1},{3,2},{7,3},{6,7},{5,6},{4,5},{8,12},{9,8},{10,9... | collective-permute-start | bytes 602120 | tf_op jit(solution)/shard_map/gather1_-1_hop2/ppermute | solution.py:155
  12.3 4.2 %collective-permute-done.2.refs_2_ = bf16[16,6272]{1,0:T(8,128)(2,1)S(1)} collective-permute-done((bf16[16,6272]{1,0:T(8,128)(2,1)S(1)}, bf16[16,6272]{1,0:T(8,128)(2,1)S(1)}, u32[]{:S(2)}, u32[]{:S(2)}) %collective-permute-start.2) | collective-permute-done | bytes 200736 | tf_op jit(solution)/shard_map/gather1_+1_hop1/ppermute | solution.py:155
  16.6 1.9 %collective-permute-start.7 = (bf16[16,6272]{1,0:T(8,128)(2,1)S(1)}, bf16[16,6272]{1,0:T(8,128)(2,1)S(1)}, u32[]{:S(2)}, u32[]{:S(2)}) collective-permute-start(bf16[16,6272]{1,0:T(8,128)(2,1)S(1)} %collective-permute-done.3.refs_3_), channel_id=1, source_target_pairs={{0,4},{1,0},{2,1},{3,2},{7,3},{6,7},{5,6},{4,5},{8,12},{9,8},{10,9... | collective-permute-start | bytes 602120 | tf_op jit(solution)/shard_map/gather0_-1_hop2/ppermute | solution.py:155
  18.6 4.0 %shard_map.74 = (f32[48,2048]{1,0:T(8,128)S(1)}, f32[48,2048]{1,0:T(8,128)S(1)}, f32[48,2048]{1,0:T(8,128)S(1)}, f32[48,2048]{1,0:T(8,128)S(1)}, f32[48,2048]{1,0:T(8,128)S(1)}, /*index=5*/f32[48,2048]{1,0:T(8,128)S(1)}) custom-call(bf16[16,6272]{1,0:T(8,128)(2,1)S(1)} %collective-permute-done.refs_0_, bf16[16,6272]{1,0:T(8,128)(2,1)S(1)} %collective-permute-done.1.refs_1_, ...), custom_call_target="tpu_custom_call" | custom-call | flops 3623878656 | bytes 16121856 | tf_op jit(solution)/shard_map/pallas_call | solution.py:224
  22.5 1.6 %collective-permute-start.9 = (bf16[16,6272]{1,0:T(8,128)(2,1)S(1)}, bf16[16,6272]{1,0:T(8,128)(2,1)S(1)}, u32[]{:S(2)}, u32[]{:S(2)}) collective-permute-start(bf16[16,6272]{1,0:T(8,128)(2,1)S(1)} %collective-permute-done.5.refs_1_), channel_id=1, source_target_pairs={{0,4},{1,0},{2,1},{3,2},{7,3},{6,7},{5,6},{4,5},{8,12},{9,8},{10,9... | collective-permute-start | bytes 602120 | tf_op jit(solution)/shard_map/gather1_-1_hop3/ppermute | solution.py:155
  24.8 1.9 %collective-permute-start.13 = (bf16[16,6272]{1,0:T(8,128)(2,1)S(1)}, bf16[16,6272]{1,0:T(8,128)(2,1)S(1)}, u32[]{:S(2)}, u32[]{:S(2)}) collective-permute-start(bf16[16,6272]{1,0:T(8,128)(2,1)S(1)} %collective-permute-done.7.refs_3_), channel_id=1, source_target_pairs={{0,4},{1,0},{2,1},{3,2},{7,3},{6,7},{5,6},{4,5},{8,12},{9,8},{10,9... | collective-permute-start | bytes 602120 | tf_op jit(solution)/shard_map/gather0_-1_hop3/ppermute | solution.py:155
  26.7 2.7 %shard_map.75 = (f32[48,2048]{1,0:T(8,128)S(1)}, f32[48,2048]{1,0:T(8,128)S(1)}, f32[48,2048]{1,0:T(8,128)S(1)}, f32[48,2048]{1,0:T(8,128)S(1)}) custom-call(bf16[16,6272]{1,0:T(8,128)(2,1)S(1)} %collective-permute-done.4.refs_0_, bf16[16,6272]{1,0:T(8,128)(2,1)S(1)} %collective-permute-done.5.refs_1_, bf16[16,6272]{1,0:T(8,128)(2,1)S(1)} %collective-permute-done.6.refs_2_, ...), custom_call_target="tpu_custom_call" | custom-call | flops 2415919104 | bytes 14942208 | tf_op jit(solution)/shard_map/pallas_call | solution.py:224
  29.7 1.3 %collective-permute-done.8.refs_0_ = bf16[16,6272]{1,0:T(8,128)(2,1)S(1)} collective-permute-done((bf16[16,6272]{1,0:T(8,128)(2,1)S(1)}, bf16[16,6272]{1,0:T(8,128)(2,1)S(1)}, u32[]{:S(2)}, u32[]{:S(2)}) %collective-permute-start.8) | collective-permute-done | bytes 200736 | tf_op jit(solution)/shard_map/gather0_+1_hop3/ppermute | solution.py:155
  31.1 1.9 %collective-permute-start.11 = (bf16[16,6272]{1,0:T(8,128)(2,1)S(1)}, bf16[16,6272]{1,0:T(8,128)(2,1)S(1)}, u32[]{:S(2)}, u32[]{:S(2)}) collective-permute-start(bf16[16,6272]{1,0:T(8,128)(2,1)S(1)} %collective-permute-done.9.refs_1_), channel_id=1, source_target_pairs={{0,4},{1,0},{2,1},{3,2},{7,3},{6,7},{5,6},{4,5},{8,12},{9,8},{10,9... | collective-permute-start | bytes 602120 | tf_op jit(solution)/shard_map/gather1_-1_hop4/ppermute | solution.py:155
  33.0 2.2 %shard_map.76 = (f32[48,2048]{1,0:T(8,128)S(1)}, f32[48,2048]{1,0:T(8,128)S(1)}) custom-call(bf16[16,6272]{1,0:T(8,128)(2,1)S(1)} %collective-permute-done.8.refs_0_, bf16[16,6272]{1,0:T(8,128)(2,1)S(1)} %collective-permute-done.9.refs_1_, bf16[1,2048,1024]{2,1,0:T(8,128)(2,1)S(1)} %copy-done, bf16[1,2048,1024]{2,1,0:T(8,128)(2,1)S(1)} %copy-done.1, ...), custom_call_target="tpu_custom_call" | custom-call | flops 1207959552 | bytes 13762560 | tf_op jit(solution)/shard_map/pallas_call | solution.py:224
  35.3 2.2 %shard_map.77 = (bf16[48,2048]{1,0:T(8,128)(2,1)S(1)}, bf16[48,2048]{1,0:T(8,128)(2,1)S(1)}) custom-call(bf16[16,6272]{1,0:T(8,128)(2,1)S(1)} %collective-permute-done.12.refs_0_, bf16[16,6272]{1,0:T(8,128)(2,1)S(1)} %collective-permute-done.13.refs_1_, bf16[1,2048,1024]{2,1,0:T(8,128)(2,1)S(1)} %copy-done, bf16[1,2048,1024]{2,1,0:T(8,128)(2,1)S(1)} %copy-done.1, ...), custom_call_target="tpu_custom_call" | custom-call | flops 1207959552 | bytes 13762560 | tf_op jit(solution)/shard_map/pallas_call | solution.py:224
  37.5 2.2 %shard_map.78 = (bf16[48,2048]{1,0:T(8,128)(2,1)S(1)}, bf16[48,2048]{1,0:T(8,128)(2,1)S(1)}) custom-call(bf16[16,6272]{1,0:T(8,128)(2,1)S(1)} %collective-permute-done.10.refs_0_, bf16[16,6272]{1,0:T(8,128)(2,1)S(1)} %collective-permute-done.11.refs_1_, bf16[1,2048,1024]{2,1,0:T(8,128)(2,1)S(1)} %copy-done, bf16[1,2048,1024]{2,1,0:T(8,128)(2,1)S(1)} %copy-done.1, ...), custom_call_target="tpu_custom_call" | custom-call | flops 1207959552 | bytes 13762560 | tf_op jit(solution)/shard_map/pallas_call | solution.py:224
  43.8 3.5 %collective-permute-done.19 = bf16[48,2048]{1,0:T(8,128)(2,1)S(1)} collective-permute-done((bf16[48,2048]{1,0:T(8,128)(2,1)S(1)}, bf16[48,2048]{1,0:T(8,128)(2,1)S(1)}, u32[]{:S(2)}, u32[]{:S(2)}) %collective-permute-start.19) | collective-permute-done | bytes 196640 | tf_op jit(solution)/shard_map/sum1_+1_left4/ppermute | solution.py:155
  49.6 1.9 %collective-permute-done.18 = bf16[48,2048]{1,0:T(8,128)(2,1)S(1)} collective-permute-done((bf16[48,2048]{1,0:T(8,128)(2,1)S(1)}, bf16[48,2048]{1,0:T(8,128)(2,1)S(1)}, u32[]{:S(2)}, u32[]{:S(2)}) %collective-permute-start.18) | collective-permute-done | bytes 196640 | tf_op jit(solution)/shard_map/sum0_+1_left3/ppermute | solution.py:155
  53.9 1.9 %collective-permute-done.21 = bf16[48,2048]{1,0:T(8,128)(2,1)S(1)} collective-permute-done((bf16[48,2048]{1,0:T(8,128)(2,1)S(1)}, bf16[48,2048]{1,0:T(8,128)(2,1)S(1)}, u32[]{:S(2)}, u32[]{:S(2)}) %collective-permute-start.21) | collective-permute-done | bytes 196640 | tf_op jit(solution)/shard_map/sum1_+1_left3/ppermute | solution.py:155
  56.7 1.3 %collective-permute-start.16 = (bf16[48,2048]{1,0:T(8,128)(2,1)S(1)}, bf16[48,2048]{1,0:T(8,128)(2,1)S(1)}, u32[]{:S(2)}, u32[]{:S(2)}) collective-permute-start(bf16[48,2048]{1,0:T(8,128)(2,1)S(1)} %add_convert_fusion.10), channel_id=1, source_target_pairs={{0,4},{1,0},{2,1},{3,2},{7,3},{6,7},{5,6},{4,5},{8,12},{9,8},{10,9... | collective-permute-start | bytes 589832 | tf_op jit(solution)/shard_map/sum0_-1_left2/ppermute | solution.py:155
  58.1 1.9 %collective-permute-done.20 = bf16[48,2048]{1,0:T(8,128)(2,1)S(1)} collective-permute-done((bf16[48,2048]{1,0:T(8,128)(2,1)S(1)}, bf16[48,2048]{1,0:T(8,128)(2,1)S(1)}, u32[]{:S(2)}, u32[]{:S(2)}) %collective-permute-start.20) | collective-permute-done | bytes 196640 | tf_op jit(solution)/shard_map/sum0_+1_left2/ppermute | solution.py:155
  61.0 1.3 %collective-permute-start.25 = (bf16[48,2048]{1,0:T(8,128)(2,1)S(1)}, bf16[48,2048]{1,0:T(8,128)(2,1)S(1)}, u32[]{:S(2)}, u32[]{:S(2)}) collective-permute-start(bf16[48,2048]{1,0:T(8,128)(2,1)S(1)} %add_convert_fusion.2), channel_id=1, source_target_pairs={{0,4},{1,0},{2,1},{3,2},{7,3},{6,7},{5,6},{4,5},{8,12},{9,8},{10,9... | collective-permute-start | bytes 589832 | tf_op jit(solution)/shard_map/sum1_-1_left1/ppermute | solution.py:155
  62.3 1.9 %collective-permute-done.26 = bf16[48,2048]{1,0:T(8,128)(2,1)S(1)} collective-permute-done((bf16[48,2048]{1,0:T(8,128)(2,1)S(1)}, bf16[48,2048]{1,0:T(8,128)(2,1)S(1)}, u32[]{:S(2)}, u32[]{:S(2)}) %collective-permute-start.26) | collective-permute-done | bytes 196640 | tf_op jit(solution)/shard_map/sum1_+1_left2/ppermute | solution.py:155
  65.2 1.3 %collective-permute-start.17 = (bf16[48,2048]{1,0:T(8,128)(2,1)S(1)}, bf16[48,2048]{1,0:T(8,128)(2,1)S(1)}, u32[]{:S(2)}, u32[]{:S(2)}) collective-permute-start(bf16[48,2048]{1,0:T(8,128)(2,1)S(1)} %add_convert_fusion.9), channel_id=1, source_target_pairs={{0,4},{1,0},{2,1},{3,2},{7,3},{6,7},{5,6},{4,5},{8,12},{9,8},{10,9... | collective-permute-start | bytes 589832 | tf_op jit(solution)/shard_map/sum0_-1_left1/ppermute | solution.py:155
  67.4 2.5 %collective-permute-done.27 = bf16[48,2048]{1,0:T(8,128)(2,1)S(1)} collective-permute-done((bf16[48,2048]{1,0:T(8,128)(2,1)S(1)}, bf16[48,2048]{1,0:T(8,128)(2,1)S(1)}, u32[]{:S(2)}, u32[]{:S(2)}) %collective-permute-start.27) | collective-permute-done | bytes 196640 | tf_op jit(solution)/shard_map/sum1_+1_left1/ppermute | solution.py:155
  (57 shorter events, 17.0 us)
Async XLA Ops:
  1.3 8.9 %collective-permute-start.1 = (bf16[16,6272]{1,0:T(8,128)(2,1)S(1)}, bf16[16,6272]{1,0:T(8,128)(2,1)S(1)}, u32[]{:S(2)}, u32[]{:S(2)}) collective-permute-start(bf16[16,6272]{1,0:T(8,128)(2,1)S(1)} %get-tuple-element.40.refs_5_), channel_id=1, source_target_pairs={{0,4},{1,0},{2,1},{3,2},{7,3},{6,7},{5,6},{4,5},{8,12},{9,8},{10,9... | collective-permute-start | bytes 602120 | tf_op jit(solution)/shard_map/gather1_-1_hop1/ppermute | solution.py:155
  4.3 7.9 %collective-permute-start = (bf16[16,6272]{1,0:T(8,128)(2,1)S(1)}, bf16[16,6272]{1,0:T(8,128)(2,1)S(1)}, u32[]{:S(2)}, u32[]{:S(2)}) collective-permute-start(bf16[16,6272]{1,0:T(8,128)(2,1)S(1)} %get-tuple-element.38.refs_4_), channel_id=1, source_target_pairs={{0,1},{1,2},{2,3},{3,7},{7,6},{6,5},{5,4},{4,0},{8,9},{9,10},{10,1... | collective-permute-start | bytes 602120 | tf_op jit(solution)/shard_map/gather0_+1_hop1/ppermute | solution.py:155
  4.4 12.1 %collective-permute-start.2 = (bf16[16,6272]{1,0:T(8,128)(2,1)S(1)}, bf16[16,6272]{1,0:T(8,128)(2,1)S(1)}, u32[]{:S(2)}, u32[]{:S(2)}) collective-permute-start(bf16[16,6272]{1,0:T(8,128)(2,1)S(1)} %get-tuple-element.40.refs_5_), channel_id=1, source_target_pairs={{0,1},{1,2},{2,3},{3,7},{7,6},{6,5},{5,4},{4,0},{8,9},{9,10},{10,1... | collective-permute-start | bytes 602120 | tf_op jit(solution)/shard_map/gather1_+1_hop1/ppermute | solution.py:155
  6.4 10.2 %collective-permute-start.3 = (bf16[16,6272]{1,0:T(8,128)(2,1)S(1)}, bf16[16,6272]{1,0:T(8,128)(2,1)S(1)}, u32[]{:S(2)}, u32[]{:S(2)}) collective-permute-start(bf16[16,6272]{1,0:T(8,128)(2,1)S(1)} %get-tuple-element.38.refs_4_), channel_id=1, source_target_pairs={{0,4},{1,0},{2,1},{3,2},{7,3},{6,7},{5,6},{4,5},{8,12},{9,8},{10,9... | collective-permute-start | bytes 602120 | tf_op jit(solution)/shard_map/gather0_-1_hop1/ppermute | solution.py:155
  10.2 12.3 %collective-permute-start.5 = (bf16[16,6272]{1,0:T(8,128)(2,1)S(1)}, bf16[16,6272]{1,0:T(8,128)(2,1)S(1)}, u32[]{:S(2)}, u32[]{:S(2)}) collective-permute-start(bf16[16,6272]{1,0:T(8,128)(2,1)S(1)} %collective-permute-done.1.refs_1_), channel_id=1, source_target_pairs={{0,4},{1,0},{2,1},{3,2},{7,3},{6,7},{5,6},{4,5},{8,12},{9,8},{10,9... | collective-permute-start | bytes 602120 | tf_op jit(solution)/shard_map/gather1_-1_hop2/ppermute | solution.py:155
  12.2 11.9 %collective-permute-start.4 = (bf16[16,6272]{1,0:T(8,128)(2,1)S(1)}, bf16[16,6272]{1,0:T(8,128)(2,1)S(1)}, u32[]{:S(2)}, u32[]{:S(2)}) collective-permute-start(bf16[16,6272]{1,0:T(8,128)(2,1)S(1)} %collective-permute-done.refs_0_), channel_id=1, source_target_pairs={{0,1},{1,2},{2,3},{3,7},{7,6},{6,5},{5,4},{4,0},{8,9},{9,10},{10,1... | collective-permute-start | bytes 602120 | tf_op jit(solution)/shard_map/gather0_+1_hop2/ppermute | solution.py:155
  16.5 8.1 %collective-permute-start.6 = (bf16[16,6272]{1,0:T(8,128)(2,1)S(1)}, bf16[16,6272]{1,0:T(8,128)(2,1)S(1)}, u32[]{:S(2)}, u32[]{:S(2)}) collective-permute-start(bf16[16,6272]{1,0:T(8,128)(2,1)S(1)} %collective-permute-done.2.refs_2_), channel_id=1, source_target_pairs={{0,1},{1,2},{2,3},{3,7},{7,6},{6,5},{5,4},{4,0},{8,9},{9,10},{10,1... | collective-permute-start | bytes 602120 | tf_op jit(solution)/shard_map/gather1_+1_hop2/ppermute | solution.py:155
  16.6 8.1 %collective-permute-start.7 = (bf16[16,6272]{1,0:T(8,128)(2,1)S(1)}, bf16[16,6272]{1,0:T(8,128)(2,1)S(1)}, u32[]{:S(2)}, u32[]{:S(2)}) collective-permute-start(bf16[16,6272]{1,0:T(8,128)(2,1)S(1)} %collective-permute-done.3.refs_3_), channel_id=1, source_target_pairs={{0,4},{1,0},{2,1},{3,2},{7,3},{6,7},{5,6},{4,5},{8,12},{9,8},{10,9... | collective-permute-start | bytes 602120 | tf_op jit(solution)/shard_map/gather0_-1_hop2/ppermute | solution.py:155
  22.5 7.1 %collective-permute-start.9 = (bf16[16,6272]{1,0:T(8,128)(2,1)S(1)}, bf16[16,6272]{1,0:T(8,128)(2,1)S(1)}, u32[]{:S(2)}, u32[]{:S(2)}) collective-permute-start(bf16[16,6272]{1,0:T(8,128)(2,1)S(1)} %collective-permute-done.5.refs_1_), channel_id=1, source_target_pairs={{0,4},{1,0},{2,1},{3,2},{7,3},{6,7},{5,6},{4,5},{8,12},{9,8},{10,9... | collective-permute-start | bytes 602120 | tf_op jit(solution)/shard_map/gather1_-1_hop3/ppermute | solution.py:155
  24.2 6.8 %collective-permute-start.8 = (bf16[16,6272]{1,0:T(8,128)(2,1)S(1)}, bf16[16,6272]{1,0:T(8,128)(2,1)S(1)}, u32[]{:S(2)}, u32[]{:S(2)}) collective-permute-start(bf16[16,6272]{1,0:T(8,128)(2,1)S(1)} %collective-permute-done.4.refs_0_), channel_id=1, source_target_pairs={{0,1},{1,2},{2,3},{3,7},{7,6},{6,5},{5,4},{4,0},{8,9},{9,10},{10,1... | collective-permute-start | bytes 602120 | tf_op jit(solution)/shard_map/gather0_+1_hop3/ppermute | solution.py:155
  24.6 10.6 %collective-permute-start.12 = (bf16[16,6272]{1,0:T(8,128)(2,1)S(1)}, bf16[16,6272]{1,0:T(8,128)(2,1)S(1)}, u32[]{:S(2)}, u32[]{:S(2)}) collective-permute-start(bf16[16,6272]{1,0:T(8,128)(2,1)S(1)} %collective-permute-done.6.refs_2_), channel_id=1, source_target_pairs={{0,1},{1,2},{2,3},{3,7},{7,6},{6,5},{5,4},{4,0},{8,9},{9,10},{10,1... | collective-permute-start | bytes 602120 | tf_op jit(solution)/shard_map/gather1_+1_hop3/ppermute | solution.py:155
  24.8 10.5 %collective-permute-start.13 = (bf16[16,6272]{1,0:T(8,128)(2,1)S(1)}, bf16[16,6272]{1,0:T(8,128)(2,1)S(1)}, u32[]{:S(2)}, u32[]{:S(2)}) collective-permute-start(bf16[16,6272]{1,0:T(8,128)(2,1)S(1)} %collective-permute-done.7.refs_3_), channel_id=1, source_target_pairs={{0,4},{1,0},{2,1},{3,2},{7,3},{6,7},{5,6},{4,5},{8,12},{9,8},{10,9... | collective-permute-start | bytes 602120 | tf_op jit(solution)/shard_map/gather0_-1_hop3/ppermute | solution.py:155
  31.0 6.5 %collective-permute-start.10 = (bf16[16,6272]{1,0:T(8,128)(2,1)S(1)}, bf16[16,6272]{1,0:T(8,128)(2,1)S(1)}, u32[]{:S(2)}, u32[]{:S(2)}) collective-permute-start(bf16[16,6272]{1,0:T(8,128)(2,1)S(1)} %collective-permute-done.8.refs_0_), channel_id=1, source_target_pairs={{0,1},{1,2},{2,3},{3,7},{7,6},{6,5},{5,4},{4,0},{8,9},{9,10},{10,1... | collective-permute-start | bytes 602120 | tf_op jit(solution)/shard_map/gather0_+1_hop4/ppermute | solution.py:155
  39.7 7.6 %collective-permute-start.19 = (bf16[48,2048]{1,0:T(8,128)(2,1)S(1)}, bf16[48,2048]{1,0:T(8,128)(2,1)S(1)}, u32[]{:S(2)}, u32[]{:S(2)}) collective-permute-start(bf16[48,2048]{1,0:T(8,128)(2,1)S(1)} %get-tuple-element.56), channel_id=1, source_target_pairs={{0,1},{1,2},{2,3},{3,7},{7,6},{6,5},{5,4},{4,0},{8,9},{9,10},{10,1... | collective-permute-start | bytes 589832 | tf_op jit(solution)/shard_map/sum1_+1_left4/ppermute | solution.py:155
  40.7 7.6 %collective-permute-start.14 = (bf16[48,2048]{1,0:T(8,128)(2,1)S(1)}, bf16[48,2048]{1,0:T(8,128)(2,1)S(1)}, u32[]{:S(2)}, u32[]{:S(2)}) collective-permute-start(bf16[48,2048]{1,0:T(8,128)(2,1)S(1)} %get-tuple-element.52), channel_id=1, source_target_pairs={{0,4},{1,0},{2,1},{3,2},{7,3},{6,7},{5,6},{4,5},{8,12},{9,8},{10,9... | collective-permute-start | bytes 589832 | tf_op jit(solution)/shard_map/sum0_-1_left4/ppermute | solution.py:155
  41.8 9.7 %collective-permute-start.18 = (bf16[48,2048]{1,0:T(8,128)(2,1)S(1)}, bf16[48,2048]{1,0:T(8,128)(2,1)S(1)}, u32[]{:S(2)}, u32[]{:S(2)}) collective-permute-start(bf16[48,2048]{1,0:T(8,128)(2,1)S(1)} %get-tuple-element.57), channel_id=1, source_target_pairs={{0,1},{1,2},{2,3},{3,7},{7,6},{6,5},{5,4},{4,0},{8,9},{9,10},{10,1... | collective-permute-start | bytes 589832 | tf_op jit(solution)/shard_map/sum0_+1_left3/ppermute | solution.py:155
  42.7 9.8 %collective-permute-start.23 = (bf16[48,2048]{1,0:T(8,128)(2,1)S(1)}, bf16[48,2048]{1,0:T(8,128)(2,1)S(1)}, u32[]{:S(2)}, u32[]{:S(2)}) collective-permute-start(bf16[48,2048]{1,0:T(8,128)(2,1)S(1)} %get-tuple-element.65.refs_5_), channel_id=1, source_target_pairs={{0,4},{1,0},{2,1},{3,2},{7,3},{6,7},{5,6},{4,5},{8,12},{9,8},{10,9... | collective-permute-start | bytes 589832 | tf_op jit(solution)/shard_map/sum1_-1_left3/ppermute | solution.py:155
  47.4 8.4 %collective-permute-start.21 = (bf16[48,2048]{1,0:T(8,128)(2,1)S(1)}, bf16[48,2048]{1,0:T(8,128)(2,1)S(1)}, u32[]{:S(2)}, u32[]{:S(2)}) collective-permute-start(bf16[48,2048]{1,0:T(8,128)(2,1)S(1)} %add_convert_fusion.7), channel_id=1, source_target_pairs={{0,1},{1,2},{2,3},{3,7},{7,6},{6,5},{5,4},{4,0},{8,9},{9,10},{10,1... | collective-permute-start | bytes 589832 | tf_op jit(solution)/shard_map/sum1_+1_left3/ppermute | solution.py:155
  48.3 8.4 %collective-permute-start.15 = (bf16[48,2048]{1,0:T(8,128)(2,1)S(1)}, bf16[48,2048]{1,0:T(8,128)(2,1)S(1)}, u32[]{:S(2)}, u32[]{:S(2)}) collective-permute-start(bf16[48,2048]{1,0:T(8,128)(2,1)S(1)} %add_convert_fusion.11), channel_id=1, source_target_pairs={{0,4},{1,0},{2,1},{3,2},{7,3},{6,7},{5,6},{4,5},{8,12},{9,8},{10,9... | collective-permute-start | bytes 589832 | tf_op jit(solution)/shard_map/sum0_-1_left3/ppermute | solution.py:155
  51.6 8.4 %collective-permute-start.20 = (bf16[48,2048]{1,0:T(8,128)(2,1)S(1)}, bf16[48,2048]{1,0:T(8,128)(2,1)S(1)}, u32[]{:S(2)}, u32[]{:S(2)}) collective-permute-start(bf16[48,2048]{1,0:T(8,128)(2,1)S(1)} %add_convert_fusion.8), channel_id=1, source_target_pairs={{0,1},{1,2},{2,3},{3,7},{7,6},{6,5},{5,4},{4,0},{8,9},{9,10},{10,1... | collective-permute-start | bytes 589832 | tf_op jit(solution)/shard_map/sum0_+1_left2/ppermute | solution.py:155
  52.5 8.4 %collective-permute-start.24 = (bf16[48,2048]{1,0:T(8,128)(2,1)S(1)}, bf16[48,2048]{1,0:T(8,128)(2,1)S(1)}, u32[]{:S(2)}, u32[]{:S(2)}) collective-permute-start(bf16[48,2048]{1,0:T(8,128)(2,1)S(1)} %add_convert_fusion.3), channel_id=1, source_target_pairs={{0,4},{1,0},{2,1},{3,2},{7,3},{6,7},{5,6},{4,5},{8,12},{9,8},{10,9... | collective-permute-start | bytes 589832 | tf_op jit(solution)/shard_map/sum1_-1_left2/ppermute | solution.py:155
  55.8 8.4 %collective-permute-start.26 = (bf16[48,2048]{1,0:T(8,128)(2,1)S(1)}, bf16[48,2048]{1,0:T(8,128)(2,1)S(1)}, u32[]{:S(2)}, u32[]{:S(2)}) collective-permute-start(bf16[48,2048]{1,0:T(8,128)(2,1)S(1)} %add_convert_fusion.5), channel_id=1, source_target_pairs={{0,1},{1,2},{2,3},{3,7},{7,6},{6,5},{5,4},{4,0},{8,9},{9,10},{10,1... | collective-permute-start | bytes 589832 | tf_op jit(solution)/shard_map/sum1_+1_left2/ppermute | solution.py:155
  56.7 8.4 %collective-permute-start.16 = (bf16[48,2048]{1,0:T(8,128)(2,1)S(1)}, bf16[48,2048]{1,0:T(8,128)(2,1)S(1)}, u32[]{:S(2)}, u32[]{:S(2)}) collective-permute-start(bf16[48,2048]{1,0:T(8,128)(2,1)S(1)} %add_convert_fusion.10), channel_id=1, source_target_pairs={{0,4},{1,0},{2,1},{3,2},{7,3},{6,7},{5,6},{4,5},{8,12},{9,8},{10,9... | collective-permute-start | bytes 589832 | tf_op jit(solution)/shard_map/sum0_-1_left2/ppermute | solution.py:155
  60.0 10.0 %collective-permute-start.22 = (bf16[48,2048]{1,0:T(8,128)(2,1)S(1)}, bf16[48,2048]{1,0:T(8,128)(2,1)S(1)}, u32[]{:S(2)}, u32[]{:S(2)}) collective-permute-start(bf16[48,2048]{1,0:T(8,128)(2,1)S(1)} %add_convert_fusion.6), channel_id=1, source_target_pairs={{0,1},{1,2},{2,3},{3,7},{7,6},{6,5},{5,4},{4,0},{8,9},{9,10},{10,1... | collective-permute-start | bytes 589832 | tf_op jit(solution)/shard_map/sum0_+1_left1/ppermute | solution.py:155
  (7 other events, 80.1 us)

commit v2 on v1

--- a/solution.py
+++ b/solution.py
@@ -252,7 +252,7 @@
 
     long_chains = [(index, 1 if index % 2 == 0 else -1) for index in range(micro)]
     short_chains = [(index, -stride) for index, stride in long_chains]
-    chains = long_chains + short_chains[::-1]
+    chains = [short_chains[1], short_chains[0], long_chains[0], long_chains[1]]
     long_reach, short_reach = experts // 2, (experts - 1) // 2
 
     gathered = [{0: packed[index]} for index in range(micro)]
@@ -300,8 +300,8 @@
     marker = mark()
     done = []
     for hop in range(1, short_reach + 1):
-        gather_hop(long_chains, hop, [marker])
-        gather_hop(short_chains[::-1], hop, [])
+        gather_hop(long_chains + short_chains[1:], hop, [marker])
+        gather_hop(short_chains[:1], hop, [])
         if hop == short_reach - 1:
             done = expert(chains, range(short_reach - 2, -1, -1), [])
     done = expert(chains, [short_reach - 1], done)

time: 71.9 us -> 72.9 us (1.014)
  waiting for transfers between devices: 25.1 us -> 26.3 us
    ppermute x28, waiting for transfers between devices: 25.1 us -> 26.3 us  [pass_on(): return lax.ppermute(block, ('ex', 'ey'), pairs)]
  transfers between devices with their start and end apart: 28 -> 28, of which waited for: 12 -> 18; matrix products, arithmetic and copies ran while one was open for 1% -> 1% of each run, Pallas kernels for 15% -> 15%
where the time goes in v2:
time: 72.9 us; the launch traced here: 72.8 us
  starting transfers between devices  30.3 us (42%)
  waiting for transfers between devices  26.3 us (36%)
  Pallas kernels  14.6 us (20%)
  other arithmetic  1.35 us (2%)
    ppermute x28, starting transfers between devices, pass_on(): return lax.ppermute(block, ('ex', 'ey'), pairs)  30.3 us
    ppermute x28, waiting for transfers between devices, pass_on(): return lax.ppermute(block, ('ex', 'ey'), pairs)  26.3 us
    pallas_call x5, Pallas kernels, run_expert(): pl.pallas_call(functools.partial(expert_kernel, count), in_specs=[in_vmem...  13.4 us
  transfers between devices with their start and end apart: 28, of which 18 were waited for; matrix products, arithmetic and copies ran while one was open for 1% of the time, Pallas kernels for 15%

profile of v2, /device:TPU:0, one launch (start us, length us, event | category | flops | bytes accessed | tf_op | source)
XLA Modules:
  0.0 72.8 jit_solution(844010741077178472)
XLA Ops:
  1.3 3.1 %collective-permute-start.2 = (bf16[16,6272]{1,0:T(8,128)(2,1)S(1)}, bf16[16,6272]{1,0:T(8,128)(2,1)S(1)}, u32[]{:S(2)}, u32[]{:S(2)}) collective-permute-start(bf16[16,6272]{1,0:T(8,128)(2,1)S(1)} %get-tuple-element.42.refs_5_), channel_id=1, source_target_pairs={{0,1},{1,2},{2,3},{3,7},{7,6},{6,5},{5,4},{4,0},{8,9},{9,10},{10,1... | collective-permute-start | bytes 602120 | tf_op jit(solution)/shard_map/gather0_+1_hop1/ppermute | solution.py:155
  4.4 2.0 %collective-permute-start = (bf16[16,6272]{1,0:T(8,128)(2,1)S(1)}, bf16[16,6272]{1,0:T(8,128)(2,1)S(1)}, u32[]{:S(2)}, u32[]{:S(2)}) collective-permute-start(bf16[16,6272]{1,0:T(8,128)(2,1)S(1)} %get-tuple-element.40.refs_4_), channel_id=1, source_target_pairs={{0,1},{1,2},{2,3},{3,7},{7,6},{6,5},{5,4},{4,0},{8,9},{9,10},{10,1... | collective-permute-start | bytes 602120 | tf_op jit(solution)/shard_map/gather1_+1_hop1/ppermute | solution.py:155
  6.4 3.7 %collective-permute-done.2.refs_2_ = bf16[16,6272]{1,0:T(8,128)(2,1)S(1)} collective-permute-done((bf16[16,6272]{1,0:T(8,128)(2,1)S(1)}, bf16[16,6272]{1,0:T(8,128)(2,1)S(1)}, u32[]{:S(2)}, u32[]{:S(2)}) %collective-permute-start.2) | collective-permute-done | bytes 200736 | tf_op jit(solution)/shard_map/gather0_+1_hop1/ppermute | solution.py:155
  10.1 2.1 %collective-permute-start.6 = (bf16[16,6272]{1,0:T(8,128)(2,1)S(1)}, bf16[16,6272]{1,0:T(8,128)(2,1)S(1)}, u32[]{:S(2)}, u32[]{:S(2)}) collective-permute-start(bf16[16,6272]{1,0:T(8,128)(2,1)S(1)} %collective-permute-done.2.refs_2_), channel_id=1, source_target_pairs={{0,1},{1,2},{2,3},{3,7},{7,6},{6,5},{5,4},{4,0},{8,9},{9,10},{10,1... | collective-permute-start | bytes 602120 | tf_op jit(solution)/shard_map/gather0_+1_hop2/ppermute | solution.py:155
  12.3 2.1 %collective-permute-done.refs_0_ = bf16[16,6272]{1,0:T(8,128)(2,1)S(1)} collective-permute-done((bf16[16,6272]{1,0:T(8,128)(2,1)S(1)}, bf16[16,6272]{1,0:T(8,128)(2,1)S(1)}, u32[]{:S(2)}, u32[]{:S(2)}) %collective-permute-start) | collective-permute-done | bytes 200736 | tf_op jit(solution)/shard_map/gather1_+1_hop1/ppermute | solution.py:155
  14.4 2.1 %collective-permute-start.4 = (bf16[16,6272]{1,0:T(8,128)(2,1)S(1)}, bf16[16,6272]{1,0:T(8,128)(2,1)S(1)}, u32[]{:S(2)}, u32[]{:S(2)}) collective-permute-start(bf16[16,6272]{1,0:T(8,128)(2,1)S(1)} %collective-permute-done.refs_0_), channel_id=1, source_target_pairs={{0,1},{1,2},{2,3},{3,7},{7,6},{6,5},{5,4},{4,0},{8,9},{9,10},{10,1... | collective-permute-start | bytes 602120 | tf_op jit(solution)/shard_map/gather1_+1_hop2/ppermute | solution.py:155
  16.6 4.0 %shard_map.74 = (f32[48,2048]{1,0:T(8,128)S(1)}, f32[48,2048]{1,0:T(8,128)S(1)}, f32[48,2048]{1,0:T(8,128)S(1)}, f32[48,2048]{1,0:T(8,128)S(1)}, f32[48,2048]{1,0:T(8,128)S(1)}, /*index=5*/f32[48,2048]{1,0:T(8,128)S(1)}) custom-call(bf16[16,6272]{1,0:T(8,128)(2,1)S(1)} %collective-permute-done.refs_0_, bf16[16,6272]{1,0:T(8,128)(2,1)S(1)} %collective-permute-done.1.refs_1_, ...), custom_call_target="tpu_custom_call" | custom-call | flops 3623878656 | bytes 16121856 | tf_op jit(solution)/shard_map/pallas_call | solution.py:224
  20.6 2.1 %collective-permute-start.8 = (bf16[16,6272]{1,0:T(8,128)(2,1)S(1)}, bf16[16,6272]{1,0:T(8,128)(2,1)S(1)}, u32[]{:S(2)}, u32[]{:S(2)}) collective-permute-start(bf16[16,6272]{1,0:T(8,128)(2,1)S(1)} %collective-permute-done.6.refs_2_), channel_id=1, source_target_pairs={{0,1},{1,2},{2,3},{3,7},{7,6},{6,5},{5,4},{4,0},{8,9},{9,10},{10,1... | collective-permute-start | bytes 602120 | tf_op jit(solution)/shard_map/gather0_+1_hop3/ppermute | solution.py:155
  23.0 2.1 %collective-permute-start.12 = (bf16[16,6272]{1,0:T(8,128)(2,1)S(1)}, bf16[16,6272]{1,0:T(8,128)(2,1)S(1)}, u32[]{:S(2)}, u32[]{:S(2)}) collective-permute-start(bf16[16,6272]{1,0:T(8,128)(2,1)S(1)} %collective-permute-done.4.refs_0_), channel_id=1, source_target_pairs={{0,1},{1,2},{2,3},{3,7},{7,6},{6,5},{5,4},{4,0},{8,9},{9,10},{10,1... | collective-permute-start | bytes 602120 | tf_op jit(solution)/shard_map/gather1_+1_hop3/ppermute | solution.py:155
  25.2 2.7 %shard_map.75 = (f32[48,2048]{1,0:T(8,128)S(1)}, f32[48,2048]{1,0:T(8,128)S(1)}, f32[48,2048]{1,0:T(8,128)S(1)}, f32[48,2048]{1,0:T(8,128)S(1)}) custom-call(bf16[16,6272]{1,0:T(8,128)(2,1)S(1)} %collective-permute-done.4.refs_0_, bf16[16,6272]{1,0:T(8,128)(2,1)S(1)} %collective-permute-done.5.refs_1_, bf16[16,6272]{1,0:T(8,128)(2,1)S(1)} %collective-permute-done.6.refs_2_, ...), custom_call_target="tpu_custom_call" | custom-call | flops 2415919104 | bytes 14942208 | tf_op jit(solution)/shard_map/pallas_call | solution.py:224
  27.9 2.5 %collective-permute-done.9.refs_1_ = bf16[16,6272]{1,0:T(8,128)(2,1)S(1)} collective-permute-done((bf16[16,6272]{1,0:T(8,128)(2,1)S(1)}, bf16[16,6272]{1,0:T(8,128)(2,1)S(1)}, u32[]{:S(2)}, u32[]{:S(2)}) %collective-permute-start.9) | collective-permute-done | bytes 200736 | tf_op jit(solution)/shard_map/gather1_-1_hop3/ppermute | solution.py:155
  32.4 2.2 %shard_map.76 = (f32[48,2048]{1,0:T(8,128)S(1)}, f32[48,2048]{1,0:T(8,128)S(1)}) custom-call(bf16[16,6272]{1,0:T(8,128)(2,1)S(1)} %collective-permute-done.8.refs_0_, bf16[16,6272]{1,0:T(8,128)(2,1)S(1)} %collective-permute-done.9.refs_1_, bf16[1,2048,1024]{2,1,0:T(8,128)(2,1)S(1)} %copy-done, bf16[1,2048,1024]{2,1,0:T(8,128)(2,1)S(1)} %copy-done.1, ...), custom_call_target="tpu_custom_call" | custom-call | flops 1207959552 | bytes 13762560 | tf_op jit(solution)/shard_map/pallas_call | solution.py:224
  34.7 2.2 %shard_map.77 = (bf16[48,2048]{1,0:T(8,128)(2,1)S(1)}, bf16[48,2048]{1,0:T(8,128)(2,1)S(1)}) custom-call(bf16[16,6272]{1,0:T(8,128)(2,1)S(1)} %collective-permute-done.12.refs_0_, bf16[16,6272]{1,0:T(8,128)(2,1)S(1)} %collective-permute-done.13.refs_1_, bf16[1,2048,1024]{2,1,0:T(8,128)(2,1)S(1)} %copy-done, bf16[1,2048,1024]{2,1,0:T(8,128)(2,1)S(1)} %copy-done.1, ...), custom_call_target="tpu_custom_call" | custom-call | flops 1207959552 | bytes 13762560 | tf_op jit(solution)/shard_map/pallas_call | solution.py:224
  37.7 2.2 %shard_map.78 = (bf16[48,2048]{1,0:T(8,128)(2,1)S(1)}, bf16[48,2048]{1,0:T(8,128)(2,1)S(1)}) custom-call(bf16[16,6272]{1,0:T(8,128)(2,1)S(1)} %collective-permute-done.10.refs_0_, bf16[16,6272]{1,0:T(8,128)(2,1)S(1)} %collective-permute-done.11.refs_1_, bf16[1,2048,1024]{2,1,0:T(8,128)(2,1)S(1)} %copy-done, bf16[1,2048,1024]{2,1,0:T(8,128)(2,1)S(1)} %copy-done.1, ...), custom_call_target="tpu_custom_call" | custom-call | flops 1207959552 | bytes 13762560 | tf_op jit(solution)/shard_map/pallas_call | solution.py:224
  44.0 3.4 %collective-permute-done.19 = bf16[48,2048]{1,0:T(8,128)(2,1)S(1)} collective-permute-done((bf16[48,2048]{1,0:T(8,128)(2,1)S(1)}, bf16[48,2048]{1,0:T(8,128)(2,1)S(1)}, u32[]{:S(2)}, u32[]{:S(2)}) %collective-permute-start.19) | collective-permute-done | bytes 196640 | tf_op jit(solution)/shard_map/sum1_+1_left4/ppermute | solution.py:155
  47.5 1.7 %collective-permute-start.21 = (bf16[48,2048]{1,0:T(8,128)(2,1)S(1)}, bf16[48,2048]{1,0:T(8,128)(2,1)S(1)}, u32[]{:S(2)}, u32[]{:S(2)}) collective-permute-start(bf16[48,2048]{1,0:T(8,128)(2,1)S(1)} %add_convert_fusion.7), channel_id=1, source_target_pairs={{0,1},{1,2},{2,3},{3,7},{7,6},{6,5},{5,4},{4,0},{8,9},{9,10},{10,1... | collective-permute-start | bytes 589832 | tf_op jit(solution)/shard_map/sum1_+1_left3/ppermute | solution.py:155
  49.7 1.9 %collective-permute-done.18 = bf16[48,2048]{1,0:T(8,128)(2,1)S(1)} collective-permute-done((bf16[48,2048]{1,0:T(8,128)(2,1)S(1)}, bf16[48,2048]{1,0:T(8,128)(2,1)S(1)}, u32[]{:S(2)}, u32[]{:S(2)}) %collective-permute-start.18) | collective-permute-done | bytes 196640 | tf_op jit(solution)/shard_map/sum0_+1_left3/ppermute | solution.py:155
  51.7 1.7 %collective-permute-start.20 = (bf16[48,2048]{1,0:T(8,128)(2,1)S(1)}, bf16[48,2048]{1,0:T(8,128)(2,1)S(1)}, u32[]{:S(2)}, u32[]{:S(2)}) collective-permute-start(bf16[48,2048]{1,0:T(8,128)(2,1)S(1)} %add_convert_fusion.8), channel_id=1, source_target_pairs={{0,1},{1,2},{2,3},{3,7},{7,6},{6,5},{5,4},{4,0},{8,9},{9,10},{10,1... | collective-permute-start | bytes 589832 | tf_op jit(solution)/shard_map/sum0_+1_left2/ppermute | solution.py:155
  53.9 1.9 %collective-permute-done.21 = bf16[48,2048]{1,0:T(8,128)(2,1)S(1)} collective-permute-done((bf16[48,2048]{1,0:T(8,128)(2,1)S(1)}, bf16[48,2048]{1,0:T(8,128)(2,1)S(1)}, u32[]{:S(2)}, u32[]{:S(2)}) %collective-permute-start.21) | collective-permute-done | bytes 196640 | tf_op jit(solution)/shard_map/sum1_+1_left3/ppermute | solution.py:155
  55.9 1.7 %collective-permute-start.26 = (bf16[48,2048]{1,0:T(8,128)(2,1)S(1)}, bf16[48,2048]{1,0:T(8,128)(2,1)S(1)}, u32[]{:S(2)}, u32[]{:S(2)}) collective-permute-start(bf16[48,2048]{1,0:T(8,128)(2,1)S(1)} %add_convert_fusion.5), channel_id=1, source_target_pairs={{0,1},{1,2},{2,3},{3,7},{7,6},{6,5},{5,4},{4,0},{8,9},{9,10},{10,1... | collective-permute-start | bytes 589832 | tf_op jit(solution)/shard_map/sum1_+1_left2/ppermute | solution.py:155
  58.1 1.9 %collective-permute-done.20 = bf16[48,2048]{1,0:T(8,128)(2,1)S(1)} collective-permute-done((bf16[48,2048]{1,0:T(8,128)(2,1)S(1)}, bf16[48,2048]{1,0:T(8,128)(2,1)S(1)}, u32[]{:S(2)}, u32[]{:S(2)}) %collective-permute-start.20) | collective-permute-done | bytes 196640 | tf_op jit(solution)/shard_map/sum0_+1_left2/ppermute | solution.py:155
  62.3 1.9 %collective-permute-done.26 = bf16[48,2048]{1,0:T(8,128)(2,1)S(1)} collective-permute-done((bf16[48,2048]{1,0:T(8,128)(2,1)S(1)}, bf16[48,2048]{1,0:T(8,128)(2,1)S(1)}, u32[]{:S(2)}, u32[]{:S(2)}) %collective-permute-start.26) | collective-permute-done | bytes 196640 | tf_op jit(solution)/shard_map/sum1_+1_left2/ppermute | solution.py:155
  66.6 1.8 %collective-permute-done.25 = bf16[48,2048]{1,0:T(8,128)(2,1)S(1)} collective-permute-done((bf16[48,2048]{1,0:T(8,128)(2,1)S(1)}, bf16[48,2048]{1,0:T(8,128)(2,1)S(1)}, u32[]{:S(2)}, u32[]{:S(2)}) %collective-permute-start.25) | collective-permute-done | bytes 196640 | tf_op jit(solution)/shard_map/sum1_-1_left1/ppermute | solution.py:155
  70.1 1.8 %collective-permute-done.17 = bf16[48,2048]{1,0:T(8,128)(2,1)S(1)} collective-permute-done((bf16[48,2048]{1,0:T(8,128)(2,1)S(1)}, bf16[48,2048]{1,0:T(8,128)(2,1)S(1)}, u32[]{:S(2)}, u32[]{:S(2)}) %collective-permute-start.17) | collective-permute-done | bytes 196640 | tf_op jit(solution)/shard_map/sum0_-1_left1/ppermute | solution.py:155
  (57 shorter events, 17.6 us)
Async XLA Ops:
  1.3 8.8 %collective-permute-start.2 = (bf16[16,6272]{1,0:T(8,128)(2,1)S(1)}, bf16[16,6272]{1,0:T(8,128)(2,1)S(1)}, u32[]{:S(2)}, u32[]{:S(2)}) collective-permute-start(bf16[16,6272]{1,0:T(8,128)(2,1)S(1)} %get-tuple-element.42.refs_5_), channel_id=1, source_target_pairs={{0,1},{1,2},{2,3},{3,7},{7,6},{6,5},{5,4},{4,0},{8,9},{9,10},{10,1... | collective-permute-start | bytes 602120 | tf_op jit(solution)/shard_map/gather0_+1_hop1/ppermute | solution.py:155
  4.4 7.9 %collective-permute-start.3 = (bf16[16,6272]{1,0:T(8,128)(2,1)S(1)}, bf16[16,6272]{1,0:T(8,128)(2,1)S(1)}, u32[]{:S(2)}, u32[]{:S(2)}) collective-permute-start(bf16[16,6272]{1,0:T(8,128)(2,1)S(1)} %get-tuple-element.40.refs_4_), channel_id=1, source_target_pairs={{0,4},{1,0},{2,1},{3,2},{7,3},{6,7},{5,6},{4,5},{8,12},{9,8},{10,9... | collective-permute-start | bytes 602120 | tf_op jit(solution)/shard_map/gather1_-1_hop1/ppermute | solution.py:155
  4.4 10.1 %collective-permute-start = (bf16[16,6272]{1,0:T(8,128)(2,1)S(1)}, bf16[16,6272]{1,0:T(8,128)(2,1)S(1)}, u32[]{:S(2)}, u32[]{:S(2)}) collective-permute-start(bf16[16,6272]{1,0:T(8,128)(2,1)S(1)} %get-tuple-element.40.refs_4_), channel_id=1, source_target_pairs={{0,1},{1,2},{2,3},{3,7},{7,6},{6,5},{5,4},{4,0},{8,9},{9,10},{10,1... | collective-permute-start | bytes 602120 | tf_op jit(solution)/shard_map/gather1_+1_hop1/ppermute | solution.py:155
  6.4 10.2 %collective-permute-start.1 = (bf16[16,6272]{1,0:T(8,128)(2,1)S(1)}, bf16[16,6272]{1,0:T(8,128)(2,1)S(1)}, u32[]{:S(2)}, u32[]{:S(2)}) collective-permute-start(bf16[16,6272]{1,0:T(8,128)(2,1)S(1)} %get-tuple-element.42.refs_5_), channel_id=1, source_target_pairs={{0,4},{1,0},{2,1},{3,2},{7,3},{6,7},{5,6},{4,5},{8,12},{9,8},{10,9... | collective-permute-start | bytes 602120 | tf_op jit(solution)/shard_map/gather0_-1_hop1/ppermute | solution.py:155
  10.1 10.5 %collective-permute-start.6 = (bf16[16,6272]{1,0:T(8,128)(2,1)S(1)}, bf16[16,6272]{1,0:T(8,128)(2,1)S(1)}, u32[]{:S(2)}, u32[]{:S(2)}) collective-permute-start(bf16[16,6272]{1,0:T(8,128)(2,1)S(1)} %collective-permute-done.2.refs_2_), channel_id=1, source_target_pairs={{0,1},{1,2},{2,3},{3,7},{7,6},{6,5},{5,4},{4,0},{8,9},{9,10},{10,1... | collective-permute-start | bytes 602120 | tf_op jit(solution)/shard_map/gather0_+1_hop2/ppermute | solution.py:155
  12.3 10.4 %collective-permute-start.7 = (bf16[16,6272]{1,0:T(8,128)(2,1)S(1)}, bf16[16,6272]{1,0:T(8,128)(2,1)S(1)}, u32[]{:S(2)}, u32[]{:S(2)}) collective-permute-start(bf16[16,6272]{1,0:T(8,128)(2,1)S(1)} %collective-permute-done.3.refs_3_), channel_id=1, source_target_pairs={{0,4},{1,0},{2,1},{3,2},{7,3},{6,7},{5,6},{4,5},{8,12},{9,8},{10,9... | collective-permute-start | bytes 602120 | tf_op jit(solution)/shard_map/gather1_-1_hop2/ppermute | solution.py:155
  14.4 8.6 %collective-permute-start.4 = (bf16[16,6272]{1,0:T(8,128)(2,1)S(1)}, bf16[16,6272]{1,0:T(8,128)(2,1)S(1)}, u32[]{:S(2)}, u32[]{:S(2)}) collective-permute-start(bf16[16,6272]{1,0:T(8,128)(2,1)S(1)} %collective-permute-done.refs_0_), channel_id=1, source_target_pairs={{0,1},{1,2},{2,3},{3,7},{7,6},{6,5},{5,4},{4,0},{8,9},{9,10},{10,1... | collective-permute-start | bytes 602120 | tf_op jit(solution)/shard_map/gather1_+1_hop2/ppermute | solution.py:155
  16.6 8.6 %collective-permute-start.5 = (bf16[16,6272]{1,0:T(8,128)(2,1)S(1)}, bf16[16,6272]{1,0:T(8,128)(2,1)S(1)}, u32[]{:S(2)}, u32[]{:S(2)}) collective-permute-start(bf16[16,6272]{1,0:T(8,128)(2,1)S(1)} %collective-permute-done.1.refs_1_), channel_id=1, source_target_pairs={{0,4},{1,0},{2,1},{3,2},{7,3},{6,7},{5,6},{4,5},{8,12},{9,8},{10,9... | collective-permute-start | bytes 602120 | tf_op jit(solution)/shard_map/gather0_-1_hop2/ppermute | solution.py:155
  20.6 9.8 %collective-permute-start.8 = (bf16[16,6272]{1,0:T(8,128)(2,1)S(1)}, bf16[16,6272]{1,0:T(8,128)(2,1)S(1)}, u32[]{:S(2)}, u32[]{:S(2)}) collective-permute-start(bf16[16,6272]{1,0:T(8,128)(2,1)S(1)} %collective-permute-done.6.refs_2_), channel_id=1, source_target_pairs={{0,1},{1,2},{2,3},{3,7},{7,6},{6,5},{5,4},{4,0},{8,9},{9,10},{10,1... | collective-permute-start | bytes 602120 | tf_op jit(solution)/shard_map/gather0_+1_hop3/ppermute | solution.py:155
  22.7 7.7 %collective-permute-start.9 = (bf16[16,6272]{1,0:T(8,128)(2,1)S(1)}, bf16[16,6272]{1,0:T(8,128)(2,1)S(1)}, u32[]{:S(2)}, u32[]{:S(2)}) collective-permute-start(bf16[16,6272]{1,0:T(8,128)(2,1)S(1)} %collective-permute-done.7.refs_3_), channel_id=1, source_target_pairs={{0,4},{1,0},{2,1},{3,2},{7,3},{6,7},{5,6},{4,5},{8,12},{9,8},{10,9... | collective-permute-start | bytes 602120 | tf_op jit(solution)/shard_map/gather1_-1_hop3/ppermute | solution.py:155
  23.0 11.6 %collective-permute-start.12 = (bf16[16,6272]{1,0:T(8,128)(2,1)S(1)}, bf16[16,6272]{1,0:T(8,128)(2,1)S(1)}, u32[]{:S(2)}, u32[]{:S(2)}) collective-permute-start(bf16[16,6272]{1,0:T(8,128)(2,1)S(1)} %collective-permute-done.4.refs_0_), channel_id=1, source_target_pairs={{0,1},{1,2},{2,3},{3,7},{7,6},{6,5},{5,4},{4,0},{8,9},{9,10},{10,1... | collective-permute-start | bytes 602120 | tf_op jit(solution)/shard_map/gather1_+1_hop3/ppermute | solution.py:155
  25.2 9.5 %collective-permute-start.13 = (bf16[16,6272]{1,0:T(8,128)(2,1)S(1)}, bf16[16,6272]{1,0:T(8,128)(2,1)S(1)}, u32[]{:S(2)}, u32[]{:S(2)}) collective-permute-start(bf16[16,6272]{1,0:T(8,128)(2,1)S(1)} %collective-permute-done.5.refs_1_), channel_id=1, source_target_pairs={{0,4},{1,0},{2,1},{3,2},{7,3},{6,7},{5,6},{4,5},{8,12},{9,8},{10,9... | collective-permute-start | bytes 602120 | tf_op jit(solution)/shard_map/gather0_-1_hop3/ppermute | solution.py:155
  30.4 6.5 %collective-permute-start.10 = (bf16[16,6272]{1,0:T(8,128)(2,1)S(1)}, bf16[16,6272]{1,0:T(8,128)(2,1)S(1)}, u32[]{:S(2)}, u32[]{:S(2)}) collective-permute-start(bf16[16,6272]{1,0:T(8,128)(2,1)S(1)} %collective-permute-done.8.refs_0_), channel_id=1, source_target_pairs={{0,1},{1,2},{2,3},{3,7},{7,6},{6,5},{5,4},{4,0},{8,9},{9,10},{10,1... | collective-permute-start | bytes 602120 | tf_op jit(solution)/shard_map/gather0_+1_hop4/ppermute | solution.py:155
  39.9 7.5 %collective-permute-start.19 = (bf16[48,2048]{1,0:T(8,128)(2,1)S(1)}, bf16[48,2048]{1,0:T(8,128)(2,1)S(1)}, u32[]{:S(2)}, u32[]{:S(2)}) collective-permute-start(bf16[48,2048]{1,0:T(8,128)(2,1)S(1)} %get-tuple-element.62), channel_id=1, source_target_pairs={{0,1},{1,2},{2,3},{3,7},{7,6},{6,5},{5,4},{4,0},{8,9},{9,10},{10,1... | collective-permute-start | bytes 589832 | tf_op jit(solution)/shard_map/sum1_+1_left4/ppermute | solution.py:155
  41.6 7.7 %collective-permute-start.14 = (bf16[48,2048]{1,0:T(8,128)(2,1)S(1)}, bf16[48,2048]{1,0:T(8,128)(2,1)S(1)}, u32[]{:S(2)}, u32[]{:S(2)}) collective-permute-start(bf16[48,2048]{1,0:T(8,128)(2,1)S(1)} %get-tuple-element.58), channel_id=1, source_target_pairs={{0,4},{1,0},{2,1},{3,2},{7,3},{6,7},{5,6},{4,5},{8,12},{9,8},{10,9... | collective-permute-start | bytes 589832 | tf_op jit(solution)/shard_map/sum0_-1_left4/ppermute | solution.py:155
  42.0 9.6 %collective-permute-start.18 = (bf16[48,2048]{1,0:T(8,128)(2,1)S(1)}, bf16[48,2048]{1,0:T(8,128)(2,1)S(1)}, u32[]{:S(2)}, u32[]{:S(2)}) collective-permute-start(bf16[48,2048]{1,0:T(8,128)(2,1)S(1)} %get-tuple-element.63), channel_id=1, source_target_pairs={{0,1},{1,2},{2,3},{3,7},{7,6},{6,5},{5,4},{4,0},{8,9},{9,10},{10,1... | collective-permute-start | bytes 589832 | tf_op jit(solution)/shard_map/sum0_+1_left3/ppermute | solution.py:155
  43.6 9.9 %collective-permute-start.23 = (bf16[48,2048]{1,0:T(8,128)(2,1)S(1)}, bf16[48,2048]{1,0:T(8,128)(2,1)S(1)}, u32[]{:S(2)}, u32[]{:S(2)}) collective-permute-start(bf16[48,2048]{1,0:T(8,128)(2,1)S(1)} %get-tuple-element.69.refs_5_), channel_id=1, source_target_pairs={{0,4},{1,0},{2,1},{3,2},{7,3},{6,7},{5,6},{4,5},{8,12},{9,8},{10,9... | collective-permute-start | bytes 589832 | tf_op jit(solution)/shard_map/sum1_-1_left3/ppermute | solution.py:155
  47.5 8.4 %collective-permute-start.21 = (bf16[48,2048]{1,0:T(8,128)(2,1)S(1)}, bf16[48,2048]{1,0:T(8,128)(2,1)S(1)}, u32[]{:S(2)}, u32[]{:S(2)}) collective-permute-start(bf16[48,2048]{1,0:T(8,128)(2,1)S(1)} %add_convert_fusion.7), channel_id=1, source_target_pairs={{0,1},{1,2},{2,3},{3,7},{7,6},{6,5},{5,4},{4,0},{8,9},{9,10},{10,1... | collective-permute-start | bytes 589832 | tf_op jit(solution)/shard_map/sum1_+1_left3/ppermute | solution.py:155
  49.3 8.4 %collective-permute-start.15 = (bf16[48,2048]{1,0:T(8,128)(2,1)S(1)}, bf16[48,2048]{1,0:T(8,128)(2,1)S(1)}, u32[]{:S(2)}, u32[]{:S(2)}) collective-permute-start(bf16[48,2048]{1,0:T(8,128)(2,1)S(1)} %add_convert_fusion.11), channel_id=1, source_target_pairs={{0,4},{1,0},{2,1},{3,2},{7,3},{6,7},{5,6},{4,5},{8,12},{9,8},{10,9... | collective-permute-start | bytes 589832 | tf_op jit(solution)/shard_map/sum0_-1_left3/ppermute | solution.py:155
  51.7 8.4 %collective-permute-start.20 = (bf16[48,2048]{1,0:T(8,128)(2,1)S(1)}, bf16[48,2048]{1,0:T(8,128)(2,1)S(1)}, u32[]{:S(2)}, u32[]{:S(2)}) collective-permute-start(bf16[48,2048]{1,0:T(8,128)(2,1)S(1)} %add_convert_fusion.8), channel_id=1, source_target_pairs={{0,1},{1,2},{2,3},{3,7},{7,6},{6,5},{5,4},{4,0},{8,9},{9,10},{10,1... | collective-permute-start | bytes 589832 | tf_op jit(solution)/shard_map/sum0_+1_left2/ppermute | solution.py:155
  53.5 8.4 %collective-permute-start.24 = (bf16[48,2048]{1,0:T(8,128)(2,1)S(1)}, bf16[48,2048]{1,0:T(8,128)(2,1)S(1)}, u32[]{:S(2)}, u32[]{:S(2)}) collective-permute-start(bf16[48,2048]{1,0:T(8,128)(2,1)S(1)} %add_convert_fusion.3), channel_id=1, source_target_pairs={{0,4},{1,0},{2,1},{3,2},{7,3},{6,7},{5,6},{4,5},{8,12},{9,8},{10,9... | collective-permute-start | bytes 589832 | tf_op jit(solution)/shard_map/sum1_-1_left2/ppermute | solution.py:155
  55.9 8.4 %collective-permute-start.26 = (bf16[48,2048]{1,0:T(8,128)(2,1)S(1)}, bf16[48,2048]{1,0:T(8,128)(2,1)S(1)}, u32[]{:S(2)}, u32[]{:S(2)}) collective-permute-start(bf16[48,2048]{1,0:T(8,128)(2,1)S(1)} %add_convert_fusion.5), channel_id=1, source_target_pairs={{0,1},{1,2},{2,3},{3,7},{7,6},{6,5},{5,4},{4,0},{8,9},{9,10},{10,1... | collective-permute-start | bytes 589832 | tf_op jit(solution)/shard_map/sum1_+1_left2/ppermute | solution.py:155
  57.8 8.4 %collective-permute-start.16 = (bf16[48,2048]{1,0:T(8,128)(2,1)S(1)}, bf16[48,2048]{1,0:T(8,128)(2,1)S(1)}, u32[]{:S(2)}, u32[]{:S(2)}) collective-permute-start(bf16[48,2048]{1,0:T(8,128)(2,1)S(1)} %add_convert_fusion.10), channel_id=1, source_target_pairs={{0,4},{1,0},{2,1},{3,2},{7,3},{6,7},{5,6},{4,5},{8,12},{9,8},{10,9... | collective-permute-start | bytes 589832 | tf_op jit(solution)/shard_map/sum0_-1_left2/ppermute | solution.py:155
  60.1 10.0 %collective-permute-start.22 = (bf16[48,2048]{1,0:T(8,128)(2,1)S(1)}, bf16[48,2048]{1,0:T(8,128)(2,1)S(1)}, u32[]{:S(2)}, u32[]{:S(2)}) collective-permute-start(bf16[48,2048]{1,0:T(8,128)(2,1)S(1)} %add_convert_fusion.6), channel_id=1, source_target_pairs={{0,1},{1,2},{2,3},{3,7},{7,6},{6,5},{5,4},{4,0},{8,9},{9,10},{10,1... | collective-permute-start | bytes 589832 | tf_op jit(solution)/shard_map/sum0_+1_left1/ppermute | solution.py:155
  (7 other events, 73.3 us)

commit v3 on v1

--- a/solution.py
+++ b/solution.py
@@ -138,7 +138,7 @@
         ],
         compiler_params=pltpu.CompilerParams(vmem_limit_bytes=4 * 1024 * 1024),
         cost_estimate=pl.CostEstimate(
-            flops=10000000000, bytes_accessed=0, transcendentals=0
+            flops=10_000_000_000, bytes_accessed=0, transcendentals=0
         ),
     )(*outside)
 
@@ -153,20 +153,6 @@
     count = len(ring)
     pairs = [(ring[index], ring[(index + stride) % count]) for index in range(count)]
     return lax.ppermute(block, ("ex", "ey"), pairs)
-
-
-def mark_kernel(marker_ref):
-    marker_ref[...] = jnp.zeros_like(marker_ref)
-
-
-def mark():
-    return pl.pallas_call(
-        mark_kernel,
-        out_specs=pl.BlockSpec(memory_space=pltpu.VMEM),
-        out_shape=pltpu.VMEM((8, 128), jnp.float32),
-        compiler_params=pltpu.CompilerParams(vmem_limit_bytes=1024 * 1024),
-        cost_estimate=pl.CostEstimate(flops=0, bytes_accessed=25000000, transcendentals=0),
-    )()
 
 
 def expert_kernel(count, *refs):
@@ -264,7 +250,6 @@
             block = gathered[index][-(hop - 1) * stride]
             with jax.named_scope(f"gather{index}_{stride:+d}_hop{hop}"):
                 gathered[index][-hop * stride] = pass_on(after(block, others), stride)
-            others = others
 
     def sum_hop(some, left, others):
         sent = []
@@ -278,7 +263,6 @@
             with jax.named_scope(f"sum{index}_{-stride:+d}_left{left}"):
                 carried[index, stride] = pass_on(partial, -stride)
             sent.append(partial)
-            others = others
         return sent
 
     def expert(some, hops, earlier):
@@ -297,24 +281,23 @@
         return [answers[0]]
 
     weights = [gate_weight, up_weight, down_weight]
-    marker = mark()
     done = []
     for hop in range(1, short_reach + 1):
-        gather_hop(long_chains, hop, [marker])
-        gather_hop(short_chains[::-1], hop, [])
+        gather_hop(chains, hop, [])
+        if hop == 1:
+            done = expert(chains, [0], [])
         if hop == short_reach - 1:
-            done = expert(chains, range(short_reach - 2, -1, -1), [])
+            done = expert(chains, range(short_reach - 2, 0, -1), done)
     done = expert(chains, [short_reach - 1], done)
     gather_hop(long_chains, long_reach, done)
-    done = expert(long_chains, [short_reach], done)
-    done = expert(short_chains[::-1], [short_reach], done)
+    done = expert(chains, [short_reach], done)
     last = [gathered[index][-long_reach * stride] for index, stride in long_chains]
     done = expert(long_chains, [long_reach], done)
     for left in range(long_reach, 0, -1):
         sent = sum_hop(long_chains, left, [])
         if left > 1:
-            sent = sum_hop(short_chains[:1], left - 1, last + sent)
-            sum_hop(short_chains[1:], left - 1, last + sent)
+            sent = sum_hop(short_chains[1:], left - 1, last + sent)
+            sum_hop(short_chains[:1], left - 1, last + sent)
 
     results = []
     for index in range(micro):

time: 71.9 us -> 70.9 us (0.986)
  transfers between devices with their start and end apart: 28 -> 28, of which waited for: 12 -> 14; matrix products, arithmetic and copies ran while one was open for 1% -> 1% of each run, Pallas kernels for 15% -> 15%
where the time goes in v3:
time: 70.9 us; the launch traced here: 70.8 us
  starting transfers between devices  30.6 us (43%)
  waiting for transfers between devices  24.7 us (35%)
  Pallas kernels  14 us (20%)
  other arithmetic  1.33 us (2%)
    ppermute x28, starting transfers between devices, pass_on(): return lax.ppermute(block, ('ex', 'ey'), pairs)  30.6 us
    ppermute x28, waiting for transfers between devices, pass_on(): return lax.ppermute(block, ('ex', 'ey'), pairs)  24.7 us
    pallas_call x5, Pallas kernels, run_expert(): pl.pallas_call(functools.partial(expert_kernel, count), in_specs=[in_vmem...  12.7 us
  transfers between devices with their start and end apart: 28, of which 14 were waited for; matrix products, arithmetic and copies ran while one was open for 1% of the time, Pallas kernels for 15%

profile of v3, /device:TPU:0, one launch (start us, length us, event | category | flops | bytes accessed | tf_op | source)
XLA Modules:
  0.0 70.8 jit_solution(1227997878315883139)
XLA Ops:
  1.3 3.1 %collective-permute-start = (bf16[16,6272]{1,0:T(8,128)(2,1)S(1)}, bf16[16,6272]{1,0:T(8,128)(2,1)S(1)}, u32[]{:S(2)}, u32[]{:S(2)}) collective-permute-start(bf16[16,6272]{1,0:T(8,128)(2,1)S(1)} %get-tuple-element.31.refs_0_), channel_id=1, source_target_pairs={{0,1},{1,2},{2,3},{3,7},{7,6},{6,5},{5,4},{4,0},{8,9},{9,10},{10,1... | collective-permute-start | bytes 602120 | tf_op jit(solution)/shard_map/gather0_+1_hop1/ppermute | solution.py:155
  4.4 2.0 %collective-permute-start.2 = (bf16[16,6272]{1,0:T(8,128)(2,1)S(1)}, bf16[16,6272]{1,0:T(8,128)(2,1)S(1)}, u32[]{:S(2)}, u32[]{:S(2)}) collective-permute-start(bf16[16,6272]{1,0:T(8,128)(2,1)S(1)} %get-tuple-element.32.refs_1_), channel_id=1, source_target_pairs={{0,1},{1,2},{2,3},{3,7},{7,6},{6,5},{5,4},{4,0},{8,9},{9,10},{10,1... | collective-permute-start | bytes 602120 | tf_op jit(solution)/shard_map/gather1_+1_hop1/ppermute | solution.py:155
  6.4 2.2 %shard_map.74 = (f32[48,2048]{1,0:T(8,128)S(1)}, f32[48,2048]{1,0:T(8,128)S(1)}) custom-call(bf16[16,6272]{1,0:T(8,128)(2,1)S(1)} %get-tuple-element.31.refs_0_, bf16[16,6272]{1,0:T(8,128)(2,1)S(1)} %get-tuple-element.32.refs_1_, bf16[1,2048,1024]{2,1,0:T(8,128)(2,1)S(1)} %copy-done, bf16[1,2048,1024]{2,1,0:T(8,128)(2,1)S(1)} %copy-done.1, ...), custom_call_target="tpu_custom_call" | custom-call | flops 1207959552 | bytes 13762560 | tf_op jit(solution)/shard_map/pallas_call | solution.py:210
  10.1 2.1 %collective-permute-start.4 = (bf16[16,6272]{1,0:T(8,128)(2,1)S(1)}, bf16[16,6272]{1,0:T(8,128)(2,1)S(1)}, u32[]{:S(2)}, u32[]{:S(2)}) collective-permute-start(bf16[16,6272]{1,0:T(8,128)(2,1)S(1)} %collective-permute-done.refs_0_), channel_id=1, source_target_pairs={{0,1},{1,2},{2,3},{3,7},{7,6},{6,5},{5,4},{4,0},{8,9},{9,10},{10,1... | collective-permute-start | bytes 602120 | tf_op jit(solution)/shard_map/gather0_+1_hop2/ppermute | solution.py:155
  12.3 2.1 %collective-permute-done.2.refs_2_ = bf16[16,6272]{1,0:T(8,128)(2,1)S(1)} collective-permute-done((bf16[16,6272]{1,0:T(8,128)(2,1)S(1)}, bf16[16,6272]{1,0:T(8,128)(2,1)S(1)}, u32[]{:S(2)}, u32[]{:S(2)}) %collective-permute-start.2) | collective-permute-done | bytes 200736 | tf_op jit(solution)/shard_map/gather1_+1_hop1/ppermute | solution.py:155
  14.4 2.1 %collective-permute-start.6 = (bf16[16,6272]{1,0:T(8,128)(2,1)S(1)}, bf16[16,6272]{1,0:T(8,128)(2,1)S(1)}, u32[]{:S(2)}, u32[]{:S(2)}) collective-permute-start(bf16[16,6272]{1,0:T(8,128)(2,1)S(1)} %collective-permute-done.2.refs_2_), channel_id=1, source_target_pairs={{0,1},{1,2},{2,3},{3,7},{7,6},{6,5},{5,4},{4,0},{8,9},{9,10},{10,1... | collective-permute-start | bytes 602120 | tf_op jit(solution)/shard_map/gather1_+1_hop2/ppermute | solution.py:155
  16.6 2.8 %shard_map.75 = (f32[48,2048]{1,0:T(8,128)S(1)}, f32[48,2048]{1,0:T(8,128)S(1)}, f32[48,2048]{1,0:T(8,128)S(1)}, f32[48,2048]{1,0:T(8,128)S(1)}) custom-call(bf16[16,6272]{1,0:T(8,128)(2,1)S(1)} %collective-permute-done.refs_0_, bf16[16,6272]{1,0:T(8,128)(2,1)S(1)} %collective-permute-done.1.refs_1_, bf16[16,6272]{1,0:T(8,128)(2,1)S(1)} %collective-permute-done.2.refs_2_, ...), custom_call_target="tpu_custom_call" | custom-call | flops 2415919104 | bytes 14942208 | tf_op jit(solution)/shard_map/pallas_call | solution.py:210
  19.4 2.1 %collective-permute-start.8 = (bf16[16,6272]{1,0:T(8,128)(2,1)S(1)}, bf16[16,6272]{1,0:T(8,128)(2,1)S(1)}, u32[]{:S(2)}, u32[]{:S(2)}) collective-permute-start(bf16[16,6272]{1,0:T(8,128)(2,1)S(1)} %collective-permute-done.4.refs_0_), channel_id=1, source_target_pairs={{0,1},{1,2},{2,3},{3,7},{7,6},{6,5},{5,4},{4,0},{8,9},{9,10},{10,1... | collective-permute-start | bytes 602120 | tf_op jit(solution)/shard_map/gather0_+1_hop3/ppermute | solution.py:155
  23.0 2.1 %collective-permute-start.10 = (bf16[16,6272]{1,0:T(8,128)(2,1)S(1)}, bf16[16,6272]{1,0:T(8,128)(2,1)S(1)}, u32[]{:S(2)}, u32[]{:S(2)}) collective-permute-start(bf16[16,6272]{1,0:T(8,128)(2,1)S(1)} %collective-permute-done.6.refs_2_), channel_id=1, source_target_pairs={{0,1},{1,2},{2,3},{3,7},{7,6},{6,5},{5,4},{4,0},{8,9},{9,10},{10,1... | collective-permute-start | bytes 602120 | tf_op jit(solution)/shard_map/gather1_+1_hop3/ppermute | solution.py:155
  25.2 2.7 %shard_map.76 = (f32[48,2048]{1,0:T(8,128)S(1)}, f32[48,2048]{1,0:T(8,128)S(1)}, f32[48,2048]{1,0:T(8,128)S(1)}, f32[48,2048]{1,0:T(8,128)S(1)}) custom-call(bf16[16,6272]{1,0:T(8,128)(2,1)S(1)} %collective-permute-done.4.refs_0_, bf16[16,6272]{1,0:T(8,128)(2,1)S(1)} %collective-permute-done.5.refs_1_, bf16[16,6272]{1,0:T(8,128)(2,1)S(1)} %collective-permute-done.6.refs_2_, ...), custom_call_target="tpu_custom_call" | custom-call | flops 2415919104 | bytes 14942208 | tf_op jit(solution)/shard_map/pallas_call | solution.py:210
  28.0 2.1 %collective-permute-start.12 = (bf16[16,6272]{1,0:T(8,128)(2,1)S(1)}, bf16[16,6272]{1,0:T(8,128)(2,1)S(1)}, u32[]{:S(2)}, u32[]{:S(2)}) collective-permute-start(bf16[16,6272]{1,0:T(8,128)(2,1)S(1)} %collective-permute-done.8.refs_0_), channel_id=1, source_target_pairs={{0,1},{1,2},{2,3},{3,7},{7,6},{6,5},{5,4},{4,0},{8,9},{9,10},{10,1... | collective-permute-start | bytes 602120 | tf_op jit(solution)/shard_map/gather0_+1_hop4/ppermute | solution.py:155
  31.6 2.2 %collective-permute-done.11.refs_3_ = bf16[16,6272]{1,0:T(8,128)(2,1)S(1)} collective-permute-done((bf16[16,6272]{1,0:T(8,128)(2,1)S(1)}, bf16[16,6272]{1,0:T(8,128)(2,1)S(1)}, u32[]{:S(2)}, u32[]{:S(2)}) %collective-permute-start.11) | collective-permute-done | bytes 200736 | tf_op jit(solution)/shard_map/gather0_-1_hop3/ppermute | solution.py:155
  33.8 2.7 %shard_map.77 = (f32[48,2048]{1,0:T(8,128)S(1)}, f32[48,2048]{1,0:T(8,128)S(1)}, bf16[48,2048]{1,0:T(8,128)(2,1)S(1)}, bf16[48,2048]{1,0:T(8,128)(2,1)S(1)}) custom-call(bf16[16,6272]{1,0:T(8,128)(2,1)S(1)} %collective-permute-done.8.refs_0_, bf16[16,6272]{1,0:T(8,128)(2,1)S(1)} %collective-permute-done.9.refs_1_, ...), custom_call_target="tpu_custom_call" | custom-call | flops 2415919104 | bytes 14942208 | tf_op jit(solution)/shard_map/pallas_call | solution.py:210
  36.6 2.2 %shard_map.78 = (bf16[48,2048]{1,0:T(8,128)(2,1)S(1)}, bf16[48,2048]{1,0:T(8,128)(2,1)S(1)}) custom-call(bf16[16,6272]{1,0:T(8,128)(2,1)S(1)} %collective-permute-done.12.refs_0_, bf16[16,6272]{1,0:T(8,128)(2,1)S(1)} %collective-permute-done.13.refs_1_, bf16[1,2048,1024]{2,1,0:T(8,128)(2,1)S(1)} %copy-done, bf16[1,2048,1024]{2,1,0:T(8,128)(2,1)S(1)} %copy-done.1, ...), custom_call_target="tpu_custom_call" | custom-call | flops 1207959552 | bytes 13762560 | tf_op jit(solution)/shard_map/pallas_call | solution.py:210
  43.0 3.8 %collective-permute-done.14 = bf16[48,2048]{1,0:T(8,128)(2,1)S(1)} collective-permute-done((bf16[48,2048]{1,0:T(8,128)(2,1)S(1)}, bf16[48,2048]{1,0:T(8,128)(2,1)S(1)}, u32[]{:S(2)}, u32[]{:S(2)}) %collective-permute-start.14) | collective-permute-done | bytes 196640 | tf_op jit(solution)/shard_map/sum0_-1_left4/ppermute | solution.py:155
  47.2 1.8 %collective-permute-start.23 = (bf16[48,2048]{1,0:T(8,128)(2,1)S(1)}, bf16[48,2048]{1,0:T(8,128)(2,1)S(1)}, u32[]{:S(2)}, u32[]{:S(2)}) collective-permute-start(bf16[48,2048]{1,0:T(8,128)(2,1)S(1)} %add_convert_fusion.6), channel_id=1, source_target_pairs={{0,1},{1,2},{2,3},{3,7},{7,6},{6,5},{5,4},{4,0},{8,9},{9,10},{10,1... | collective-permute-start | bytes 589832 | tf_op jit(solution)/shard_map/sum1_+1_left3/ppermute | solution.py:155
  49.0 2.0 %collective-permute-done.19 = bf16[48,2048]{1,0:T(8,128)(2,1)S(1)} collective-permute-done((bf16[48,2048]{1,0:T(8,128)(2,1)S(1)}, bf16[48,2048]{1,0:T(8,128)(2,1)S(1)}, u32[]{:S(2)}, u32[]{:S(2)}) %collective-permute-start.19) | collective-permute-done | bytes 196640 | tf_op jit(solution)/shard_map/sum1_-1_left3/ppermute | solution.py:155
  51.4 1.8 %collective-permute-start.21 = (bf16[48,2048]{1,0:T(8,128)(2,1)S(1)}, bf16[48,2048]{1,0:T(8,128)(2,1)S(1)}, u32[]{:S(2)}, u32[]{:S(2)}) collective-permute-start(bf16[48,2048]{1,0:T(8,128)(2,1)S(1)} %add_convert_fusion.8), channel_id=1, source_target_pairs={{0,1},{1,2},{2,3},{3,7},{7,6},{6,5},{5,4},{4,0},{8,9},{9,10},{10,1... | collective-permute-start | bytes 589832 | tf_op jit(solution)/shard_map/sum0_+1_left2/ppermute | solution.py:155
  53.2 2.0 %collective-permute-done.15 = bf16[48,2048]{1,0:T(8,128)(2,1)S(1)} collective-permute-done((bf16[48,2048]{1,0:T(8,128)(2,1)S(1)}, bf16[48,2048]{1,0:T(8,128)(2,1)S(1)}, u32[]{:S(2)}, u32[]{:S(2)}) %collective-permute-start.15) | collective-permute-done | bytes 196640 | tf_op jit(solution)/shard_map/sum0_-1_left3/ppermute | solution.py:155
  57.4 2.0 %collective-permute-done.22 = bf16[48,2048]{1,0:T(8,128)(2,1)S(1)} collective-permute-done((bf16[48,2048]{1,0:T(8,128)(2,1)S(1)}, bf16[48,2048]{1,0:T(8,128)(2,1)S(1)}, u32[]{:S(2)}, u32[]{:S(2)}) %collective-permute-start.22) | collective-permute-done | bytes 196640 | tf_op jit(solution)/shard_map/sum1_-1_left2/ppermute | solution.py:155
  61.6 2.0 %collective-permute-done.16 = bf16[48,2048]{1,0:T(8,128)(2,1)S(1)} collective-permute-done((bf16[48,2048]{1,0:T(8,128)(2,1)S(1)}, bf16[48,2048]{1,0:T(8,128)(2,1)S(1)}, u32[]{:S(2)}, u32[]{:S(2)}) %collective-permute-start.16) | collective-permute-done | bytes 196640 | tf_op jit(solution)/shard_map/sum0_-1_left2/ppermute | solution.py:155
  64.1 1.8 %collective-permute-start.27 = (bf16[48,2048]{1,0:T(8,128)(2,1)S(1)}, bf16[48,2048]{1,0:T(8,128)(2,1)S(1)}, u32[]{:S(2)}, u32[]{:S(2)}) collective-permute-start(bf16[48,2048]{1,0:T(8,128)(2,1)S(1)} %add_convert_fusion.1), channel_id=1, source_target_pairs={{0,1},{1,2},{2,3},{3,7},{7,6},{6,5},{5,4},{4,0},{8,9},{9,10},{10,1... | collective-permute-start | bytes 589832 | tf_op jit(solution)/shard_map/sum1_+1_left1/ppermute | solution.py:155
  65.8 2.0 %collective-permute-done.24 = bf16[48,2048]{1,0:T(8,128)(2,1)S(1)} collective-permute-done((bf16[48,2048]{1,0:T(8,128)(2,1)S(1)}, bf16[48,2048]{1,0:T(8,128)(2,1)S(1)}, u32[]{:S(2)}, u32[]{:S(2)}) %collective-permute-start.24) | collective-permute-done | bytes 196640 | tf_op jit(solution)/shard_map/sum0_+1_left1/ppermute | solution.py:155
  67.8 1.8 %collective-permute-done.17 = bf16[48,2048]{1,0:T(8,128)(2,1)S(1)} collective-permute-done((bf16[48,2048]{1,0:T(8,128)(2,1)S(1)}, bf16[48,2048]{1,0:T(8,128)(2,1)S(1)}, u32[]{:S(2)}, u32[]{:S(2)}) %collective-permute-start.17) | collective-permute-done | bytes 196640 | tf_op jit(solution)/shard_map/sum0_-1_left1/ppermute | solution.py:155
  (57 shorter events, 17.2 us)
Async XLA Ops:
  1.3 8.8 %collective-permute-start = (bf16[16,6272]{1,0:T(8,128)(2,1)S(1)}, bf16[16,6272]{1,0:T(8,128)(2,1)S(1)}, u32[]{:S(2)}, u32[]{:S(2)}) collective-permute-start(bf16[16,6272]{1,0:T(8,128)(2,1)S(1)} %get-tuple-element.31.refs_0_), channel_id=1, source_target_pairs={{0,1},{1,2},{2,3},{3,7},{7,6},{6,5},{5,4},{4,0},{8,9},{9,10},{10,1... | collective-permute-start | bytes 602120 | tf_op jit(solution)/shard_map/gather0_+1_hop1/ppermute | solution.py:155
  4.4 7.9 %collective-permute-start.1 = (bf16[16,6272]{1,0:T(8,128)(2,1)S(1)}, bf16[16,6272]{1,0:T(8,128)(2,1)S(1)}, u32[]{:S(2)}, u32[]{:S(2)}) collective-permute-start(bf16[16,6272]{1,0:T(8,128)(2,1)S(1)} %get-tuple-element.32.refs_1_), channel_id=1, source_target_pairs={{0,4},{1,0},{2,1},{3,2},{7,3},{6,7},{5,6},{4,5},{8,12},{9,8},{10,9... | collective-permute-start | bytes 602120 | tf_op jit(solution)/shard_map/gather1_-1_hop1/ppermute | solution.py:155
  4.4 10.1 %collective-permute-start.2 = (bf16[16,6272]{1,0:T(8,128)(2,1)S(1)}, bf16[16,6272]{1,0:T(8,128)(2,1)S(1)}, u32[]{:S(2)}, u32[]{:S(2)}) collective-permute-start(bf16[16,6272]{1,0:T(8,128)(2,1)S(1)} %get-tuple-element.32.refs_1_), channel_id=1, source_target_pairs={{0,1},{1,2},{2,3},{3,7},{7,6},{6,5},{5,4},{4,0},{8,9},{9,10},{10,1... | collective-permute-start | bytes 602120 | tf_op jit(solution)/shard_map/gather1_+1_hop1/ppermute | solution.py:155
  6.4 10.2 %collective-permute-start.3 = (bf16[16,6272]{1,0:T(8,128)(2,1)S(1)}, bf16[16,6272]{1,0:T(8,128)(2,1)S(1)}, u32[]{:S(2)}, u32[]{:S(2)}) collective-permute-start(bf16[16,6272]{1,0:T(8,128)(2,1)S(1)} %get-tuple-element.31.refs_0_), channel_id=1, source_target_pairs={{0,4},{1,0},{2,1},{3,2},{7,3},{6,7},{5,6},{4,5},{8,12},{9,8},{10,9... | collective-permute-start | bytes 602120 | tf_op jit(solution)/shard_map/gather0_-1_hop1/ppermute | solution.py:155
  10.1 9.2 %collective-permute-start.4 = (bf16[16,6272]{1,0:T(8,128)(2,1)S(1)}, bf16[16,6272]{1,0:T(8,128)(2,1)S(1)}, u32[]{:S(2)}, u32[]{:S(2)}) collective-permute-start(bf16[16,6272]{1,0:T(8,128)(2,1)S(1)} %collective-permute-done.refs_0_), channel_id=1, source_target_pairs={{0,1},{1,2},{2,3},{3,7},{7,6},{6,5},{5,4},{4,0},{8,9},{9,10},{10,1... | collective-permute-start | bytes 602120 | tf_op jit(solution)/shard_map/gather0_+1_hop2/ppermute | solution.py:155
  12.3 9.2 %collective-permute-start.5 = (bf16[16,6272]{1,0:T(8,128)(2,1)S(1)}, bf16[16,6272]{1,0:T(8,128)(2,1)S(1)}, u32[]{:S(2)}, u32[]{:S(2)}) collective-permute-start(bf16[16,6272]{1,0:T(8,128)(2,1)S(1)} %collective-permute-done.1.refs_1_), channel_id=1, source_target_pairs={{0,4},{1,0},{2,1},{3,2},{7,3},{6,7},{5,6},{4,5},{8,12},{9,8},{10,9... | collective-permute-start | bytes 602120 | tf_op jit(solution)/shard_map/gather1_-1_hop2/ppermute | solution.py:155
  14.4 8.6 %collective-permute-start.6 = (bf16[16,6272]{1,0:T(8,128)(2,1)S(1)}, bf16[16,6272]{1,0:T(8,128)(2,1)S(1)}, u32[]{:S(2)}, u32[]{:S(2)}) collective-permute-start(bf16[16,6272]{1,0:T(8,128)(2,1)S(1)} %collective-permute-done.2.refs_2_), channel_id=1, source_target_pairs={{0,1},{1,2},{2,3},{3,7},{7,6},{6,5},{5,4},{4,0},{8,9},{9,10},{10,1... | collective-permute-start | bytes 602120 | tf_op jit(solution)/shard_map/gather1_+1_hop2/ppermute | solution.py:155
  16.6 8.6 %collective-permute-start.7 = (bf16[16,6272]{1,0:T(8,128)(2,1)S(1)}, bf16[16,6272]{1,0:T(8,128)(2,1)S(1)}, u32[]{:S(2)}, u32[]{:S(2)}) collective-permute-start(bf16[16,6272]{1,0:T(8,128)(2,1)S(1)} %collective-permute-done.3.refs_3_), channel_id=1, source_target_pairs={{0,4},{1,0},{2,1},{3,2},{7,3},{6,7},{5,6},{4,5},{8,12},{9,8},{10,9... | collective-permute-start | bytes 602120 | tf_op jit(solution)/shard_map/gather0_-1_hop2/ppermute | solution.py:155
  19.4 8.6 %collective-permute-start.8 = (bf16[16,6272]{1,0:T(8,128)(2,1)S(1)}, bf16[16,6272]{1,0:T(8,128)(2,1)S(1)}, u32[]{:S(2)}, u32[]{:S(2)}) collective-permute-start(bf16[16,6272]{1,0:T(8,128)(2,1)S(1)} %collective-permute-done.4.refs_0_), channel_id=1, source_target_pairs={{0,1},{1,2},{2,3},{3,7},{7,6},{6,5},{5,4},{4,0},{8,9},{9,10},{10,1... | collective-permute-start | bytes 602120 | tf_op jit(solution)/shard_map/gather0_+1_hop3/ppermute | solution.py:155
  21.5 8.6 %collective-permute-start.9 = (bf16[16,6272]{1,0:T(8,128)(2,1)S(1)}, bf16[16,6272]{1,0:T(8,128)(2,1)S(1)}, u32[]{:S(2)}, u32[]{:S(2)}) collective-permute-start(bf16[16,6272]{1,0:T(8,128)(2,1)S(1)} %collective-permute-done.5.refs_1_), channel_id=1, source_target_pairs={{0,4},{1,0},{2,1},{3,2},{7,3},{6,7},{5,6},{4,5},{8,12},{9,8},{10,9... | collective-permute-start | bytes 602120 | tf_op jit(solution)/shard_map/gather1_-1_hop3/ppermute | solution.py:155
  23.0 8.6 %collective-permute-start.10 = (bf16[16,6272]{1,0:T(8,128)(2,1)S(1)}, bf16[16,6272]{1,0:T(8,128)(2,1)S(1)}, u32[]{:S(2)}, u32[]{:S(2)}) collective-permute-start(bf16[16,6272]{1,0:T(8,128)(2,1)S(1)} %collective-permute-done.6.refs_2_), channel_id=1, source_target_pairs={{0,1},{1,2},{2,3},{3,7},{7,6},{6,5},{5,4},{4,0},{8,9},{9,10},{10,1... | collective-permute-start | bytes 602120 | tf_op jit(solution)/shard_map/gather1_+1_hop3/ppermute | solution.py:155
  25.2 8.6 %collective-permute-start.11 = (bf16[16,6272]{1,0:T(8,128)(2,1)S(1)}, bf16[16,6272]{1,0:T(8,128)(2,1)S(1)}, u32[]{:S(2)}, u32[]{:S(2)}) collective-permute-start(bf16[16,6272]{1,0:T(8,128)(2,1)S(1)} %collective-permute-done.7.refs_3_), channel_id=1, source_target_pairs={{0,4},{1,0},{2,1},{3,2},{7,3},{6,7},{5,6},{4,5},{8,12},{9,8},{10,9... | collective-permute-start | bytes 602120 | tf_op jit(solution)/shard_map/gather0_-1_hop3/ppermute | solution.py:155
  28.0 8.6 %collective-permute-start.12 = (bf16[16,6272]{1,0:T(8,128)(2,1)S(1)}, bf16[16,6272]{1,0:T(8,128)(2,1)S(1)}, u32[]{:S(2)}, u32[]{:S(2)}) collective-permute-start(bf16[16,6272]{1,0:T(8,128)(2,1)S(1)} %collective-permute-done.8.refs_0_), channel_id=1, source_target_pairs={{0,1},{1,2},{2,3},{3,7},{7,6},{6,5},{5,4},{4,0},{8,9},{9,10},{10,1... | collective-permute-start | bytes 602120 | tf_op jit(solution)/shard_map/gather0_+1_hop4/ppermute | solution.py:155
  39.2 7.9 %collective-permute-start.20 = (bf16[48,2048]{1,0:T(8,128)(2,1)S(1)}, bf16[48,2048]{1,0:T(8,128)(2,1)S(1)}, u32[]{:S(2)}, u32[]{:S(2)}) collective-permute-start(bf16[48,2048]{1,0:T(8,128)(2,1)S(1)} %get-tuple-element.44), channel_id=1, source_target_pairs={{0,1},{1,2},{2,3},{3,7},{7,6},{6,5},{5,4},{4,0},{8,9},{9,10},{10,1... | collective-permute-start | bytes 589832 | tf_op jit(solution)/shard_map/sum1_+1_left4/ppermute | solution.py:155
  41.0 10.0 %collective-permute-start.19 = (bf16[48,2048]{1,0:T(8,128)(2,1)S(1)}, bf16[48,2048]{1,0:T(8,128)(2,1)S(1)}, u32[]{:S(2)}, u32[]{:S(2)}) collective-permute-start(bf16[48,2048]{1,0:T(8,128)(2,1)S(1)} %get-tuple-element.45), channel_id=1, source_target_pairs={{0,4},{1,0},{2,1},{3,2},{7,3},{6,7},{5,6},{4,5},{8,12},{9,8},{10,9... | collective-permute-start | bytes 589832 | tf_op jit(solution)/shard_map/sum1_-1_left3/ppermute | solution.py:155
  41.3 10.1 %collective-permute-start.18 = (bf16[48,2048]{1,0:T(8,128)(2,1)S(1)}, bf16[48,2048]{1,0:T(8,128)(2,1)S(1)}, u32[]{:S(2)}, u32[]{:S(2)}) collective-permute-start(bf16[48,2048]{1,0:T(8,128)(2,1)S(1)} %get-tuple-element.46), channel_id=1, source_target_pairs={{0,1},{1,2},{2,3},{3,7},{7,6},{6,5},{5,4},{4,0},{8,9},{9,10},{10,1... | collective-permute-start | bytes 589832 | tf_op jit(solution)/shard_map/sum0_+1_left3/ppermute | solution.py:155
  46.8 8.4 %collective-permute-start.15 = (bf16[48,2048]{1,0:T(8,128)(2,1)S(1)}, bf16[48,2048]{1,0:T(8,128)(2,1)S(1)}, u32[]{:S(2)}, u32[]{:S(2)}) collective-permute-start(bf16[48,2048]{1,0:T(8,128)(2,1)S(1)} %add_convert_fusion.11), channel_id=1, source_target_pairs={{0,4},{1,0},{2,1},{3,2},{7,3},{6,7},{5,6},{4,5},{8,12},{9,8},{10,9... | collective-permute-start | bytes 589832 | tf_op jit(solution)/shard_map/sum0_-1_left3/ppermute | solution.py:155
  47.2 8.4 %collective-permute-start.23 = (bf16[48,2048]{1,0:T(8,128)(2,1)S(1)}, bf16[48,2048]{1,0:T(8,128)(2,1)S(1)}, u32[]{:S(2)}, u32[]{:S(2)}) collective-permute-start(bf16[48,2048]{1,0:T(8,128)(2,1)S(1)} %add_convert_fusion.6), channel_id=1, source_target_pairs={{0,1},{1,2},{2,3},{3,7},{7,6},{6,5},{5,4},{4,0},{8,9},{9,10},{10,1... | collective-permute-start | bytes 589832 | tf_op jit(solution)/shard_map/sum1_+1_left3/ppermute | solution.py:155
  51.0 8.4 %collective-permute-start.22 = (bf16[48,2048]{1,0:T(8,128)(2,1)S(1)}, bf16[48,2048]{1,0:T(8,128)(2,1)S(1)}, u32[]{:S(2)}, u32[]{:S(2)}) collective-permute-start(bf16[48,2048]{1,0:T(8,128)(2,1)S(1)} %add_convert_fusion.7), channel_id=1, source_target_pairs={{0,4},{1,0},{2,1},{3,2},{7,3},{6,7},{5,6},{4,5},{8,12},{9,8},{10,9... | collective-permute-start | bytes 589832 | tf_op jit(solution)/shard_map/sum1_-1_left2/ppermute | solution.py:155
  51.4 8.4 %collective-permute-start.21 = (bf16[48,2048]{1,0:T(8,128)(2,1)S(1)}, bf16[48,2048]{1,0:T(8,128)(2,1)S(1)}, u32[]{:S(2)}, u32[]{:S(2)}) collective-permute-start(bf16[48,2048]{1,0:T(8,128)(2,1)S(1)} %add_convert_fusion.8), channel_id=1, source_target_pairs={{0,1},{1,2},{2,3},{3,7},{7,6},{6,5},{5,4},{4,0},{8,9},{9,10},{10,1... | collective-permute-start | bytes 589832 | tf_op jit(solution)/shard_map/sum0_+1_left2/ppermute | solution.py:155
  55.2 8.4 %collective-permute-start.16 = (bf16[48,2048]{1,0:T(8,128)(2,1)S(1)}, bf16[48,2048]{1,0:T(8,128)(2,1)S(1)}, u32[]{:S(2)}, u32[]{:S(2)}) collective-permute-start(bf16[48,2048]{1,0:T(8,128)(2,1)S(1)} %add_convert_fusion.10), channel_id=1, source_target_pairs={{0,4},{1,0},{2,1},{3,2},{7,3},{6,7},{5,6},{4,5},{8,12},{9,8},{10,9... | collective-permute-start | bytes 589832 | tf_op jit(solution)/shard_map/sum0_-1_left2/ppermute | solution.py:155
  55.6 8.4 %collective-permute-start.26 = (bf16[48,2048]{1,0:T(8,128)(2,1)S(1)}, bf16[48,2048]{1,0:T(8,128)(2,1)S(1)}, u32[]{:S(2)}, u32[]{:S(2)}) collective-permute-start(bf16[48,2048]{1,0:T(8,128)(2,1)S(1)} %add_convert_fusion.3), channel_id=1, source_target_pairs={{0,1},{1,2},{2,3},{3,7},{7,6},{6,5},{5,4},{4,0},{8,9},{9,10},{10,1... | collective-permute-start | bytes 589832 | tf_op jit(solution)/shard_map/sum1_+1_left2/ppermute | solution.py:155
  59.4 10.3 %collective-permute-start.25 = (bf16[48,2048]{1,0:T(8,128)(2,1)S(1)}, bf16[48,2048]{1,0:T(8,128)(2,1)S(1)}, u32[]{:S(2)}, u32[]{:S(2)}) collective-permute-start(bf16[48,2048]{1,0:T(8,128)(2,1)S(1)} %add_convert_fusion.4), channel_id=1, source_target_pairs={{0,4},{1,0},{2,1},{3,2},{7,3},{6,7},{5,6},{4,5},{8,12},{9,8},{10,9... | collective-permute-start | bytes 589832 | tf_op jit(solution)/shard_map/sum1_-1_left1/ppermute | solution.py:155
  59.9 8.0 %collective-permute-start.24 = (bf16[48,2048]{1,0:T(8,128)(2,1)S(1)}, bf16[48,2048]{1,0:T(8,128)(2,1)S(1)}, u32[]{:S(2)}, u32[]{:S(2)}) collective-permute-start(bf16[48,2048]{1,0:T(8,128)(2,1)S(1)} %add_convert_fusion.5), channel_id=1, source_target_pairs={{0,1},{1,2},{2,3},{3,7},{7,6},{6,5},{5,4},{4,0},{8,9},{9,10},{10,1... | collective-permute-start | bytes 589832 | tf_op jit(solution)/shard_map/sum0_+1_left1/ppermute | solution.py:155
  (7 other events, 45.6 us)

commit v4 on v3

--- a/solution.py
+++ b/solution.py
@@ -164,7 +164,7 @@
     rows = blocks[0].shape[0]
     groups = blocks[0].shape[1] // width
     tok_dev = rows * groups
-    part = 256
+    part = 512
 
     me = lax.axis_index("ex") * lax.axis_size("ey") + lax.axis_index("ey")
     experts = lax.axis_size("ex") * lax.axis_size("ey")

time: 70.9 us -> 70.9 us (level)
  no operation moved by 1% of the time
where the time goes in v4:
time: 70.9 us; the launch traced here: 70.8 us
  starting transfers between devices  30.4 us (43%)
  waiting for transfers between devices  25.1 us (35%)
  Pallas kernels  13.8 us (19%)
  other arithmetic  1.33 us (2%)
    ppermute x28, starting transfers between devices, pass_on(): return lax.ppermute(block, ('ex', 'ey'), pairs)  30.4 us
    ppermute x28, waiting for transfers between devices, pass_on(): return lax.ppermute(block, ('ex', 'ey'), pairs)  25.1 us
    pallas_call x5, Pallas kernels, run_expert(): pl.pallas_call(functools.partial(expert_kernel, count), in_specs=[in_vmem...  12.5 us
  transfers between devices with their start and end apart: 28, of which 14 were waited for; matrix products, arithmetic and copies ran while one was open for 1% of the time, Pallas kernels for 15%

profile of v4, /device:TPU:0, one launch (start us, length us, event | category | flops | bytes accessed | tf_op | source)
XLA Modules:
  0.0 70.8 jit_solution(7069866010777730499)
XLA Ops:
  1.3 3.1 %collective-permute-start = (bf16[16,6272]{1,0:T(8,128)(2,1)S(1)}, bf16[16,6272]{1,0:T(8,128)(2,1)S(1)}, u32[]{:S(2)}, u32[]{:S(2)}) collective-permute-start(bf16[16,6272]{1,0:T(8,128)(2,1)S(1)} %get-tuple-element.31.refs_0_), channel_id=1, source_target_pairs={{0,1},{1,2},{2,3},{3,7},{7,6},{6,5},{5,4},{4,0},{8,9},{9,10},{10,1... | collective-permute-start | bytes 602120 | tf_op jit(solution)/shard_map/gather0_+1_hop1/ppermute | solution.py:155
  4.4 2.0 %collective-permute-start.2 = (bf16[16,6272]{1,0:T(8,128)(2,1)S(1)}, bf16[16,6272]{1,0:T(8,128)(2,1)S(1)}, u32[]{:S(2)}, u32[]{:S(2)}) collective-permute-start(bf16[16,6272]{1,0:T(8,128)(2,1)S(1)} %get-tuple-element.32.refs_1_), channel_id=1, source_target_pairs={{0,1},{1,2},{2,3},{3,7},{7,6},{6,5},{5,4},{4,0},{8,9},{9,10},{10,1... | collective-permute-start | bytes 602120 | tf_op jit(solution)/shard_map/gather1_+1_hop1/ppermute | solution.py:155
  6.4 2.2 %shard_map.74 = (f32[48,2048]{1,0:T(8,128)S(1)}, f32[48,2048]{1,0:T(8,128)S(1)}) custom-call(bf16[16,6272]{1,0:T(8,128)(2,1)S(1)} %get-tuple-element.31.refs_0_, bf16[16,6272]{1,0:T(8,128)(2,1)S(1)} %get-tuple-element.32.refs_1_, bf16[1,2048,1024]{2,1,0:T(8,128)(2,1)S(1)} %copy-done, bf16[1,2048,1024]{2,1,0:T(8,128)(2,1)S(1)} %copy-done.1, ...), custom_call_target="tpu_custom_call" | custom-call | flops 1207959552 | bytes 13762560 | tf_op jit(solution)/shard_map/pallas_call | solution.py:210
  10.1 2.1 %collective-permute-start.4 = (bf16[16,6272]{1,0:T(8,128)(2,1)S(1)}, bf16[16,6272]{1,0:T(8,128)(2,1)S(1)}, u32[]{:S(2)}, u32[]{:S(2)}) collective-permute-start(bf16[16,6272]{1,0:T(8,128)(2,1)S(1)} %collective-permute-done.refs_0_), channel_id=1, source_target_pairs={{0,1},{1,2},{2,3},{3,7},{7,6},{6,5},{5,4},{4,0},{8,9},{9,10},{10,1... | collective-permute-start | bytes 602120 | tf_op jit(solution)/shard_map/gather0_+1_hop2/ppermute | solution.py:155
  12.3 2.1 %collective-permute-done.2.refs_2_ = bf16[16,6272]{1,0:T(8,128)(2,1)S(1)} collective-permute-done((bf16[16,6272]{1,0:T(8,128)(2,1)S(1)}, bf16[16,6272]{1,0:T(8,128)(2,1)S(1)}, u32[]{:S(2)}, u32[]{:S(2)}) %collective-permute-start.2) | collective-permute-done | bytes 200736 | tf_op jit(solution)/shard_map/gather1_+1_hop1/ppermute | solution.py:155
  14.4 2.1 %collective-permute-start.6 = (bf16[16,6272]{1,0:T(8,128)(2,1)S(1)}, bf16[16,6272]{1,0:T(8,128)(2,1)S(1)}, u32[]{:S(2)}, u32[]{:S(2)}) collective-permute-start(bf16[16,6272]{1,0:T(8,128)(2,1)S(1)} %collective-permute-done.2.refs_2_), channel_id=1, source_target_pairs={{0,1},{1,2},{2,3},{3,7},{7,6},{6,5},{5,4},{4,0},{8,9},{9,10},{10,1... | collective-permute-start | bytes 602120 | tf_op jit(solution)/shard_map/gather1_+1_hop2/ppermute | solution.py:155
  16.6 2.7 %shard_map.75 = (f32[48,2048]{1,0:T(8,128)S(1)}, f32[48,2048]{1,0:T(8,128)S(1)}, f32[48,2048]{1,0:T(8,128)S(1)}, f32[48,2048]{1,0:T(8,128)S(1)}) custom-call(bf16[16,6272]{1,0:T(8,128)(2,1)S(1)} %collective-permute-done.refs_0_, bf16[16,6272]{1,0:T(8,128)(2,1)S(1)} %collective-permute-done.1.refs_1_, bf16[16,6272]{1,0:T(8,128)(2,1)S(1)} %collective-permute-done.2.refs_2_, ...), custom_call_target="tpu_custom_call" | custom-call | flops 2415919104 | bytes 14942208 | tf_op jit(solution)/shard_map/pallas_call | solution.py:210
  19.3 2.1 %collective-permute-start.8 = (bf16[16,6272]{1,0:T(8,128)(2,1)S(1)}, bf16[16,6272]{1,0:T(8,128)(2,1)S(1)}, u32[]{:S(2)}, u32[]{:S(2)}) collective-permute-start(bf16[16,6272]{1,0:T(8,128)(2,1)S(1)} %collective-permute-done.4.refs_0_), channel_id=1, source_target_pairs={{0,1},{1,2},{2,3},{3,7},{7,6},{6,5},{5,4},{4,0},{8,9},{9,10},{10,1... | collective-permute-start | bytes 602120 | tf_op jit(solution)/shard_map/gather0_+1_hop3/ppermute | solution.py:155
  23.0 2.1 %collective-permute-start.10 = (bf16[16,6272]{1,0:T(8,128)(2,1)S(1)}, bf16[16,6272]{1,0:T(8,128)(2,1)S(1)}, u32[]{:S(2)}, u32[]{:S(2)}) collective-permute-start(bf16[16,6272]{1,0:T(8,128)(2,1)S(1)} %collective-permute-done.6.refs_2_), channel_id=1, source_target_pairs={{0,1},{1,2},{2,3},{3,7},{7,6},{6,5},{5,4},{4,0},{8,9},{9,10},{10,1... | collective-permute-start | bytes 602120 | tf_op jit(solution)/shard_map/gather1_+1_hop3/ppermute | solution.py:155
  25.2 2.7 %shard_map.76 = (f32[48,2048]{1,0:T(8,128)S(1)}, f32[48,2048]{1,0:T(8,128)S(1)}, f32[48,2048]{1,0:T(8,128)S(1)}, f32[48,2048]{1,0:T(8,128)S(1)}) custom-call(bf16[16,6272]{1,0:T(8,128)(2,1)S(1)} %collective-permute-done.4.refs_0_, bf16[16,6272]{1,0:T(8,128)(2,1)S(1)} %collective-permute-done.5.refs_1_, bf16[16,6272]{1,0:T(8,128)(2,1)S(1)} %collective-permute-done.6.refs_2_, ...), custom_call_target="tpu_custom_call" | custom-call | flops 2415919104 | bytes 14942208 | tf_op jit(solution)/shard_map/pallas_call | solution.py:210
  27.9 2.1 %collective-permute-start.12 = (bf16[16,6272]{1,0:T(8,128)(2,1)S(1)}, bf16[16,6272]{1,0:T(8,128)(2,1)S(1)}, u32[]{:S(2)}, u32[]{:S(2)}) collective-permute-start(bf16[16,6272]{1,0:T(8,128)(2,1)S(1)} %collective-permute-done.8.refs_0_), channel_id=1, source_target_pairs={{0,1},{1,2},{2,3},{3,7},{7,6},{6,5},{5,4},{4,0},{8,9},{9,10},{10,1... | collective-permute-start | bytes 602120 | tf_op jit(solution)/shard_map/gather0_+1_hop4/ppermute | solution.py:155
  31.6 2.2 %collective-permute-done.11.refs_3_ = bf16[16,6272]{1,0:T(8,128)(2,1)S(1)} collective-permute-done((bf16[16,6272]{1,0:T(8,128)(2,1)S(1)}, bf16[16,6272]{1,0:T(8,128)(2,1)S(1)}, u32[]{:S(2)}, u32[]{:S(2)}) %collective-permute-start.11) | collective-permute-done | bytes 200736 | tf_op jit(solution)/shard_map/gather0_-1_hop3/ppermute | solution.py:155
  33.8 2.7 %shard_map.77 = (f32[48,2048]{1,0:T(8,128)S(1)}, f32[48,2048]{1,0:T(8,128)S(1)}, bf16[48,2048]{1,0:T(8,128)(2,1)S(1)}, bf16[48,2048]{1,0:T(8,128)(2,1)S(1)}) custom-call(bf16[16,6272]{1,0:T(8,128)(2,1)S(1)} %collective-permute-done.8.refs_0_, bf16[16,6272]{1,0:T(8,128)(2,1)S(1)} %collective-permute-done.9.refs_1_, ...), custom_call_target="tpu_custom_call" | custom-call | flops 2415919104 | bytes 14942208 | tf_op jit(solution)/shard_map/pallas_call | solution.py:210
  36.6 2.2 %shard_map.78 = (bf16[48,2048]{1,0:T(8,128)(2,1)S(1)}, bf16[48,2048]{1,0:T(8,128)(2,1)S(1)}) custom-call(bf16[16,6272]{1,0:T(8,128)(2,1)S(1)} %collective-permute-done.12.refs_0_, bf16[16,6272]{1,0:T(8,128)(2,1)S(1)} %collective-permute-done.13.refs_1_, bf16[1,2048,1024]{2,1,0:T(8,128)(2,1)S(1)} %copy-done, bf16[1,2048,1024]{2,1,0:T(8,128)(2,1)S(1)} %copy-done.1, ...), custom_call_target="tpu_custom_call" | custom-call | flops 1207959552 | bytes 13762560 | tf_op jit(solution)/shard_map/pallas_call | solution.py:210
  42.9 3.8 %collective-permute-done.14 = bf16[48,2048]{1,0:T(8,128)(2,1)S(1)} collective-permute-done((bf16[48,2048]{1,0:T(8,128)(2,1)S(1)}, bf16[48,2048]{1,0:T(8,128)(2,1)S(1)}, u32[]{:S(2)}, u32[]{:S(2)}) %collective-permute-start.14) | collective-permute-done | bytes 196640 | tf_op jit(solution)/shard_map/sum0_-1_left4/ppermute | solution.py:155
  47.2 1.8 %collective-permute-start.23 = (bf16[48,2048]{1,0:T(8,128)(2,1)S(1)}, bf16[48,2048]{1,0:T(8,128)(2,1)S(1)}, u32[]{:S(2)}, u32[]{:S(2)}) collective-permute-start(bf16[48,2048]{1,0:T(8,128)(2,1)S(1)} %add_convert_fusion.6), channel_id=1, source_target_pairs={{0,1},{1,2},{2,3},{3,7},{7,6},{6,5},{5,4},{4,0},{8,9},{9,10},{10,1... | collective-permute-start | bytes 589832 | tf_op jit(solution)/shard_map/sum1_+1_left3/ppermute | solution.py:155
  49.0 2.0 %collective-permute-done.19 = bf16[48,2048]{1,0:T(8,128)(2,1)S(1)} collective-permute-done((bf16[48,2048]{1,0:T(8,128)(2,1)S(1)}, bf16[48,2048]{1,0:T(8,128)(2,1)S(1)}, u32[]{:S(2)}, u32[]{:S(2)}) %collective-permute-start.19) | collective-permute-done | bytes 196640 | tf_op jit(solution)/shard_map/sum1_-1_left3/ppermute | solution.py:155
  51.4 1.8 %collective-permute-start.21 = (bf16[48,2048]{1,0:T(8,128)(2,1)S(1)}, bf16[48,2048]{1,0:T(8,128)(2,1)S(1)}, u32[]{:S(2)}, u32[]{:S(2)}) collective-permute-start(bf16[48,2048]{1,0:T(8,128)(2,1)S(1)} %add_convert_fusion.8), channel_id=1, source_target_pairs={{0,1},{1,2},{2,3},{3,7},{7,6},{6,5},{5,4},{4,0},{8,9},{9,10},{10,1... | collective-permute-start | bytes 589832 | tf_op jit(solution)/shard_map/sum0_+1_left2/ppermute | solution.py:155
  53.2 2.0 %collective-permute-done.15 = bf16[48,2048]{1,0:T(8,128)(2,1)S(1)} collective-permute-done((bf16[48,2048]{1,0:T(8,128)(2,1)S(1)}, bf16[48,2048]{1,0:T(8,128)(2,1)S(1)}, u32[]{:S(2)}, u32[]{:S(2)}) %collective-permute-start.15) | collective-permute-done | bytes 196640 | tf_op jit(solution)/shard_map/sum0_-1_left3/ppermute | solution.py:155
  57.4 2.0 %collective-permute-done.22 = bf16[48,2048]{1,0:T(8,128)(2,1)S(1)} collective-permute-done((bf16[48,2048]{1,0:T(8,128)(2,1)S(1)}, bf16[48,2048]{1,0:T(8,128)(2,1)S(1)}, u32[]{:S(2)}, u32[]{:S(2)}) %collective-permute-start.22) | collective-permute-done | bytes 196640 | tf_op jit(solution)/shard_map/sum1_-1_left2/ppermute | solution.py:155
  59.8 1.8 %collective-permute-start.24 = (bf16[48,2048]{1,0:T(8,128)(2,1)S(1)}, bf16[48,2048]{1,0:T(8,128)(2,1)S(1)}, u32[]{:S(2)}, u32[]{:S(2)}) collective-permute-start(bf16[48,2048]{1,0:T(8,128)(2,1)S(1)} %add_convert_fusion.5), channel_id=1, source_target_pairs={{0,1},{1,2},{2,3},{3,7},{7,6},{6,5},{5,4},{4,0},{8,9},{9,10},{10,1... | collective-permute-start | bytes 589832 | tf_op jit(solution)/shard_map/sum0_+1_left1/ppermute | solution.py:155
  61.6 2.0 %collective-permute-done.16 = bf16[48,2048]{1,0:T(8,128)(2,1)S(1)} collective-permute-done((bf16[48,2048]{1,0:T(8,128)(2,1)S(1)}, bf16[48,2048]{1,0:T(8,128)(2,1)S(1)}, u32[]{:S(2)}, u32[]{:S(2)}) %collective-permute-start.16) | collective-permute-done | bytes 196640 | tf_op jit(solution)/shard_map/sum0_-1_left2/ppermute | solution.py:155
  64.0 1.8 %collective-permute-start.27 = (bf16[48,2048]{1,0:T(8,128)(2,1)S(1)}, bf16[48,2048]{1,0:T(8,128)(2,1)S(1)}, u32[]{:S(2)}, u32[]{:S(2)}) collective-permute-start(bf16[48,2048]{1,0:T(8,128)(2,1)S(1)} %add_convert_fusion.1), channel_id=1, source_target_pairs={{0,1},{1,2},{2,3},{3,7},{7,6},{6,5},{5,4},{4,0},{8,9},{9,10},{10,1... | collective-permute-start | bytes 589832 | tf_op jit(solution)/shard_map/sum1_+1_left1/ppermute | solution.py:155
  65.8 2.0 %collective-permute-done.24 = bf16[48,2048]{1,0:T(8,128)(2,1)S(1)} collective-permute-done((bf16[48,2048]{1,0:T(8,128)(2,1)S(1)}, bf16[48,2048]{1,0:T(8,128)(2,1)S(1)}, u32[]{:S(2)}, u32[]{:S(2)}) %collective-permute-start.24) | collective-permute-done | bytes 196640 | tf_op jit(solution)/shard_map/sum0_+1_left1/ppermute | solution.py:155
  (57 shorter events, 17.3 us)
Async XLA Ops:
  1.3 8.8 %collective-permute-start = (bf16[16,6272]{1,0:T(8,128)(2,1)S(1)}, bf16[16,6272]{1,0:T(8,128)(2,1)S(1)}, u32[]{:S(2)}, u32[]{:S(2)}) collective-permute-start(bf16[16,6272]{1,0:T(8,128)(2,1)S(1)} %get-tuple-element.31.refs_0_), channel_id=1, source_target_pairs={{0,1},{1,2},{2,3},{3,7},{7,6},{6,5},{5,4},{4,0},{8,9},{9,10},{10,1... | collective-permute-start | bytes 602120 | tf_op jit(solution)/shard_map/gather0_+1_hop1/ppermute | solution.py:155
  4.4 7.9 %collective-permute-start.1 = (bf16[16,6272]{1,0:T(8,128)(2,1)S(1)}, bf16[16,6272]{1,0:T(8,128)(2,1)S(1)}, u32[]{:S(2)}, u32[]{:S(2)}) collective-permute-start(bf16[16,6272]{1,0:T(8,128)(2,1)S(1)} %get-tuple-element.32.refs_1_), channel_id=1, source_target_pairs={{0,4},{1,0},{2,1},{3,2},{7,3},{6,7},{5,6},{4,5},{8,12},{9,8},{10,9... | collective-permute-start | bytes 602120 | tf_op jit(solution)/shard_map/gather1_-1_hop1/ppermute | solution.py:155
  4.4 10.1 %collective-permute-start.2 = (bf16[16,6272]{1,0:T(8,128)(2,1)S(1)}, bf16[16,6272]{1,0:T(8,128)(2,1)S(1)}, u32[]{:S(2)}, u32[]{:S(2)}) collective-permute-start(bf16[16,6272]{1,0:T(8,128)(2,1)S(1)} %get-tuple-element.32.refs_1_), channel_id=1, source_target_pairs={{0,1},{1,2},{2,3},{3,7},{7,6},{6,5},{5,4},{4,0},{8,9},{9,10},{10,1... | collective-permute-start | bytes 602120 | tf_op jit(solution)/shard_map/gather1_+1_hop1/ppermute | solution.py:155
  6.4 10.2 %collective-permute-start.3 = (bf16[16,6272]{1,0:T(8,128)(2,1)S(1)}, bf16[16,6272]{1,0:T(8,128)(2,1)S(1)}, u32[]{:S(2)}, u32[]{:S(2)}) collective-permute-start(bf16[16,6272]{1,0:T(8,128)(2,1)S(1)} %get-tuple-element.31.refs_0_), channel_id=1, source_target_pairs={{0,4},{1,0},{2,1},{3,2},{7,3},{6,7},{5,6},{4,5},{8,12},{9,8},{10,9... | collective-permute-start | bytes 602120 | tf_op jit(solution)/shard_map/gather0_-1_hop1/ppermute | solution.py:155
  10.1 9.2 %collective-permute-start.4 = (bf16[16,6272]{1,0:T(8,128)(2,1)S(1)}, bf16[16,6272]{1,0:T(8,128)(2,1)S(1)}, u32[]{:S(2)}, u32[]{:S(2)}) collective-permute-start(bf16[16,6272]{1,0:T(8,128)(2,1)S(1)} %collective-permute-done.refs_0_), channel_id=1, source_target_pairs={{0,1},{1,2},{2,3},{3,7},{7,6},{6,5},{5,4},{4,0},{8,9},{9,10},{10,1... | collective-permute-start | bytes 602120 | tf_op jit(solution)/shard_map/gather0_+1_hop2/ppermute | solution.py:155
  12.3 9.1 %collective-permute-start.5 = (bf16[16,6272]{1,0:T(8,128)(2,1)S(1)}, bf16[16,6272]{1,0:T(8,128)(2,1)S(1)}, u32[]{:S(2)}, u32[]{:S(2)}) collective-permute-start(bf16[16,6272]{1,0:T(8,128)(2,1)S(1)} %collective-permute-done.1.refs_1_), channel_id=1, source_target_pairs={{0,4},{1,0},{2,1},{3,2},{7,3},{6,7},{5,6},{4,5},{8,12},{9,8},{10,9... | collective-permute-start | bytes 602120 | tf_op jit(solution)/shard_map/gather1_-1_hop2/ppermute | solution.py:155
  14.4 8.6 %collective-permute-start.6 = (bf16[16,6272]{1,0:T(8,128)(2,1)S(1)}, bf16[16,6272]{1,0:T(8,128)(2,1)S(1)}, u32[]{:S(2)}, u32[]{:S(2)}) collective-permute-start(bf16[16,6272]{1,0:T(8,128)(2,1)S(1)} %collective-permute-done.2.refs_2_), channel_id=1, source_target_pairs={{0,1},{1,2},{2,3},{3,7},{7,6},{6,5},{5,4},{4,0},{8,9},{9,10},{10,1... | collective-permute-start | bytes 602120 | tf_op jit(solution)/shard_map/gather1_+1_hop2/ppermute | solution.py:155
  16.6 8.6 %collective-permute-start.7 = (bf16[16,6272]{1,0:T(8,128)(2,1)S(1)}, bf16[16,6272]{1,0:T(8,128)(2,1)S(1)}, u32[]{:S(2)}, u32[]{:S(2)}) collective-permute-start(bf16[16,6272]{1,0:T(8,128)(2,1)S(1)} %collective-permute-done.3.refs_3_), channel_id=1, source_target_pairs={{0,4},{1,0},{2,1},{3,2},{7,3},{6,7},{5,6},{4,5},{8,12},{9,8},{10,9... | collective-permute-start | bytes 602120 | tf_op jit(solution)/shard_map/gather0_-1_hop2/ppermute | solution.py:155
  19.3 8.6 %collective-permute-start.8 = (bf16[16,6272]{1,0:T(8,128)(2,1)S(1)}, bf16[16,6272]{1,0:T(8,128)(2,1)S(1)}, u32[]{:S(2)}, u32[]{:S(2)}) collective-permute-start(bf16[16,6272]{1,0:T(8,128)(2,1)S(1)} %collective-permute-done.4.refs_0_), channel_id=1, source_target_pairs={{0,1},{1,2},{2,3},{3,7},{7,6},{6,5},{5,4},{4,0},{8,9},{9,10},{10,1... | collective-permute-start | bytes 602120 | tf_op jit(solution)/shard_map/gather0_+1_hop3/ppermute | solution.py:155
  21.4 8.6 %collective-permute-start.9 = (bf16[16,6272]{1,0:T(8,128)(2,1)S(1)}, bf16[16,6272]{1,0:T(8,128)(2,1)S(1)}, u32[]{:S(2)}, u32[]{:S(2)}) collective-permute-start(bf16[16,6272]{1,0:T(8,128)(2,1)S(1)} %collective-permute-done.5.refs_1_), channel_id=1, source_target_pairs={{0,4},{1,0},{2,1},{3,2},{7,3},{6,7},{5,6},{4,5},{8,12},{9,8},{10,9... | collective-permute-start | bytes 602120 | tf_op jit(solution)/shard_map/gather1_-1_hop3/ppermute | solution.py:155
  23.0 8.6 %collective-permute-start.10 = (bf16[16,6272]{1,0:T(8,128)(2,1)S(1)}, bf16[16,6272]{1,0:T(8,128)(2,1)S(1)}, u32[]{:S(2)}, u32[]{:S(2)}) collective-permute-start(bf16[16,6272]{1,0:T(8,128)(2,1)S(1)} %collective-permute-done.6.refs_2_), channel_id=1, source_target_pairs={{0,1},{1,2},{2,3},{3,7},{7,6},{6,5},{5,4},{4,0},{8,9},{9,10},{10,1... | collective-permute-start | bytes 602120 | tf_op jit(solution)/shard_map/gather1_+1_hop3/ppermute | solution.py:155
  25.2 8.6 %collective-permute-start.11 = (bf16[16,6272]{1,0:T(8,128)(2,1)S(1)}, bf16[16,6272]{1,0:T(8,128)(2,1)S(1)}, u32[]{:S(2)}, u32[]{:S(2)}) collective-permute-start(bf16[16,6272]{1,0:T(8,128)(2,1)S(1)} %collective-permute-done.7.refs_3_), channel_id=1, source_target_pairs={{0,4},{1,0},{2,1},{3,2},{7,3},{6,7},{5,6},{4,5},{8,12},{9,8},{10,9... | collective-permute-start | bytes 602120 | tf_op jit(solution)/shard_map/gather0_-1_hop3/ppermute | solution.py:155
  27.9 8.6 %collective-permute-start.12 = (bf16[16,6272]{1,0:T(8,128)(2,1)S(1)}, bf16[16,6272]{1,0:T(8,128)(2,1)S(1)}, u32[]{:S(2)}, u32[]{:S(2)}) collective-permute-start(bf16[16,6272]{1,0:T(8,128)(2,1)S(1)} %collective-permute-done.8.refs_0_), channel_id=1, source_target_pairs={{0,1},{1,2},{2,3},{3,7},{7,6},{6,5},{5,4},{4,0},{8,9},{9,10},{10,1... | collective-permute-start | bytes 602120 | tf_op jit(solution)/shard_map/gather0_+1_hop4/ppermute | solution.py:155
  39.2 7.9 %collective-permute-start.20 = (bf16[48,2048]{1,0:T(8,128)(2,1)S(1)}, bf16[48,2048]{1,0:T(8,128)(2,1)S(1)}, u32[]{:S(2)}, u32[]{:S(2)}) collective-permute-start(bf16[48,2048]{1,0:T(8,128)(2,1)S(1)} %get-tuple-element.44), channel_id=1, source_target_pairs={{0,1},{1,2},{2,3},{3,7},{7,6},{6,5},{5,4},{4,0},{8,9},{9,10},{10,1... | collective-permute-start | bytes 589832 | tf_op jit(solution)/shard_map/sum1_+1_left4/ppermute | solution.py:155
  40.9 10.0 %collective-permute-start.19 = (bf16[48,2048]{1,0:T(8,128)(2,1)S(1)}, bf16[48,2048]{1,0:T(8,128)(2,1)S(1)}, u32[]{:S(2)}, u32[]{:S(2)}) collective-permute-start(bf16[48,2048]{1,0:T(8,128)(2,1)S(1)} %get-tuple-element.45), channel_id=1, source_target_pairs={{0,4},{1,0},{2,1},{3,2},{7,3},{6,7},{5,6},{4,5},{8,12},{9,8},{10,9... | collective-permute-start | bytes 589832 | tf_op jit(solution)/shard_map/sum1_-1_left3/ppermute | solution.py:155
  41.2 10.1 %collective-permute-start.18 = (bf16[48,2048]{1,0:T(8,128)(2,1)S(1)}, bf16[48,2048]{1,0:T(8,128)(2,1)S(1)}, u32[]{:S(2)}, u32[]{:S(2)}) collective-permute-start(bf16[48,2048]{1,0:T(8,128)(2,1)S(1)} %get-tuple-element.46), channel_id=1, source_target_pairs={{0,1},{1,2},{2,3},{3,7},{7,6},{6,5},{5,4},{4,0},{8,9},{9,10},{10,1... | collective-permute-start | bytes 589832 | tf_op jit(solution)/shard_map/sum0_+1_left3/ppermute | solution.py:155
  46.8 8.4 %collective-permute-start.15 = (bf16[48,2048]{1,0:T(8,128)(2,1)S(1)}, bf16[48,2048]{1,0:T(8,128)(2,1)S(1)}, u32[]{:S(2)}, u32[]{:S(2)}) collective-permute-start(bf16[48,2048]{1,0:T(8,128)(2,1)S(1)} %add_convert_fusion.11), channel_id=1, source_target_pairs={{0,4},{1,0},{2,1},{3,2},{7,3},{6,7},{5,6},{4,5},{8,12},{9,8},{10,9... | collective-permute-start | bytes 589832 | tf_op jit(solution)/shard_map/sum0_-1_left3/ppermute | solution.py:155
  47.2 8.4 %collective-permute-start.23 = (bf16[48,2048]{1,0:T(8,128)(2,1)S(1)}, bf16[48,2048]{1,0:T(8,128)(2,1)S(1)}, u32[]{:S(2)}, u32[]{:S(2)}) collective-permute-start(bf16[48,2048]{1,0:T(8,128)(2,1)S(1)} %add_convert_fusion.6), channel_id=1, source_target_pairs={{0,1},{1,2},{2,3},{3,7},{7,6},{6,5},{5,4},{4,0},{8,9},{9,10},{10,1... | collective-permute-start | bytes 589832 | tf_op jit(solution)/shard_map/sum1_+1_left3/ppermute | solution.py:155
  51.0 8.4 %collective-permute-start.22 = (bf16[48,2048]{1,0:T(8,128)(2,1)S(1)}, bf16[48,2048]{1,0:T(8,128)(2,1)S(1)}, u32[]{:S(2)}, u32[]{:S(2)}) collective-permute-start(bf16[48,2048]{1,0:T(8,128)(2,1)S(1)} %add_convert_fusion.7), channel_id=1, source_target_pairs={{0,4},{1,0},{2,1},{3,2},{7,3},{6,7},{5,6},{4,5},{8,12},{9,8},{10,9... | collective-permute-start | bytes 589832 | tf_op jit(solution)/shard_map/sum1_-1_left2/ppermute | solution.py:155
  51.4 8.4 %collective-permute-start.21 = (bf16[48,2048]{1,0:T(8,128)(2,1)S(1)}, bf16[48,2048]{1,0:T(8,128)(2,1)S(1)}, u32[]{:S(2)}, u32[]{:S(2)}) collective-permute-start(bf16[48,2048]{1,0:T(8,128)(2,1)S(1)} %add_convert_fusion.8), channel_id=1, source_target_pairs={{0,1},{1,2},{2,3},{3,7},{7,6},{6,5},{5,4},{4,0},{8,9},{9,10},{10,1... | collective-permute-start | bytes 589832 | tf_op jit(solution)/shard_map/sum0_+1_left2/ppermute | solution.py:155
  55.2 8.4 %collective-permute-start.16 = (bf16[48,2048]{1,0:T(8,128)(2,1)S(1)}, bf16[48,2048]{1,0:T(8,128)(2,1)S(1)}, u32[]{:S(2)}, u32[]{:S(2)}) collective-permute-start(bf16[48,2048]{1,0:T(8,128)(2,1)S(1)} %add_convert_fusion.10), channel_id=1, source_target_pairs={{0,4},{1,0},{2,1},{3,2},{7,3},{6,7},{5,6},{4,5},{8,12},{9,8},{10,9... | collective-permute-start | bytes 589832 | tf_op jit(solution)/shard_map/sum0_-1_left2/ppermute | solution.py:155
  55.6 8.4 %collective-permute-start.26 = (bf16[48,2048]{1,0:T(8,128)(2,1)S(1)}, bf16[48,2048]{1,0:T(8,128)(2,1)S(1)}, u32[]{:S(2)}, u32[]{:S(2)}) collective-permute-start(bf16[48,2048]{1,0:T(8,128)(2,1)S(1)} %add_convert_fusion.3), channel_id=1, source_target_pairs={{0,1},{1,2},{2,3},{3,7},{7,6},{6,5},{5,4},{4,0},{8,9},{9,10},{10,1... | collective-permute-start | bytes 589832 | tf_op jit(solution)/shard_map/sum1_+1_left2/ppermute | solution.py:155
  59.4 10.3 %collective-permute-start.25 = (bf16[48,2048]{1,0:T(8,128)(2,1)S(1)}, bf16[48,2048]{1,0:T(8,128)(2,1)S(1)}, u32[]{:S(2)}, u32[]{:S(2)}) collective-permute-start(bf16[48,2048]{1,0:T(8,128)(2,1)S(1)} %add_convert_fusion.4), channel_id=1, source_target_pairs={{0,4},{1,0},{2,1},{3,2},{7,3},{6,7},{5,6},{4,5},{8,12},{9,8},{10,9... | collective-permute-start | bytes 589832 | tf_op jit(solution)/shard_map/sum1_-1_left1/ppermute | solution.py:155
  59.8 8.0 %collective-permute-start.24 = (bf16[48,2048]{1,0:T(8,128)(2,1)S(1)}, bf16[48,2048]{1,0:T(8,128)(2,1)S(1)}, u32[]{:S(2)}, u32[]{:S(2)}) collective-permute-start(bf16[48,2048]{1,0:T(8,128)(2,1)S(1)} %add_convert_fusion.5), channel_id=1, source_target_pairs={{0,1},{1,2},{2,3},{3,7},{7,6},{6,5},{5,4},{4,0},{8,9},{9,10},{10,1... | collective-permute-start | bytes 589832 | tf_op jit(solution)/shard_map/sum0_+1_left1/ppermute | solution.py:155
  (7 other events, 45.7 us)

commit v5 on v2

--- a/solution.py
+++ b/solution.py
@@ -252,7 +252,7 @@
 
     long_chains = [(index, 1 if index % 2 == 0 else -1) for index in range(micro)]
     short_chains = [(index, -stride) for index, stride in long_chains]
-    chains = [short_chains[1], short_chains[0], long_chains[0], long_chains[1]]
+    chains = [long_chains[0], long_chains[1], short_chains[1], short_chains[0]]
     long_reach, short_reach = experts // 2, (experts - 1) // 2
 
     gathered = [{0: packed[index]} for index in range(micro)]
@@ -300,14 +300,15 @@
     marker = mark()
     done = []
     for hop in range(1, short_reach + 1):
-        gather_hop(long_chains + short_chains[1:], hop, [marker])
-        gather_hop(short_chains[:1], hop, [])
+        gather_hop(long_chains + short_chains[:1], hop, [marker] + [])
+        gather_hop(short_chains[1:], hop, [])
+        if hop == 1:
+            done = expert(chains, [0], [])
         if hop == short_reach - 1:
-            done = expert(chains, range(short_reach - 2, -1, -1), [])
+            done = expert(chains, range(short_reach - 2, 0, -1), done)
     done = expert(chains, [short_reach - 1], done)
     gather_hop(long_chains, long_reach, done)
-    done = expert(long_chains, [short_reach], done)
-    done = expert(short_chains[::-1], [short_reach], done)
+    done = expert(long_chains + short_chains[::-1], [short_reach], done)
     last = [gathered[index][-long_reach * stride] for index, stride in long_chains]
     done = expert(long_chains, [long_reach], done)
     for left in range(long_reach, 0, -1):

time: 72.9 us -> 72.4 us (level)
  transfers between devices with their start and end apart: 28 -> 28, of which waited for: 18 -> 12; matrix products, arithmetic and copies ran while one was open for 1% -> 1% of each run, Pallas kernels for 15% -> 15%
where the time goes in v5:
time: 72.4 us; the launch traced here: 72.3 us
  starting transfers between devices  30.2 us (42%)
  waiting for transfers between devices  26.6 us (37%)
  Pallas kernels  14 us (19%)
  other arithmetic  1.35 us (2%)
    ppermute x28, starting transfers between devices, pass_on(): return lax.ppermute(block, ('ex', 'ey'), pairs)  30.2 us
    ppermute x28, waiting for transfers between devices, pass_on(): return lax.ppermute(block, ('ex', 'ey'), pairs)  26.6 us
    pallas_call x5, Pallas kernels, run_expert(): pl.pallas_call(functools.partial(expert_kernel, count), in_specs=[in_vmem...  12.7 us
  transfers between devices with their start and end apart: 28, of which 12 were waited for; matrix products, arithmetic and copies ran while one was open for 1% of the time, Pallas kernels for 15%

profile of v5, /device:TPU:0, one launch (start us, length us, event | category | flops | bytes accessed | tf_op | source)
XLA Modules:
  0.0 72.3 jit_solution(5608178699572701003)
XLA Ops:
  1.3 3.1 %collective-permute-start = (bf16[16,6272]{1,0:T(8,128)(2,1)S(1)}, bf16[16,6272]{1,0:T(8,128)(2,1)S(1)}, u32[]{:S(2)}, u32[]{:S(2)}) collective-permute-start(bf16[16,6272]{1,0:T(8,128)(2,1)S(1)} %get-tuple-element.42.refs_0_), channel_id=1, source_target_pairs={{0,1},{1,2},{2,3},{3,7},{7,6},{6,5},{5,4},{4,0},{8,9},{9,10},{10,1... | collective-permute-start | bytes 602120 | tf_op jit(solution)/shard_map/gather0_+1_hop1/ppermute | solution.py:155
  4.4 2.0 %collective-permute-start.3 = (bf16[16,6272]{1,0:T(8,128)(2,1)S(1)}, bf16[16,6272]{1,0:T(8,128)(2,1)S(1)}, u32[]{:S(2)}, u32[]{:S(2)}) collective-permute-start(bf16[16,6272]{1,0:T(8,128)(2,1)S(1)} %get-tuple-element.42.refs_0_), channel_id=1, source_target_pairs={{0,4},{1,0},{2,1},{3,2},{7,3},{6,7},{5,6},{4,5},{8,12},{9,8},{10,9... | collective-permute-start | bytes 602120 | tf_op jit(solution)/shard_map/gather0_-1_hop1/ppermute | solution.py:155
  6.4 2.3 %shard_map.74 = (f32[48,2048]{1,0:T(8,128)S(1)}, f32[48,2048]{1,0:T(8,128)S(1)}) custom-call(bf16[16,6272]{1,0:T(8,128)(2,1)S(1)} %get-tuple-element.42.refs_0_, bf16[16,6272]{1,0:T(8,128)(2,1)S(1)} %get-tuple-element.43.refs_1_, bf16[1,2048,1024]{2,1,0:T(8,128)(2,1)S(1)} %copy-done, bf16[1,2048,1024]{2,1,0:T(8,128)(2,1)S(1)} %copy-done.1, ...), custom_call_target="tpu_custom_call" | custom-call | flops 1207959552 | bytes 13762560 | tf_op jit(solution)/shard_map/pallas_call | solution.py:224
  10.1 2.1 %collective-permute-start.4 = (bf16[16,6272]{1,0:T(8,128)(2,1)S(1)}, bf16[16,6272]{1,0:T(8,128)(2,1)S(1)}, u32[]{:S(2)}, u32[]{:S(2)}) collective-permute-start(bf16[16,6272]{1,0:T(8,128)(2,1)S(1)} %collective-permute-done.refs_0_), channel_id=1, source_target_pairs={{0,1},{1,2},{2,3},{3,7},{7,6},{6,5},{5,4},{4,0},{8,9},{9,10},{10,1... | collective-permute-start | bytes 602120 | tf_op jit(solution)/shard_map/gather0_+1_hop2/ppermute | solution.py:155
  12.3 4.3 %collective-permute-done.3.refs_3_ = bf16[16,6272]{1,0:T(8,128)(2,1)S(1)} collective-permute-done((bf16[16,6272]{1,0:T(8,128)(2,1)S(1)}, bf16[16,6272]{1,0:T(8,128)(2,1)S(1)}, u32[]{:S(2)}, u32[]{:S(2)}) %collective-permute-start.3) | collective-permute-done | bytes 200736 | tf_op jit(solution)/shard_map/gather0_-1_hop1/ppermute | solution.py:155
  16.6 2.0 %collective-permute-start.6 = (bf16[16,6272]{1,0:T(8,128)(2,1)S(1)}, bf16[16,6272]{1,0:T(8,128)(2,1)S(1)}, u32[]{:S(2)}, u32[]{:S(2)}) collective-permute-start(bf16[16,6272]{1,0:T(8,128)(2,1)S(1)} %collective-permute-done.2.refs_2_), channel_id=1, source_target_pairs={{0,1},{1,2},{2,3},{3,7},{7,6},{6,5},{5,4},{4,0},{8,9},{9,10},{10,1... | collective-permute-start | bytes 602120 | tf_op jit(solution)/shard_map/gather1_+1_hop2/ppermute | solution.py:155
  18.6 2.8 %shard_map.75 = (f32[48,2048]{1,0:T(8,128)S(1)}, f32[48,2048]{1,0:T(8,128)S(1)}, f32[48,2048]{1,0:T(8,128)S(1)}, f32[48,2048]{1,0:T(8,128)S(1)}) custom-call(bf16[16,6272]{1,0:T(8,128)(2,1)S(1)} %collective-permute-done.refs_0_, bf16[16,6272]{1,0:T(8,128)(2,1)S(1)} %collective-permute-done.1.refs_1_, bf16[16,6272]{1,0:T(8,128)(2,1)S(1)} %collective-permute-done.2.refs_2_, ...), custom_call_target="tpu_custom_call" | custom-call | flops 2415919104 | bytes 14942208 | tf_op jit(solution)/shard_map/pallas_call | solution.py:224
  21.4 1.6 %collective-permute-start.8 = (bf16[16,6272]{1,0:T(8,128)(2,1)S(1)}, bf16[16,6272]{1,0:T(8,128)(2,1)S(1)}, u32[]{:S(2)}, u32[]{:S(2)}) collective-permute-start(bf16[16,6272]{1,0:T(8,128)(2,1)S(1)} %collective-permute-done.4.refs_0_), channel_id=1, source_target_pairs={{0,1},{1,2},{2,3},{3,7},{7,6},{6,5},{5,4},{4,0},{8,9},{9,10},{10,1... | collective-permute-start | bytes 602120 | tf_op jit(solution)/shard_map/gather0_+1_hop3/ppermute | solution.py:155
  23.5 1.7 %collective-permute-done.7.refs_3_ = bf16[16,6272]{1,0:T(8,128)(2,1)S(1)} collective-permute-done((bf16[16,6272]{1,0:T(8,128)(2,1)S(1)}, bf16[16,6272]{1,0:T(8,128)(2,1)S(1)}, u32[]{:S(2)}, u32[]{:S(2)}) %collective-permute-start.7) | collective-permute-done | bytes 200736 | tf_op jit(solution)/shard_map/gather0_-1_hop2/ppermute | solution.py:155
  25.2 2.0 %collective-permute-start.10 = (bf16[16,6272]{1,0:T(8,128)(2,1)S(1)}, bf16[16,6272]{1,0:T(8,128)(2,1)S(1)}, u32[]{:S(2)}, u32[]{:S(2)}) collective-permute-start(bf16[16,6272]{1,0:T(8,128)(2,1)S(1)} %collective-permute-done.6.refs_2_), channel_id=1, source_target_pairs={{0,1},{1,2},{2,3},{3,7},{7,6},{6,5},{5,4},{4,0},{8,9},{9,10},{10,1... | collective-permute-start | bytes 602120 | tf_op jit(solution)/shard_map/gather1_+1_hop3/ppermute | solution.py:155
  27.2 2.7 %shard_map.76 = (f32[48,2048]{1,0:T(8,128)S(1)}, f32[48,2048]{1,0:T(8,128)S(1)}, f32[48,2048]{1,0:T(8,128)S(1)}, f32[48,2048]{1,0:T(8,128)S(1)}) custom-call(bf16[16,6272]{1,0:T(8,128)(2,1)S(1)} %collective-permute-done.4.refs_0_, bf16[16,6272]{1,0:T(8,128)(2,1)S(1)} %collective-permute-done.5.refs_1_, bf16[16,6272]{1,0:T(8,128)(2,1)S(1)} %collective-permute-done.6.refs_2_, ...), custom_call_target="tpu_custom_call" | custom-call | flops 2415919104 | bytes 14942208 | tf_op jit(solution)/shard_map/pallas_call | solution.py:224
  30.0 1.6 %collective-permute-start.12 = (bf16[16,6272]{1,0:T(8,128)(2,1)S(1)}, bf16[16,6272]{1,0:T(8,128)(2,1)S(1)}, u32[]{:S(2)}, u32[]{:S(2)}) collective-permute-start(bf16[16,6272]{1,0:T(8,128)(2,1)S(1)} %collective-permute-done.8.refs_0_), channel_id=1, source_target_pairs={{0,1},{1,2},{2,3},{3,7},{7,6},{6,5},{5,4},{4,0},{8,9},{9,10},{10,1... | collective-permute-start | bytes 602120 | tf_op jit(solution)/shard_map/gather0_+1_hop4/ppermute | solution.py:155
  32.1 2.0 %collective-permute-done.11.refs_3_ = bf16[16,6272]{1,0:T(8,128)(2,1)S(1)} collective-permute-done((bf16[16,6272]{1,0:T(8,128)(2,1)S(1)}, bf16[16,6272]{1,0:T(8,128)(2,1)S(1)}, u32[]{:S(2)}, u32[]{:S(2)}) %collective-permute-start.11) | collective-permute-done | bytes 200736 | tf_op jit(solution)/shard_map/gather0_-1_hop3/ppermute | solution.py:155
  34.0 2.7 %shard_map.77 = (f32[48,2048]{1,0:T(8,128)S(1)}, f32[48,2048]{1,0:T(8,128)S(1)}, bf16[48,2048]{1,0:T(8,128)(2,1)S(1)}, bf16[48,2048]{1,0:T(8,128)(2,1)S(1)}) custom-call(bf16[16,6272]{1,0:T(8,128)(2,1)S(1)} %collective-permute-done.8.refs_0_, bf16[16,6272]{1,0:T(8,128)(2,1)S(1)} %collective-permute-done.9.refs_1_, ...), custom_call_target="tpu_custom_call" | custom-call | flops 2415919104 | bytes 14942208 | tf_op jit(solution)/shard_map/pallas_call | solution.py:224
  37.3 2.2 %shard_map.78 = (bf16[48,2048]{1,0:T(8,128)(2,1)S(1)}, bf16[48,2048]{1,0:T(8,128)(2,1)S(1)}) custom-call(bf16[16,6272]{1,0:T(8,128)(2,1)S(1)} %collective-permute-done.12.refs_0_, bf16[16,6272]{1,0:T(8,128)(2,1)S(1)} %collective-permute-done.13.refs_1_, bf16[1,2048,1024]{2,1,0:T(8,128)(2,1)S(1)} %copy-done, bf16[1,2048,1024]{2,1,0:T(8,128)(2,1)S(1)} %copy-done.1, ...), custom_call_target="tpu_custom_call" | custom-call | flops 1207959552 | bytes 13762560 | tf_op jit(solution)/shard_map/pallas_call | solution.py:224
  43.7 3.7 %collective-permute-done.14 = bf16[48,2048]{1,0:T(8,128)(2,1)S(1)} collective-permute-done((bf16[48,2048]{1,0:T(8,128)(2,1)S(1)}, bf16[48,2048]{1,0:T(8,128)(2,1)S(1)}, u32[]{:S(2)}, u32[]{:S(2)}) %collective-permute-start.14) | collective-permute-done | bytes 196640 | tf_op jit(solution)/shard_map/sum0_-1_left4/ppermute | solution.py:155
  48.0 1.6 %collective-permute-start.21 = (bf16[48,2048]{1,0:T(8,128)(2,1)S(1)}, bf16[48,2048]{1,0:T(8,128)(2,1)S(1)}, u32[]{:S(2)}, u32[]{:S(2)}) collective-permute-start(bf16[48,2048]{1,0:T(8,128)(2,1)S(1)} %add_convert_fusion.7), channel_id=1, source_target_pairs={{0,1},{1,2},{2,3},{3,7},{7,6},{6,5},{5,4},{4,0},{8,9},{9,10},{10,1... | collective-permute-start | bytes 589832 | tf_op jit(solution)/shard_map/sum1_+1_left3/ppermute | solution.py:155
  49.6 2.3 %collective-permute-done.18 = bf16[48,2048]{1,0:T(8,128)(2,1)S(1)} collective-permute-done((bf16[48,2048]{1,0:T(8,128)(2,1)S(1)}, bf16[48,2048]{1,0:T(8,128)(2,1)S(1)}, u32[]{:S(2)}, u32[]{:S(2)}) %collective-permute-start.18) | collective-permute-done | bytes 196640 | tf_op jit(solution)/shard_map/sum0_+1_left3/ppermute | solution.py:155
  54.1 1.7 %collective-permute-done.15 = bf16[48,2048]{1,0:T(8,128)(2,1)S(1)} collective-permute-done((bf16[48,2048]{1,0:T(8,128)(2,1)S(1)}, bf16[48,2048]{1,0:T(8,128)(2,1)S(1)}, u32[]{:S(2)}, u32[]{:S(2)}) %collective-permute-start.15) | collective-permute-done | bytes 196640 | tf_op jit(solution)/shard_map/sum0_-1_left3/ppermute | solution.py:155
  56.4 1.6 %collective-permute-start.26 = (bf16[48,2048]{1,0:T(8,128)(2,1)S(1)}, bf16[48,2048]{1,0:T(8,128)(2,1)S(1)}, u32[]{:S(2)}, u32[]{:S(2)}) collective-permute-start(bf16[48,2048]{1,0:T(8,128)(2,1)S(1)} %add_convert_fusion.5), channel_id=1, source_target_pairs={{0,1},{1,2},{2,3},{3,7},{7,6},{6,5},{5,4},{4,0},{8,9},{9,10},{10,1... | collective-permute-start | bytes 589832 | tf_op jit(solution)/shard_map/sum1_+1_left2/ppermute | solution.py:155
  58.0 2.3 %collective-permute-done.20 = bf16[48,2048]{1,0:T(8,128)(2,1)S(1)} collective-permute-done((bf16[48,2048]{1,0:T(8,128)(2,1)S(1)}, bf16[48,2048]{1,0:T(8,128)(2,1)S(1)}, u32[]{:S(2)}, u32[]{:S(2)}) %collective-permute-start.20) | collective-permute-done | bytes 196640 | tf_op jit(solution)/shard_map/sum0_+1_left2/ppermute | solution.py:155
  62.5 2.9 %collective-permute-done.16 = bf16[48,2048]{1,0:T(8,128)(2,1)S(1)} collective-permute-done((bf16[48,2048]{1,0:T(8,128)(2,1)S(1)}, bf16[48,2048]{1,0:T(8,128)(2,1)S(1)}, u32[]{:S(2)}, u32[]{:S(2)}) %collective-permute-start.16) | collective-permute-done | bytes 196640 | tf_op jit(solution)/shard_map/sum0_-1_left2/ppermute | solution.py:155
  65.7 1.9 %collective-permute-start.27 = (bf16[48,2048]{1,0:T(8,128)(2,1)S(1)}, bf16[48,2048]{1,0:T(8,128)(2,1)S(1)}, u32[]{:S(2)}, u32[]{:S(2)}) collective-permute-start(bf16[48,2048]{1,0:T(8,128)(2,1)S(1)} %add_convert_fusion.1), channel_id=1, source_target_pairs={{0,1},{1,2},{2,3},{3,7},{7,6},{6,5},{5,4},{4,0},{8,9},{9,10},{10,1... | collective-permute-start | bytes 589832 | tf_op jit(solution)/shard_map/sum1_+1_left1/ppermute | solution.py:155
  67.7 3.5 %collective-permute-done.17 = bf16[48,2048]{1,0:T(8,128)(2,1)S(1)} collective-permute-done((bf16[48,2048]{1,0:T(8,128)(2,1)S(1)}, bf16[48,2048]{1,0:T(8,128)(2,1)S(1)}, u32[]{:S(2)}, u32[]{:S(2)}) %collective-permute-start.17) | collective-permute-done | bytes 196640 | tf_op jit(solution)/shard_map/sum0_-1_left1/ppermute | solution.py:155
  (57 shorter events, 15.4 us)
Async XLA Ops:
  1.3 8.8 %collective-permute-start = (bf16[16,6272]{1,0:T(8,128)(2,1)S(1)}, bf16[16,6272]{1,0:T(8,128)(2,1)S(1)}, u32[]{:S(2)}, u32[]{:S(2)}) collective-permute-start(bf16[16,6272]{1,0:T(8,128)(2,1)S(1)} %get-tuple-element.42.refs_0_), channel_id=1, source_target_pairs={{0,1},{1,2},{2,3},{3,7},{7,6},{6,5},{5,4},{4,0},{8,9},{9,10},{10,1... | collective-permute-start | bytes 602120 | tf_op jit(solution)/shard_map/gather0_+1_hop1/ppermute | solution.py:155
  4.4 7.9 %collective-permute-start.1 = (bf16[16,6272]{1,0:T(8,128)(2,1)S(1)}, bf16[16,6272]{1,0:T(8,128)(2,1)S(1)}, u32[]{:S(2)}, u32[]{:S(2)}) collective-permute-start(bf16[16,6272]{1,0:T(8,128)(2,1)S(1)} %get-tuple-element.43.refs_1_), channel_id=1, source_target_pairs={{0,4},{1,0},{2,1},{3,2},{7,3},{6,7},{5,6},{4,5},{8,12},{9,8},{10,9... | collective-permute-start | bytes 602120 | tf_op jit(solution)/shard_map/gather1_-1_hop1/ppermute | solution.py:155
  4.4 12.2 %collective-permute-start.3 = (bf16[16,6272]{1,0:T(8,128)(2,1)S(1)}, bf16[16,6272]{1,0:T(8,128)(2,1)S(1)}, u32[]{:S(2)}, u32[]{:S(2)}) collective-permute-start(bf16[16,6272]{1,0:T(8,128)(2,1)S(1)} %get-tuple-element.42.refs_0_), channel_id=1, source_target_pairs={{0,4},{1,0},{2,1},{3,2},{7,3},{6,7},{5,6},{4,5},{8,12},{9,8},{10,9... | collective-permute-start | bytes 602120 | tf_op jit(solution)/shard_map/gather0_-1_hop1/ppermute | solution.py:155
  6.3 10.3 %collective-permute-start.2 = (bf16[16,6272]{1,0:T(8,128)(2,1)S(1)}, bf16[16,6272]{1,0:T(8,128)(2,1)S(1)}, u32[]{:S(2)}, u32[]{:S(2)}) collective-permute-start(bf16[16,6272]{1,0:T(8,128)(2,1)S(1)} %get-tuple-element.43.refs_1_), channel_id=1, source_target_pairs={{0,1},{1,2},{2,3},{3,7},{7,6},{6,5},{5,4},{4,0},{8,9},{9,10},{10,1... | collective-permute-start | bytes 602120 | tf_op jit(solution)/shard_map/gather1_+1_hop1/ppermute | solution.py:155
  10.1 11.3 %collective-permute-start.4 = (bf16[16,6272]{1,0:T(8,128)(2,1)S(1)}, bf16[16,6272]{1,0:T(8,128)(2,1)S(1)}, u32[]{:S(2)}, u32[]{:S(2)}) collective-permute-start(bf16[16,6272]{1,0:T(8,128)(2,1)S(1)} %collective-permute-done.refs_0_), channel_id=1, source_target_pairs={{0,1},{1,2},{2,3},{3,7},{7,6},{6,5},{5,4},{4,0},{8,9},{9,10},{10,1... | collective-permute-start | bytes 602120 | tf_op jit(solution)/shard_map/gather0_+1_hop2/ppermute | solution.py:155
  12.3 10.7 %collective-permute-start.5 = (bf16[16,6272]{1,0:T(8,128)(2,1)S(1)}, bf16[16,6272]{1,0:T(8,128)(2,1)S(1)}, u32[]{:S(2)}, u32[]{:S(2)}) collective-permute-start(bf16[16,6272]{1,0:T(8,128)(2,1)S(1)} %collective-permute-done.1.refs_1_), channel_id=1, source_target_pairs={{0,4},{1,0},{2,1},{3,2},{7,3},{6,7},{5,6},{4,5},{8,12},{9,8},{10,9... | collective-permute-start | bytes 602120 | tf_op jit(solution)/shard_map/gather1_-1_hop2/ppermute | solution.py:155
  16.6 8.6 %collective-permute-start.7 = (bf16[16,6272]{1,0:T(8,128)(2,1)S(1)}, bf16[16,6272]{1,0:T(8,128)(2,1)S(1)}, u32[]{:S(2)}, u32[]{:S(2)}) collective-permute-start(bf16[16,6272]{1,0:T(8,128)(2,1)S(1)} %collective-permute-done.3.refs_3_), channel_id=1, source_target_pairs={{0,4},{1,0},{2,1},{3,2},{7,3},{6,7},{5,6},{4,5},{8,12},{9,8},{10,9... | collective-permute-start | bytes 602120 | tf_op jit(solution)/shard_map/gather0_-1_hop2/ppermute | solution.py:155
  16.6 8.6 %collective-permute-start.6 = (bf16[16,6272]{1,0:T(8,128)(2,1)S(1)}, bf16[16,6272]{1,0:T(8,128)(2,1)S(1)}, u32[]{:S(2)}, u32[]{:S(2)}) collective-permute-start(bf16[16,6272]{1,0:T(8,128)(2,1)S(1)} %collective-permute-done.2.refs_2_), channel_id=1, source_target_pairs={{0,1},{1,2},{2,3},{3,7},{7,6},{6,5},{5,4},{4,0},{8,9},{9,10},{10,1... | collective-permute-start | bytes 602120 | tf_op jit(solution)/shard_map/gather1_+1_hop2/ppermute | solution.py:155
  21.4 8.6 %collective-permute-start.8 = (bf16[16,6272]{1,0:T(8,128)(2,1)S(1)}, bf16[16,6272]{1,0:T(8,128)(2,1)S(1)}, u32[]{:S(2)}, u32[]{:S(2)}) collective-permute-start(bf16[16,6272]{1,0:T(8,128)(2,1)S(1)} %collective-permute-done.4.refs_0_), channel_id=1, source_target_pairs={{0,1},{1,2},{2,3},{3,7},{7,6},{6,5},{5,4},{4,0},{8,9},{9,10},{10,1... | collective-permute-start | bytes 602120 | tf_op jit(solution)/shard_map/gather0_+1_hop3/ppermute | solution.py:155
  23.0 8.6 %collective-permute-start.9 = (bf16[16,6272]{1,0:T(8,128)(2,1)S(1)}, bf16[16,6272]{1,0:T(8,128)(2,1)S(1)}, u32[]{:S(2)}, u32[]{:S(2)}) collective-permute-start(bf16[16,6272]{1,0:T(8,128)(2,1)S(1)} %collective-permute-done.5.refs_1_), channel_id=1, source_target_pairs={{0,4},{1,0},{2,1},{3,2},{7,3},{6,7},{5,6},{4,5},{8,12},{9,8},{10,9... | collective-permute-start | bytes 602120 | tf_op jit(solution)/shard_map/gather1_-1_hop3/ppermute | solution.py:155
  25.2 8.9 %collective-permute-start.11 = (bf16[16,6272]{1,0:T(8,128)(2,1)S(1)}, bf16[16,6272]{1,0:T(8,128)(2,1)S(1)}, u32[]{:S(2)}, u32[]{:S(2)}) collective-permute-start(bf16[16,6272]{1,0:T(8,128)(2,1)S(1)} %collective-permute-done.7.refs_3_), channel_id=1, source_target_pairs={{0,4},{1,0},{2,1},{3,2},{7,3},{6,7},{5,6},{4,5},{8,12},{9,8},{10,9... | collective-permute-start | bytes 602120 | tf_op jit(solution)/shard_map/gather0_-1_hop3/ppermute | solution.py:155
  25.2 8.9 %collective-permute-start.10 = (bf16[16,6272]{1,0:T(8,128)(2,1)S(1)}, bf16[16,6272]{1,0:T(8,128)(2,1)S(1)}, u32[]{:S(2)}, u32[]{:S(2)}) collective-permute-start(bf16[16,6272]{1,0:T(8,128)(2,1)S(1)} %collective-permute-done.6.refs_2_), channel_id=1, source_target_pairs={{0,1},{1,2},{2,3},{3,7},{7,6},{6,5},{5,4},{4,0},{8,9},{9,10},{10,1... | collective-permute-start | bytes 602120 | tf_op jit(solution)/shard_map/gather1_+1_hop3/ppermute | solution.py:155
  39.6 7.8 %collective-permute-start.14 = (bf16[48,2048]{1,0:T(8,128)(2,1)S(1)}, bf16[48,2048]{1,0:T(8,128)(2,1)S(1)}, u32[]{:S(2)}, u32[]{:S(2)}) collective-permute-start(bf16[48,2048]{1,0:T(8,128)(2,1)S(1)} %get-tuple-element.55), channel_id=1, source_target_pairs={{0,4},{1,0},{2,1},{3,2},{7,3},{6,7},{5,6},{4,5},{8,12},{9,8},{10,9... | collective-permute-start | bytes 589832 | tf_op jit(solution)/shard_map/sum0_-1_left4/ppermute | solution.py:155
  40.1 7.9 %collective-permute-start.19 = (bf16[48,2048]{1,0:T(8,128)(2,1)S(1)}, bf16[48,2048]{1,0:T(8,128)(2,1)S(1)}, u32[]{:S(2)}, u32[]{:S(2)}) collective-permute-start(bf16[48,2048]{1,0:T(8,128)(2,1)S(1)} %get-tuple-element.59), channel_id=1, source_target_pairs={{0,1},{1,2},{2,3},{3,7},{7,6},{6,5},{5,4},{4,0},{8,9},{9,10},{10,1... | collective-permute-start | bytes 589832 | tf_op jit(solution)/shard_map/sum1_+1_left4/ppermute | solution.py:155
  41.6 10.2 %collective-permute-start.18 = (bf16[48,2048]{1,0:T(8,128)(2,1)S(1)}, bf16[48,2048]{1,0:T(8,128)(2,1)S(1)}, u32[]{:S(2)}, u32[]{:S(2)}) collective-permute-start(bf16[48,2048]{1,0:T(8,128)(2,1)S(1)} %get-tuple-element.60), channel_id=1, source_target_pairs={{0,1},{1,2},{2,3},{3,7},{7,6},{6,5},{5,4},{4,0},{8,9},{9,10},{10,1... | collective-permute-start | bytes 589832 | tf_op jit(solution)/shard_map/sum0_+1_left3/ppermute | solution.py:155
  43.2 10.3 %collective-permute-start.23 = (bf16[48,2048]{1,0:T(8,128)(2,1)S(1)}, bf16[48,2048]{1,0:T(8,128)(2,1)S(1)}, u32[]{:S(2)}, u32[]{:S(2)}) collective-permute-start(bf16[48,2048]{1,0:T(8,128)(2,1)S(1)} %get-tuple-element.69), channel_id=1, source_target_pairs={{0,4},{1,0},{2,1},{3,2},{7,3},{6,7},{5,6},{4,5},{8,12},{9,8},{10,9... | collective-permute-start | bytes 589832 | tf_op jit(solution)/shard_map/sum1_-1_left3/ppermute | solution.py:155
  47.4 8.4 %collective-permute-start.15 = (bf16[48,2048]{1,0:T(8,128)(2,1)S(1)}, bf16[48,2048]{1,0:T(8,128)(2,1)S(1)}, u32[]{:S(2)}, u32[]{:S(2)}) collective-permute-start(bf16[48,2048]{1,0:T(8,128)(2,1)S(1)} %add_convert_fusion.11), channel_id=1, source_target_pairs={{0,4},{1,0},{2,1},{3,2},{7,3},{6,7},{5,6},{4,5},{8,12},{9,8},{10,9... | collective-permute-start | bytes 589832 | tf_op jit(solution)/shard_map/sum0_-1_left3/ppermute | solution.py:155
  48.0 8.4 %collective-permute-start.21 = (bf16[48,2048]{1,0:T(8,128)(2,1)S(1)}, bf16[48,2048]{1,0:T(8,128)(2,1)S(1)}, u32[]{:S(2)}, u32[]{:S(2)}) collective-permute-start(bf16[48,2048]{1,0:T(8,128)(2,1)S(1)} %add_convert_fusion.7), channel_id=1, source_target_pairs={{0,1},{1,2},{2,3},{3,7},{7,6},{6,5},{5,4},{4,0},{8,9},{9,10},{10,1... | collective-permute-start | bytes 589832 | tf_op jit(solution)/shard_map/sum1_+1_left3/ppermute | solution.py:155
  51.9 8.4 %collective-permute-start.20 = (bf16[48,2048]{1,0:T(8,128)(2,1)S(1)}, bf16[48,2048]{1,0:T(8,128)(2,1)S(1)}, u32[]{:S(2)}, u32[]{:S(2)}) collective-permute-start(bf16[48,2048]{1,0:T(8,128)(2,1)S(1)} %add_convert_fusion.8), channel_id=1, source_target_pairs={{0,1},{1,2},{2,3},{3,7},{7,6},{6,5},{5,4},{4,0},{8,9},{9,10},{10,1... | collective-permute-start | bytes 589832 | tf_op jit(solution)/shard_map/sum0_+1_left2/ppermute | solution.py:155
  53.5 8.0 %collective-permute-start.24 = (bf16[48,2048]{1,0:T(8,128)(2,1)S(1)}, bf16[48,2048]{1,0:T(8,128)(2,1)S(1)}, u32[]{:S(2)}, u32[]{:S(2)}) collective-permute-start(bf16[48,2048]{1,0:T(8,128)(2,1)S(1)} %add_convert_fusion.3), channel_id=1, source_target_pairs={{0,4},{1,0},{2,1},{3,2},{7,3},{6,7},{5,6},{4,5},{8,12},{9,8},{10,9... | collective-permute-start | bytes 589832 | tf_op jit(solution)/shard_map/sum1_-1_left2/ppermute | solution.py:155
  55.8 9.6 %collective-permute-start.16 = (bf16[48,2048]{1,0:T(8,128)(2,1)S(1)}, bf16[48,2048]{1,0:T(8,128)(2,1)S(1)}, u32[]{:S(2)}, u32[]{:S(2)}) collective-permute-start(bf16[48,2048]{1,0:T(8,128)(2,1)S(1)} %add_convert_fusion.10), channel_id=1, source_target_pairs={{0,4},{1,0},{2,1},{3,2},{7,3},{6,7},{5,6},{4,5},{8,12},{9,8},{10,9... | collective-permute-start | bytes 589832 | tf_op jit(solution)/shard_map/sum0_-1_left2/ppermute | solution.py:155
  56.4 9.3 %collective-permute-start.26 = (bf16[48,2048]{1,0:T(8,128)(2,1)S(1)}, bf16[48,2048]{1,0:T(8,128)(2,1)S(1)}, u32[]{:S(2)}, u32[]{:S(2)}) collective-permute-start(bf16[48,2048]{1,0:T(8,128)(2,1)S(1)} %add_convert_fusion.5), channel_id=1, source_target_pairs={{0,1},{1,2},{2,3},{3,7},{7,6},{6,5},{5,4},{4,0},{8,9},{9,10},{10,1... | collective-permute-start | bytes 589832 | tf_op jit(solution)/shard_map/sum1_+1_left2/ppermute | solution.py:155
  60.4 7.3 %collective-permute-start.22 = (bf16[48,2048]{1,0:T(8,128)(2,1)S(1)}, bf16[48,2048]{1,0:T(8,128)(2,1)S(1)}, u32[]{:S(2)}, u32[]{:S(2)}) collective-permute-start(bf16[48,2048]{1,0:T(8,128)(2,1)S(1)} %add_convert_fusion.6), channel_id=1, source_target_pairs={{0,1},{1,2},{2,3},{3,7},{7,6},{6,5},{5,4},{4,0},{8,9},{9,10},{10,1... | collective-permute-start | bytes 589832 | tf_op jit(solution)/shard_map/sum0_+1_left1/ppermute | solution.py:155
  61.6 9.7 %collective-permute-start.25 = (bf16[48,2048]{1,0:T(8,128)(2,1)S(1)}, bf16[48,2048]{1,0:T(8,128)(2,1)S(1)}, u32[]{:S(2)}, u32[]{:S(2)}) collective-permute-start(bf16[48,2048]{1,0:T(8,128)(2,1)S(1)} %add_convert_fusion.2), channel_id=1, source_target_pairs={{0,4},{1,0},{2,1},{3,2},{7,3},{6,7},{5,6},{4,5},{8,12},{9,8},{10,9... | collective-permute-start | bytes 589832 | tf_op jit(solution)/shard_map/sum1_-1_left1/ppermute | solution.py:155
  (7 other events, 43.3 us)
